TPU v7x, 32 devices: a whole 2x2x4 slice. The times are simulated.
32 devices in a mesh: line: 8 (over y, x, core), seg: 4 (over z).
Axes of the slice: x: 2, y: 2, z: 4, core: 2. Of those that a mesh axis runs over, the one named last changes fastest.
Arguments:
- points: float32 [8, 4, 3, 32768], P('line', 'seg'), may hold values from -1 to 1
- rows: int32 [8, 4, 2, 3072], P('line', 'seg'), may hold values from -1 to 32767, as said below
- cells: int32 [8, 4, 2, 24], P('line', 'seg'), may hold values from -1 to 15, as said below
- pose: float32 [12, 8], P(None, 'line'), as said below
Outputs:
- matched: float32 [8, 4, 2, 5, 3072], P('line', 'seg')
- fitted_pose: float32 [12, 8], P(None, 'line')
- final_spread: float32 [1], replicated
Inputs may be any that keep to these rules, and one draw needn't show every extreme that they name: In each block of 128 slots the filled slots come first; every slot of an empty block is empty; rows toward the lower line lie in the lower margin (below 8192), rows toward the upper line in the upper margin (24576 or more); the lists of line 0 toward the lower side and of line 8 - 1 toward the upper side are empty. `cells`: empty blocks come after the others; in segment 0 of every line all blocks toward an existing adjacent line are filled. `pose`: every 3x3 part is within about 0.5 of the identity.
All inputs are finite; a program needn't handle non-finite values.
Results may differ from a plain program's by a relative error of at most 0.0003.
Values sent between devices are 32-bit elements; how exact they have to be, the bound alone decides.
No kernel may reach another device: no remote copies, remote signals or barrier semaphores. Data moves between devices by JAX's collectives and lax.ppermute only.
A program may use at most 64 MiB of HBM per device.

v0:
```python
import jax
import jax.numpy as jnp
from jax import lax
from jax.sharding import PartitionSpec as P

NCELL = 16
CT = 512
BLOCK = 128
ITERS = 2


OUTLIER_MASS = 1.0
SPREAD_START = 0.05
PRIOR_TOP = 0.05
PRIOR_BOTTOM = 1.0
REGULARIZE = 1.0
blocks_per_turn = 4


def from_behind(value, axis, steps):
    count = lax.axis_size(axis)
    initial, last = (max(0, -steps), min(count, count - steps))
    return lax.ppermute(value, axis, [(source, source + steps) for source in range(initial, last)])


def match_block(source_block, cell_id, world_points, spread):
    first_column = jnp.maximum(cell_id, 0) * CT
    target = lax.dynamic_slice_in_dim(world_points, first_column, CT, 1)
    distance = (source_block[0][:, None] - target[0][None, :]) ** 2
    distance = distance + (source_block[1][:, None] - target[1][None, :]) ** 2
    distance = distance + (source_block[2][:, None] - target[2][None, :]) ** 2
    weight = jnp.exp(-distance / (2.0 * spread))
    total_weight = jnp.sum(weight, axis=1)
    posterior = weight / (total_weight + OUTLIER_MASS)[:, None]
    pulled = lax.dot_general(
        target,
        posterior,
        (((1,), (1,)), ((), ())),
        precision=lax.Precision.HIGHEST,
        preferred_element_type=jnp.float32,
    )
    share_row = total_weight / (total_weight + OUTLIER_MASS)
    energy_row = jnp.sum(posterior * distance, axis=1)
    merged_rows = jnp.concatenate([pulled, share_row[None, :], energy_row[None, :]], axis=0)
    return jnp.where(cell_id >= 0, merged_rows, jnp.zeros_like(merged_rows))


def match_all(sources, block_cells, worlds, spread):
    block_total = block_cells.shape[1]
    turns = 2 * block_total // blocks_per_turn
    grouped = (
        sources.reshape(2, 3, block_total, BLOCK)
        .transpose(0, 2, 1, 3)
        .reshape(turns, blocks_per_turn, 3, BLOCK)
    )
    grouped_cells = block_cells.reshape(turns, blocks_per_turn)
    sides = jnp.arange(turns) // (turns // 2)

    def one_turn(packed):
        turn_blocks, turn_cells, side = packed
        target_world = lax.dynamic_index_in_dim(worlds, side, 0, keepdims=False)

        def compute(unused):
            return jax.vmap(
                lambda block_points, block_cell: match_block(
                    block_points, block_cell, target_world, spread
                )
            )(turn_blocks, turn_cells)

        def skipped(unused):
            return jnp.zeros((blocks_per_turn, 5, BLOCK), jnp.float32)

        return lax.cond(jnp.any(turn_cells >= 0), compute, skipped, 0)

    output = lax.map(one_turn, (grouped, grouped_cells, sides))
    return (
        output.reshape(2, block_total, 5, BLOCK)
        .transpose(0, 2, 1, 3)
        .reshape(2, 5, block_total * BLOCK)
    )


def solve_pose(gram_matrix, cross_matrix, pose_column):
    old_pose = jnp.concatenate(
        [pose_column[:9].reshape(3, 3), pose_column[9:].reshape(3, 1)], axis=1
    )
    left_side = gram_matrix + REGULARIZE * jnp.eye(4, dtype=gram_matrix.dtype)
    right_side = cross_matrix + REGULARIZE * old_pose
    factor = jnp.linalg.cholesky(left_side)
    solved = jax.scipy.linalg.cho_solve((factor, True), right_side.T)
    new_pose = solved.T
    return jnp.concatenate([new_pose[:, :3].reshape(9), new_pose[:, 3]])


def send_lists(lists, marks, step):
    return from_behind((lists, marks), "line", step)


def send_back(piece, step):
    return from_behind(piece, "line", step)


def on_device(points, rows, cells, pose):
    own_points = points[0, 0]
    row_list = rows[0, 0]
    cell_ids = cells[0, 0]
    pose_column = pose[:, 0]
    margin = NCELL * CT
    point_total = own_points.shape[1]
    slot_total = row_list.shape[1]
    live_slots = (row_list >= 0).astype(jnp.float32)
    safe_rows = jnp.where(row_list >= 0, row_list, 0)
    raw_source = (
        jnp.take(own_points, safe_rows.reshape(-1), axis=1)
        .reshape(3, 2, slot_total)
        .transpose(1, 0, 2)
    )
    extended = jnp.concatenate([raw_source, jnp.ones((2, 1, slot_total), jnp.float32)], axis=1)
    spread = jnp.float32(SPREAD_START)
    result = None
    for iteration in range(ITERS):
        linear_part = pose_column[:9].reshape(3, 3)
        offset_part = pose_column[9:]
        world_points = (
            jnp.dot(
                linear_part,
                own_points,
                precision=lax.Precision.HIGHEST,
                preferred_element_type=jnp.float32,
            )
            + offset_part[:, None]
        )
        moved_source = (
            jnp.einsum("km,dms->dks", linear_part, raw_source, precision=lax.Precision.HIGHEST)
            + offset_part[None, :, None]
        )
        lower_margin = world_points[:, :margin]
        upper_margin = world_points[:, point_total - margin :]
        cell_marks = (cell_ids + 1).astype(jnp.float32)
        lists_down, marks_down = send_lists(moved_source[0], cell_marks[0], -1)
        lists_up, marks_up = send_lists(moved_source[1], cell_marks[1], 1)
        incoming = jnp.stack([lists_down, lists_up])
        got_cells = jnp.stack([marks_down, marks_up]).astype(jnp.int32) - 1
        own_worlds = jnp.stack([upper_margin, lower_margin])
        answers = match_all(incoming, got_cells, own_worlds, spread)
        result = jnp.stack([send_back(answers[0], 1), send_back(answers[1], -1)])
        result = result * live_slots[:, None, :]
        pulled = result[:, :3]
        share_all = result[:, 3]
        energy_all = result[:, 4]
        gram_matrix = jnp.einsum(
            "dks,dms->km",
            extended * share_all[:, None, :],
            extended,
            precision=lax.Precision.HIGHEST,
        )
        cross_matrix = jnp.einsum("dks,dms->km", pulled, extended, precision=lax.Precision.HIGHEST)
        energy_part = jnp.sum(energy_all)
        share_part = jnp.sum(share_all)
        gram_sum, cross_sum = lax.psum((gram_matrix, cross_matrix), "seg")
        energy_sum, share_sum = lax.psum((energy_part, share_part), ("line", "seg"))
        pose_column = solve_pose(gram_sum, cross_sum, pose_column)
        spread = (energy_sum + PRIOR_TOP) / (3.0 * share_sum + PRIOR_BOTTOM)
    return (result[None, None], pose_column[:, None], spread.reshape(1))


def solution(mesh):
    return jax.shard_map(
        on_device,
        mesh=mesh,
        in_specs=(
            P("line", "seg", None, None),
            P("line", "seg", None, None),
            P("line", "seg", None, None),
            P(None, "line"),
        ),
        out_specs=(P("line", "seg", None, None, None), P(None, "line"), P()),
        check_vma=False,
    )
```

profile of v0, /device:TPU:0, one launch (start us, length us, event | category | flops | bytes accessed | tf_op | source)
XLA Modules:
  0.0 500.9 jit_solution(13187992715287983889)
XLA Ops:
  3.6 9.4 %copy.18 = f32[1,1,3,32768]{2,3,1,0:T(8,128)} copy(f32[1,1,3,32768]{3,1,2,0:T(1,128)} %param.15) | data formatting | bytes 786432 | tf_op args[0]
  13.1 21.8 %gather_fusion = f32[6144,3]{1,0:T(8,128)S(1)} fusion(f32[3,32768]{0,1:T(8,128)} %bitcast.285, s32[6144]{0:T(1024)S(1)} %broadcast_clamp_fusion), kind=kCustom, calls=%fused_computation | custom fusion | bytes 172032 | tf_op jit(solution)/shard_map/jit(_take)/gather | solution.py:114
  41.6 5.8 %collective-permute-start.1 = (f32[24]{0:T(128)S(1)}, f32[24]{0:T(128)S(1)}, u32[]{:S(2)}, u32[]{:S(2)}) collective-permute-start(f32[24]{0:T(128)S(1)} %get-tuple-element.440), channel_id=1, source_target_pairs={{0,4},{4,8},{8,12},{12,16},{16,20},{20,24},{24,28},{1,5},{5,9},{9,... | collective-permute-start | bytes 296 | tf_op jit(solution)/shard_map/ppermute | solution.py:23
  47.4 16.7 %convolution_add_fusion.1 = f32[3,32768]{1,0:T(4,128)S(1)} fusion(f32[3,3]{1,0:T(4,128)S(1)} %reshape.263, f32[3]{0:T(128)S(1)} %get-tuple-element.442, f32[1,1,3,32768]{2,3,1,0:T(8,128)} %copy.18), kind=kOutput, calls=%fused_computation.61 | convolution fusion | flops 3637248 | bytes 786480 | tf_op jit(solution)/shard_map/dot_general | solution.py:125
  64.5 78.0 %while.28 = (s32[]{:T(128)}, f32[12,4,5,128]{3,2,1,0:T(8,128)S(1)}, s32[12,4]{1,0:T(8,128)S(1)}, f32[2,3,8192]{2,1,0:T(4,128)S(1)}, f32[12,4,3,128]{3,1,2,0:T(4,128)S(1)}, /*index=5*/s32[]{:T(128)}, s32[]{:T(128)}, s32[]{:T(128)}) while((s32[]{:T(128)}, f32[12,4,5,128]{3,2,1,0:T(8,128)S(1)}, s32[12,4]{1,0:T(8,128)S(1)}, ...), condition=%wide.region_6.7_spmd.clone, body=%wide.region_0.6_spmd.clone.sunk | while | flops 18620548 | bytes 529362 | solution.py:75
  65.8 10.3 %conditional.6 = (f32[1,4,5,128]{3,2,1,0:T(8,128)S(1)}) conditional(s32[]{:T(128)} %convert_element_type.49, () %tuple.138, (s32[4]{0:T(128)S(1)}, s32[12]{0:T(128)S(1)}, s32[]{:T(128)}, f32[2,3,8192]{2,1,0:T(4,128)S(1)}, f32[12,4,3,128]{3,1,2,0:T(4,128)S(1)}, /*index=5*/s32[12]{0:T(128)S(1)}, s32[12]{0:T(128)S(1)}, s32[12]{0:T(128)S(1)}, ...), branch_computations={%region_2.2_spmd, %region_3.5_spmd.clone} | conditional | flops 18620528 | bytes 496227 | solution.py:73
  68.3 4.9 while.26
  77.4 10.3 %conditional.6 = (f32[1,4,5,128]{3,2,1,0:T(8,128)S(1)}) conditional(s32[]{:T(128)} %convert_element_type.49, () %tuple.138, (s32[4]{0:T(128)S(1)}, s32[12]{0:T(128)S(1)}, s32[]{:T(128)}, f32[2,3,8192]{2,1,0:T(4,128)S(1)}, f32[12,4,3,128]{3,1,2,0:T(4,128)S(1)}, /*index=5*/s32[12]{0:T(128)S(1)}, s32[12]{0:T(128)S(1)}, s32[12]{0:T(128)S(1)}, ...), branch_computations={%region_2.2_spmd, %region_3.5_spmd.clone} | conditional | flops 18620528 | bytes 496227 | solution.py:73
  79.9 4.9 while.26
  89.1 10.3 %conditional.6 = (f32[1,4,5,128]{3,2,1,0:T(8,128)S(1)}) conditional(s32[]{:T(128)} %convert_element_type.49, () %tuple.138, (s32[4]{0:T(128)S(1)}, s32[12]{0:T(128)S(1)}, s32[]{:T(128)}, f32[2,3,8192]{2,1,0:T(4,128)S(1)}, f32[12,4,3,128]{3,1,2,0:T(4,128)S(1)}, /*index=5*/s32[12]{0:T(128)S(1)}, s32[12]{0:T(128)S(1)}, s32[12]{0:T(128)S(1)}, ...), branch_computations={%region_2.2_spmd, %region_3.5_spmd.clone} | conditional | flops 18620528 | bytes 496227 | solution.py:73
  91.6 4.9 while.26
  100.7 10.3 %conditional.6 = (f32[1,4,5,128]{3,2,1,0:T(8,128)S(1)}) conditional(s32[]{:T(128)} %convert_element_type.49, () %tuple.138, (s32[4]{0:T(128)S(1)}, s32[12]{0:T(128)S(1)}, s32[]{:T(128)}, f32[2,3,8192]{2,1,0:T(4,128)S(1)}, f32[12,4,3,128]{3,1,2,0:T(4,128)S(1)}, /*index=5*/s32[12]{0:T(128)S(1)}, s32[12]{0:T(128)S(1)}, s32[12]{0:T(128)S(1)}, ...), branch_computations={%region_2.2_spmd, %region_3.5_spmd.clone} | conditional | flops 18620528 | bytes 496227 | solution.py:73
  103.2 4.9 while.26
  112.4 10.3 %conditional.6 = (f32[1,4,5,128]{3,2,1,0:T(8,128)S(1)}) conditional(s32[]{:T(128)} %convert_element_type.49, () %tuple.138, (s32[4]{0:T(128)S(1)}, s32[12]{0:T(128)S(1)}, s32[]{:T(128)}, f32[2,3,8192]{2,1,0:T(4,128)S(1)}, f32[12,4,3,128]{3,1,2,0:T(4,128)S(1)}, /*index=5*/s32[12]{0:T(128)S(1)}, s32[12]{0:T(128)S(1)}, s32[12]{0:T(128)S(1)}, ...), branch_computations={%region_2.2_spmd, %region_3.5_spmd.clone} | conditional | flops 18620528 | bytes 496227 | solution.py:73
  114.9 4.9 while.26
  124.0 10.3 %conditional.6 = (f32[1,4,5,128]{3,2,1,0:T(8,128)S(1)}) conditional(s32[]{:T(128)} %convert_element_type.49, () %tuple.138, (s32[4]{0:T(128)S(1)}, s32[12]{0:T(128)S(1)}, s32[]{:T(128)}, f32[2,3,8192]{2,1,0:T(4,128)S(1)}, f32[12,4,3,128]{3,1,2,0:T(4,128)S(1)}, /*index=5*/s32[12]{0:T(128)S(1)}, s32[12]{0:T(128)S(1)}, s32[12]{0:T(128)S(1)}, ...), branch_computations={%region_2.2_spmd, %region_3.5_spmd.clone} | conditional | flops 18620528 | bytes 496227 | solution.py:73
  126.5 4.9 while.26
  142.6 65.3 %collective-permute-start.4 = (f32[5,3072]{1,0:T(8,128)S(1)}, f32[5,3072]{1,0:T(8,128)S(1)}, u32[]{:S(2)}, u32[]{:S(2)}) collective-permute-start(f32[5,3072]{1,0:T(8,128)S(1)} %bitcast.309), channel_id=1, source_target_pairs={{0,4},{4,8},{8,12},{12,16},{16,20},{20,24},{24,28},{1,5},{5,9},{9,... | collective-permute-start | bytes 184328 | tf_op jit(solution)/shard_map/ppermute | solution.py:23
  213.1 8.5 %all-reduce.6 = (f32[3,4]{1,0:T(4,128)S(1)}, f32[4,4]{0,1:T(4,128)S(1)}) all-reduce(f32[3,4]{1,0:T(4,128)S(1)} %convolution_bitcast_fusion.6, f32[4,4]{0,1:T(4,128)S(1)} %convolution_bitcast_fusion.7), channel_id=1, replica_groups=mesh['line'=8,'seg'=4] {'seg'}, use_global_device_ids=true, to_apply=%region_10.12 | all-reduce | flops 28 | bytes 224 | tf_op jit(solution)/shard_map/psum | solution.py:160
  224.6 16.7 %convolution_add_fusion = f32[3,32768]{1,0:T(4,128)S(1)} fusion(f32[3]{0:T(128)S(1)} %slice_reduce_fusion.3, f32[3,4]{1,0:T(4,128)S(1)} %convolution_bitcast_fusion.5, f32[1,1,3,32768]{2,3,1,0:T(8,128)} %copy.18), kind=kOutput, calls=%fused_computation.60 | convolution fusion | flops 3637248 | bytes 786492 | tf_op jit(solution)/shard_map/dot_general | solution.py:125
  246.5 44.6 %all-reduce.4 = (f32[]{:T(128)}, f32[]{:T(128)}) all-reduce(f32[]{:T(128)} %get-tuple-element.356, f32[]{:T(128)} %get-tuple-element.355), channel_id=1, replica_groups=mesh['line'=8,'seg'=4] {'line','seg'}, use_global_device_ids=true, to_apply=%region_12.15 | all-reduce | flops 2 | bytes 16 | tf_op jit(solution)/shard_map/psum | solution.py:161
  292.5 78.5 %while.29 = (s32[]{:T(128)}, f32[12,4,5,128]{3,2,1,0:T(8,128)S(1)}, s32[12,4]{1,0:T(8,128)S(1)}, f32[2,3,8192]{2,1,0:T(4,128)S(1)}, f32[12,4,3,128]{3,1,2,0:T(4,...) while((s32[]{:T(128)}, f32[12,4,5,128]{3,2,1,0:T(8,128)S(1)}, ...), condition=%wide.region_21.24_spmd.clone, body=%wide.region_15.23_spmd.clone.sunk | while | flops 18620552 | bytes 529402 | solution.py:75
  293.8 10.4 %conditional.7 = (f32[1,4,5,128]{3,2,1,0:T(8,128)S(1)}) conditional(s32[]{:T(128)} %convert_element_type.50, () %tuple.142, (s32[4]{0:T(128)S(1)}, s32[12]{0:T(128)S(1)}, s32[]{:T(128)}, f32[2,3,8192]{2,1,0:T(4,128)S(1)}, f32[12,4,3,128]{3,1,2,0:T(4,128)S(1)}, /*index=5*/f32[]{:T(128)}, s32[12]{0:T(128)S(1)}, s32[12]{0:T(128)S(1)}, ...), branch_computations={%region_17.19_spmd, %region_18.22_spmd.clone} | conditional | flops 18620530 | bytes 496251 | solution.py:73
  296.3 4.9 while.27
  305.6 10.4 %conditional.7 = (f32[1,4,5,128]{3,2,1,0:T(8,128)S(1)}) conditional(s32[]{:T(128)} %convert_element_type.50, () %tuple.142, (s32[4]{0:T(128)S(1)}, s32[12]{0:T(128)S(1)}, s32[]{:T(128)}, f32[2,3,8192]{2,1,0:T(4,128)S(1)}, f32[12,4,3,128]{3,1,2,0:T(4,128)S(1)}, /*index=5*/f32[]{:T(128)}, s32[12]{0:T(128)S(1)}, s32[12]{0:T(128)S(1)}, ...), branch_computations={%region_17.19_spmd, %region_18.22_spmd.clone} | conditional | flops 18620530 | bytes 496251 | solution.py:73
  317.3 10.4 %conditional.7 = (f32[1,4,5,128]{3,2,1,0:T(8,128)S(1)}) conditional(s32[]{:T(128)} %convert_element_type.50, () %tuple.142, (s32[4]{0:T(128)S(1)}, s32[12]{0:T(128)S(1)}, s32[]{:T(128)}, f32[2,3,8192]{2,1,0:T(4,128)S(1)}, f32[12,4,3,128]{3,1,2,0:T(4,128)S(1)}, /*index=5*/f32[]{:T(128)}, s32[12]{0:T(128)S(1)}, s32[12]{0:T(128)S(1)}, ...), branch_computations={%region_17.19_spmd, %region_18.22_spmd.clone} | conditional | flops 18620530 | bytes 496251 | solution.py:73
  329.0 10.4 %conditional.7 = (f32[1,4,5,128]{3,2,1,0:T(8,128)S(1)}) conditional(s32[]{:T(128)} %convert_element_type.50, () %tuple.142, (s32[4]{0:T(128)S(1)}, s32[12]{0:T(128)S(1)}, s32[]{:T(128)}, f32[2,3,8192]{2,1,0:T(4,128)S(1)}, f32[12,4,3,128]{3,1,2,0:T(4,128)S(1)}, /*index=5*/f32[]{:T(128)}, s32[12]{0:T(128)S(1)}, s32[12]{0:T(128)S(1)}, ...), branch_computations={%region_17.19_spmd, %region_18.22_spmd.clone} | conditional | flops 18620530 | bytes 496251 | solution.py:73
  340.7 10.4 %conditional.7 = (f32[1,4,5,128]{3,2,1,0:T(8,128)S(1)}) conditional(s32[]{:T(128)} %convert_element_type.50, () %tuple.142, (s32[4]{0:T(128)S(1)}, s32[12]{0:T(128)S(1)}, s32[]{:T(128)}, f32[2,3,8192]{2,1,0:T(4,128)S(1)}, f32[12,4,3,128]{3,1,2,0:T(4,128)S(1)}, /*index=5*/f32[]{:T(128)}, s32[12]{0:T(128)S(1)}, s32[12]{0:T(128)S(1)}, ...), branch_computations={%region_17.19_spmd, %region_18.22_spmd.clone} | conditional | flops 18620530 | bytes 496251 | solution.py:73
  352.4 10.4 %conditional.7 = (f32[1,4,5,128]{3,2,1,0:T(8,128)S(1)}) conditional(s32[]{:T(128)} %convert_element_type.50, () %tuple.142, (s32[4]{0:T(128)S(1)}, s32[12]{0:T(128)S(1)}, s32[]{:T(128)}, f32[2,3,8192]{2,1,0:T(4,128)S(1)}, f32[12,4,3,128]{3,1,2,0:T(4,128)S(1)}, /*index=5*/f32[]{:T(128)}, s32[12]{0:T(128)S(1)}, s32[12]{0:T(128)S(1)}, ...), branch_computations={%region_17.19_spmd, %region_18.22_spmd.clone} | conditional | flops 18620530 | bytes 496251 | solution.py:73
  371.1 63.3 %collective-permute-start.8 = (f32[5,3072]{1,0:T(8,128)S(1)}, f32[5,3072]{1,0:T(8,128)S(1)}, u32[]{:S(2)}, u32[]{:S(2)}) collective-permute-start(f32[5,3072]{1,0:T(8,128)S(1)} %bitcast.310), channel_id=1, source_target_pairs={{0,4},{4,8},{8,12},{12,16},{16,20},{20,24},{24,28},{1,5},{5,9},{9,... | collective-permute-start | bytes 184328 | tf_op jit(solution)/shard_map/ppermute | solution.py:23
  441.4 41.5 %all-reduce.3 = (f32[]{:T(128)}, f32[]{:T(128)}) all-reduce(f32[]{:T(128)} %get-tuple-element.354, f32[]{:T(128)} %get-tuple-element.353), channel_id=1, replica_groups=mesh['line'=8,'seg'=4] {'line','seg'}, use_global_device_ids=true, to_apply=%region_25.28 | all-reduce | flops 2 | bytes 16 | tf_op jit(solution)/shard_map/psum | solution.py:161
  484.8 10.7 %all-reduce.5 = (f32[4,4]{0,1:T(4,128)S(1)}, f32[3,4]{1,0:T(4,128)S(1)}) all-reduce(f32[4,4]{0,1:T(4,128)S(1)} %convolution_bitcast_fusion.4, f32[3,4]{1,0:T(4,128)S(1)} %convolution_bitcast_fusion.3), channel_id=1, replica_groups=mesh['line'=8,'seg'=4] {'seg'}, use_global_device_ids=true, to_apply=%region_22.25 | all-reduce | flops 28 | bytes 224 | tf_op jit(solution)/shard_map/psum | solution.py:160
  (605 shorter events, 178.2 us)
Async XLA Ops:
  0.6 39.6 %copy-start = (s32[1,1,2,24]{3,2,1,0:T(2,128)S(1)}, s32[1,1,2,24]{3,2,1,0:T(2,128)}, u32[]{:S(2)}) copy-start(s32[1,1,2,24]{3,2,1,0:T(2,128)} %param.17) | copy-start | bytes 580
  36.6 27.8 %collective-permute-start.3 = (f32[3,3072]{1,0:T(4,128)S(1)}, f32[3,3072]{1,0:T(4,128)S(1)}, u32[]{:S(2)}, u32[]{:S(2)}) collective-permute-start(f32[3,3072]{1,0:T(4,128)S(1)} %get-tuple-element.436), channel_id=1, source_target_pairs={{0,4},{4,8},{8,12},{12,16},{16,20},{20,24},{24,28},{1,5},{5,9},{9,... | collective-permute-start | bytes 110600 | tf_op jit(solution)/shard_map/ppermute | solution.py:23
  38.9 25.5 %collective-permute-start.2 = (f32[3,3072]{1,0:T(4,128)S(1)}, f32[3,3072]{1,0:T(4,128)S(1)}, u32[]{:S(2)}, u32[]{:S(2)}) collective-permute-start(f32[3,3072]{1,0:T(4,128)S(1)} %get-tuple-element.435), channel_id=1, source_target_pairs={{4,0},{8,4},{12,8},{16,12},{20,16},{24,20},{28,24},{5,1},{9,5},{13... | collective-permute-start | bytes 110600 | tf_op jit(solution)/shard_map/ppermute | solution.py:23
  40.3 24.0 %collective-permute-start = (f32[24]{0:T(128)S(1)}, f32[24]{0:T(128)S(1)}, u32[]{:S(2)}, u32[]{:S(2)}) collective-permute-start(f32[24]{0:T(128)S(1)} %get-tuple-element.439), channel_id=1, source_target_pairs={{4,0},{8,4},{12,8},{16,12},{20,16},{24,20},{28,24},{5,1},{9,5},{13... | collective-permute-start | bytes 296 | tf_op jit(solution)/shard_map/ppermute | solution.py:23
  41.6 22.7 %collective-permute-start.1 = (f32[24]{0:T(128)S(1)}, f32[24]{0:T(128)S(1)}, u32[]{:S(2)}, u32[]{:S(2)}) collective-permute-start(f32[24]{0:T(128)S(1)} %get-tuple-element.440), channel_id=1, source_target_pairs={{0,4},{4,8},{8,12},{12,16},{16,20},{20,24},{24,28},{1,5},{5,9},{9,... | collective-permute-start | bytes 296 | tf_op jit(solution)/shard_map/ppermute | solution.py:23
  142.6 66.7 %collective-permute-start.4 = (f32[5,3072]{1,0:T(8,128)S(1)}, f32[5,3072]{1,0:T(8,128)S(1)}, u32[]{:S(2)}, u32[]{:S(2)}) collective-permute-start(f32[5,3072]{1,0:T(8,128)S(1)} %bitcast.309), channel_id=1, source_target_pairs={{0,4},{4,8},{8,12},{12,16},{16,20},{20,24},{24,28},{1,5},{5,9},{9,... | collective-permute-start | bytes 184328 | tf_op jit(solution)/shard_map/ppermute | solution.py:23
  208.0 3.2 collective-permute-start.5
  241.3 51.1 %collective-permute-start.7 = (f32[3,3072]{1,0:T(4,128)S(1)}, f32[3,3072]{1,0:T(4,128)S(1)}, u32[]{:S(2)}, u32[]{:S(2)}) collective-permute-start(f32[3,3072]{1,0:T(4,128)S(1)} %get-tuple-element.434), channel_id=1, source_target_pairs={{0,4},{4,8},{8,12},{12,16},{16,20},{20,24},{24,28},{1,5},{5,9},{9,... | collective-permute-start | bytes 110600 | tf_op jit(solution)/shard_map/ppermute | solution.py:23
  245.0 47.4 %collective-permute-start.6 = (f32[3,3072]{1,0:T(4,128)S(1)}, f32[3,3072]{1,0:T(4,128)S(1)}, u32[]{:S(2)}, u32[]{:S(2)}) collective-permute-start(f32[3,3072]{1,0:T(4,128)S(1)} %get-tuple-element.433), channel_id=1, source_target_pairs={{4,0},{8,4},{12,8},{16,12},{20,16},{24,20},{28,24},{5,1},{9,5},{13... | collective-permute-start | bytes 110600 | tf_op jit(solution)/shard_map/ppermute | solution.py:23
  371.1 64.6 %collective-permute-start.8 = (f32[5,3072]{1,0:T(8,128)S(1)}, f32[5,3072]{1,0:T(8,128)S(1)}, u32[]{:S(2)}, u32[]{:S(2)}) collective-permute-start(f32[5,3072]{1,0:T(8,128)S(1)} %bitcast.310), channel_id=1, source_target_pairs={{0,4},{4,8},{8,12},{12,16},{16,20},{20,24},{24,28},{1,5},{5,9},{9,... | collective-permute-start | bytes 184328 | tf_op jit(solution)/shard_map/ppermute | solution.py:23
  434.4 5.8 %collective-permute-start.9 = (f32[5,3072]{1,0:T(8,128)S(1)}, f32[5,3072]{1,0:T(8,128)S(1)}, u32[]{:S(2)}, u32[]{:S(2)}) collective-permute-start(f32[5,3072]{1,0:T(8,128)S(1)} %bitcast.312), channel_id=1, source_target_pairs={{4,0},{8,4},{12,8},{16,12},{20,16},{24,20},{28,24},{5,1},{9,5},{13... | collective-permute-start | bytes 184328 | tf_op jit(solution)/shard_map/ppermute | solution.py:23
where the time goes:
time: 503 us; the launch traced here: 501 us
  starting transfers between devices  147 us (29%)
  blocking collectives  105 us (21%)
  local copies, waits for them, and re-layouts  104 us (21%)
  matrix products  53.8 us (11%)
  other arithmetic  41.6 us (8%)
  loops' own time  38.1 us (8%)
  waiting for transfers between devices  6.42 us (1%)
    ppermute x10, starting transfers between devices, from_behind(): lax.ppermute(value, axis, [(source, source + steps) for source in range(i...  147 us
    psum x2, blocking collectives, on_device(): energy_sum, share_sum = lax.psum((energy_part, share_part), ('line', 'seg'))  86.1 us
    gather x144, local copies, waits for them, and re-layouts  58.8 us
    dot_general x2, matrix products, on_device(): jnp.dot(linear_part, own_points, precision=lax.Precision.HIGHEST, preferr...  33.5 us
    gather x2, local copies, waits for them, and re-layouts, on_device(): jnp.take(own_points, safe_rows.reshape(-1), axis=1)  23 us
    another operation x24, loops' own time, one_turn(): return lax.cond(jnp.any(turn_cells >= 0), compute, skipped, 0)  21.8 us
    psum x2, blocking collectives, on_device(): gram_sum, cross_sum = lax.psum((gram_matrix, cross_matrix), 'seg')  19.2 us
    dot_general x12, matrix products, match_block(): lax.dot_general(target, posterior, (((1,), (1,)), ((), ())), precision=la...  16.8 us
  transfers between devices with their start and end apart: 10, of which 2 were waited for; matrix products, arithmetic and copies ran while one was open for 3% of the time, Pallas kernels for 0%

commit v1 on v0

v1 whole, which is shorter than its diff:
```python
import functools
import math

import jax
import jax.numpy as jnp
from jax import lax
from jax.experimental import pallas as pl
from jax.experimental.pallas import tpu as pltpu
from jax.sharding import PartitionSpec as P

NCELL = 16
CT = 512
BLOCK = 128
MARGIN = NCELL * CT
MROWS = MARGIN // 128
TILES = CT // 128
GROUPS = BLOCK // 8
UNROLL = 2

OUTLIER_MASS = 1.0
SPREAD_START = 0.05
PRIOR_TOP = 0.05
PRIOR_BOTTOM = 1.0
REGULARIZE = 1.0
LOG2E = math.log2(math.e)

F32 = jnp.float32
TILE = (8, 128)
ONE = 24
SHARE = ONE + 3
ENERGY = ONE + 4
QUAD = 32


def iota(axis):
    return lax.broadcasted_iota(jnp.int32, TILE, axis)


def spread_out(value):
    return jnp.broadcast_to(value, TILE)


def gather_kernel(low_ref, up_ref, rows_ref, source_ref):
    slot_rows = rows_ref.shape[0]
    count = slot_rows // 8
    upward = (iota(0) & 1) == 1
    high, low, live = [], [], []
    for v in range(count):
        row = rows_ref[8 * v : 8 * v + 8, :]
        live.append((row >= 0).astype(F32))
        spot = jnp.maximum(row, 0) & (MARGIN - 1)
        high.append(spot >> 7)
        low.append(spot & 127)

    def step(r, carry):
        table = []
        for k in range(3):
            a = spread_out(low_ref[k, pl.ds(r, 1), :])
            b = spread_out(up_ref[k, pl.ds(r, 1), :])
            table.append(jnp.where(upward, b, a))
        out = []
        for v in range(count):
            hit = high[v] == r
            for k in range(3):
                got = jnp.take_along_axis(table[k], low[v], axis=1, mode="promise_in_bounds")
                out.append(jnp.where(hit, got, carry[3 * v + k]))
        return tuple(out)

    done = lax.fori_loop(0, MROWS, step, tuple(jnp.zeros(TILE, F32) for _ in range(3 * count)), unroll=4)
    for v in range(count):
        for k in range(3):
            source_ref[k, 8 * v : 8 * v + 8, :] = done[3 * v + k]
        source_ref[3, 8 * v : 8 * v + 8, :] = live[v]


def gather(points, rows):
    last = points.shape[1] // MROWS - 1
    slot_rows = rows.shape[0]
    return pl.pallas_call(
        gather_kernel,
        grid=(1,),
        in_specs=[
            pl.BlockSpec((3, MROWS, 128), lambda i: (0, 0, 0)),
            pl.BlockSpec((3, MROWS, 128), lambda i: (0, last, 0)),
            pl.BlockSpec((slot_rows, 128), lambda i: (0, 0)),
        ],
        out_specs=pl.BlockSpec((4, slot_rows, 128), lambda i: (0, 0, 0)),
        out_shape=jax.ShapeDtypeStruct((4, slot_rows, 128), F32),
        name="gather_sources",
    )(points, points, rows)


def apply_pose(coefs, xyz):
    out = []
    for k in range(3):
        total = coefs[3 * k] * xyz[0]
        total = total + coefs[3 * k + 1] * xyz[1]
        total = total + coefs[3 * k + 2] * xyz[2]
        out.append(total + coefs[9 + k])
    return out


def match(own, nbrs, negc, dirs, cells_ref, source_ref, margin_refs, world_ref, moved_ref, column_ref, out_ref):
    slot_rows = source_ref.shape[1]
    for v in range(slot_rows // 8):
        xyz = [source_ref[k, 8 * v : 8 * v + 8, :] for k in range(3)]
        for k, value in enumerate(apply_pose(own, xyz)):
            moved_ref[k, 8 * v : 8 * v + 8, :] = value
    for k in range(3):
        column_ref[k] = jnp.transpose(moved_ref[k])
    for side in range(2):
        for v in range(MROWS // 8):
            xyz = [margin_refs[side][k * MROWS + 8 * v : k * MROWS + 8 * v + 8, :] for k in range(3)]
            for k, value in enumerate(apply_pose(nbrs[side], xyz)):
                world_ref[side, k, 8 * v : 8 * v + 8, :] = value
    lane, sub = iota(1), iota(0)
    if out_ref is not None:
        out_ref[...] = jnp.zeros(out_ref.shape, F32)

    def one_block(side, row, cell):
        first = jnp.maximum(cell, 0) * TILES
        target = [
            [spread_out(world_ref[side, k, pl.ds(first + t, 1), :]) for t in range(TILES)] for k in range(3)
        ]
        pick = jnp.full(TILE, row, jnp.int32)
        parts = []
        for g in range(GROUPS):
            m = [
                jnp.take_along_axis(column_ref[k, 8 * g : 8 * g + 8, :], pick, axis=1, mode="promise_in_bounds")
                for k in range(3)
            ]
            sums = None
            for t in range(TILES):
                d = [m[k] - target[k][t] for k in range(3)]
                dist = d[0] * d[0] + d[1] * d[1] + d[2] * d[2]
                weight = jnp.exp2(dist * negc)
                terms = [weight * target[k][t] for k in range(3)] + [weight, weight * dist]
                sums = terms if sums is None else [a + b for a, b in zip(sums, terms)]
            part = jnp.zeros(TILE, F32)
            for q in range(5):
                part = jnp.where(lane == q, jnp.sum(sums[q], axis=1, keepdims=True), part)
            parts.append(part)
        flat = jnp.transpose(jnp.concatenate(parts, axis=0))[:8, :]
        result = flat * (1.0 / (spread_out(flat[3:4, :]) + OUTLIER_MASS))
        xt = [spread_out(source_ref[k, pl.ds(row, 1), :]) for k in range(4)]
        result = result * xt[3]
        return result, xt

    x_left = (sub < 3).astype(F32)
    y_left = ((sub == 3) | (sub == 4)).astype(F32)
    z_left = (sub == 5).astype(F32)
    x_right = (sub == 0).astype(F32)
    y_right = ((sub == 1) | (sub == 3)).astype(F32)
    z_right = ((sub == 2) | (sub == 4) | (sub == 5)).astype(F32)

    def add_block(carry, side, row, cell):
        result, xt = one_block(side, row, cell)
        if out_ref is not None:
            for q in range(5):
                out_ref[q, pl.ds(row, 1), :] = result[q : q + 1, :]
        factor = (x_left * xt[0] + y_left * xt[1] + z_left * xt[2]) * (
            x_right * xt[0] + y_right * xt[1] + z_right * xt[2]
        )
        share = spread_out(result[3:4, :])
        return (
            carry[0] + result * xt[0],
            carry[1] + result * xt[1],
            carry[2] + result * xt[2],
            carry[3] + result,
            carry[4] + share * factor,
        )

    carry = tuple(jnp.zeros(TILE, F32) for _ in range(5))
    blocks = cells_ref.shape[1]
    for side in range(2):
        d = dirs[side]

        def filled(b, n, d=d):
            return n + (cells_ref[d, b] >= 0).astype(jnp.int32)

        live_blocks = lax.fori_loop(0, blocks, filled, jnp.int32(0))

        def step(i, carry, side=side, d=d):
            for u in range(UNROLL):
                b = i * UNROLL + u
                carry = add_block(carry, side, 2 * b + d, cells_ref[d, b])
            return carry

        carry = lax.fori_loop(0, (live_blocks + UNROLL - 1) // UNROLL, step, carry)
    return carry


def pack_sums(sums, out_ref):
    lane, sub = iota(1), iota(0)
    total = jnp.zeros(TILE, F32)
    for c in range(5):
        total = total + jnp.where(lane == 8 * c + sub, jnp.sum(sums[c], axis=1, keepdims=True), 0.0)
    row = jnp.sum(total, axis=0, keepdims=True)
    out_ref[...] = jnp.broadcast_to(row, out_ref.shape)


def pose_of_row(row):
    return [spread_out(row[:, j : j + 1]) for j in range(12)]


def sides_of(line):
    odd = line & 1
    return [1 - odd, odd]


def first_kernel(cells_ref, pose_ref, source_ref, margin_a, margin_b, sums_ref, world_ref, moved_ref, column_ref):
    line = lax.axis_index("line")
    own = pose_of_row(pose_ref[...])
    nbrs = [pose_of_row(margin[3 * MROWS : 3 * MROWS + 1, :]) for margin in (margin_a, margin_b)]
    negc = F32(-LOG2E / (2.0 * SPREAD_START))
    sums = match(
        own, nbrs, negc, sides_of(line), cells_ref, source_ref, (margin_a, margin_b), world_ref, moved_ref, column_ref, None
    )
    pack_sums(sums, sums_ref)


def solve(totals, old):
    def at(q):
        return spread_out(totals[:, q : q + 1])

    gram = {}
    for n, (a, b) in enumerate([(0, 0), (0, 1), (0, 2), (1, 1), (1, 2), (2, 2)]):
        gram[a, b] = at(QUAD + n)
    for a in range(3):
        gram[a, 3] = at(8 * a + 3)
    gram[3, 3] = at(SHARE)
    for a in range(4):
        gram[a, a] = gram[a, a] + REGULARIZE
    lower, diag, inverse = {}, [], []
    for j in range(4):
        scaled = [lower[j, k] * diag[k] for k in range(j)]
        pivot = gram[j, j]
        for k in range(j):
            pivot = pivot - lower[j, k] * scaled[k]
        diag.append(pivot)
        inverse.append(1.0 / pivot)
        for i in range(j + 1, 4):
            value = gram[j, i]
            for k in range(j):
                value = value - lower[i, k] * scaled[k]
            lower[i, j] = value * inverse[j]
    new = [None] * 12
    for k in range(3):
        right = []
        for m in range(4):
            j = 3 * k + m if m < 3 else 9 + k
            value = at(8 * m + k) + REGULARIZE * spread_out(old[:, j : j + 1])
            for n in range(m):
                value = value - lower[m, n] * right[n]
            right.append(value)
        found = [None] * 4
        for m in reversed(range(4)):
            value = right[m] * inverse[m]
            for n in range(m + 1, 4):
                value = value - lower[n, m] * found[n]
            found[m] = value
        for m in range(4):
            new[3 * k + m if m < 3 else 9 + k] = found[m]
    return new


def line_sum(all_ref, line, segs):
    return jnp.sum(all_ref[pl.ds(line * segs, segs), :], axis=0, keepdims=True)


def new_spread(all_ref):
    everything = jnp.sum(all_ref[...], axis=0, keepdims=True)
    top = spread_out(everything[:, ENERGY : ENERGY + 1]) + PRIOR_TOP
    return top / (3.0 * spread_out(everything[:, SHARE : SHARE + 1]) + PRIOR_BOTTOM)


def pose_row(new, sub):
    lane = iota(1)
    row = jnp.zeros(TILE, F32)
    for j in range(12):
        row = jnp.where(lane == j, spread_out(new[j][sub : sub + 1, :]), row)
    return row


def second_kernel(
    lines, segs, cells_ref, pose_ref, all_ref, source_ref, margin_a, margin_b,
    sums_ref, pose_out_ref, out_ref, world_ref, moved_ref, column_ref,
):
    line = lax.axis_index("line")
    dirs = sides_of(line)
    partner = [jnp.clip(line + 2 * d - 1, 0, lines - 1) for d in dirs]
    sub = iota(0)

    def stacked(a, b, c):
        return jnp.where(sub == 0, spread_out(a), jnp.where(sub == 1, spread_out(b), spread_out(c)))

    totals = stacked(*[line_sum(all_ref, n, segs) for n in (line, partner[0], partner[1])])
    old = stacked(pose_ref[...], margin_a[3 * MROWS : 3 * MROWS + 1, :], margin_b[3 * MROWS : 3 * MROWS + 1, :])
    new = solve(totals, old)
    negc = (-0.5 * LOG2E) / new_spread(all_ref)
    own, near_a, near_b = [[spread_out(value[n : n + 1, :]) for value in new] for n in range(3)]
    pose_out_ref[...] = pose_row(new, 0)[:1, :]
    sums = match(
        own, [near_a, near_b], negc, dirs, cells_ref, source_ref, (margin_a, margin_b), world_ref, moved_ref, column_ref, out_ref
    )
    pack_sums(sums, sums_ref)


def last_kernel(segs, pose_ref, all_ref, fitted_ref, spread_ref):
    line = lax.axis_index("line")
    totals = spread_out(line_sum(all_ref, line, segs))
    new = solve(totals, spread_out(pose_ref[...]))
    fitted_ref[...] = pose_row(new, 0)[:1, :12]
    spread_ref[...] = new_spread(all_ref)[:1, :1]


def vmem(count):
    return [pl.BlockSpec(memory_space=pltpu.VMEM)] * count


SMEM = pl.BlockSpec(memory_space=pltpu.SMEM)
PARAMS = pltpu.CompilerParams(vmem_limit_bytes=32 * 1024 * 1024)


def scratch():
    return [
        pltpu.VMEM((2, 3, MROWS, 128), F32),
        pltpu.VMEM((3, 128, 128), F32),
        pltpu.VMEM((3, 128, 128), F32),
    ]


def exchange(sums):
    return lax.all_to_all(sums, ("line", "seg"), 0, 0)


def on_device(lines, segs, points, rows, cells, pose):
    own_points = points.reshape(3, -1, 128)
    slots = rows.shape[-1]
    blocks = slots // BLOCK
    row_list = rows.reshape(2, blocks, 128).transpose(1, 0, 2).reshape(2 * blocks, 128)
    cell_ids = cells.reshape(2, blocks)
    devices = lines * segs
    odd = lax.axis_index("line") & 1
    tail = own_points.shape[1] - MROWS
    pose_line = jnp.pad(pose.reshape(1, 12), ((0, 0), (0, 116)))
    pose_tile = jnp.pad(pose_line, ((0, 7), (0, 0)))

    def margin_at(first):
        part = lax.dynamic_slice_in_dim(own_points, first, MROWS, 1)
        return jnp.concatenate([part.reshape(3 * MROWS, 128), pose_tile], axis=0)

    pairs_a = [(i, i ^ 1) for i in range(lines) if i ^ 1 < lines]
    pairs_b = [(i, ((i + 1) ^ 1) - 1) for i in range(lines)]
    pairs_b = [(i, j) for i, j in pairs_b if 0 <= j < lines]
    margin_a = lax.ppermute(margin_at(jnp.where(odd == 1, 0, tail)), "line", pairs_a)
    margin_b = lax.ppermute(margin_at(jnp.where(odd == 1, tail, 0)), "line", pairs_b)
    source = gather(own_points, row_list)
    sums_shape = jax.ShapeDtypeStruct((devices, 128), F32)
    pair_ops = 2 * blocks * BLOCK * CT
    cost = pl.CostEstimate(flops=18 * pair_ops, bytes_accessed=1 << 20, transcendentals=pair_ops)
    sums = pl.pallas_call(
        first_kernel,
        in_specs=[SMEM] + vmem(4),
        out_specs=vmem(1)[0],
        out_shape=sums_shape,
        scratch_shapes=scratch(),
        compiler_params=PARAMS,
        cost_estimate=cost,
        name="match_first",
    )(cell_ids, pose_line, source, margin_a, margin_b)
    everyone = exchange(sums)
    sums, pose_line, result = pl.pallas_call(
        functools.partial(second_kernel, lines, segs),
        in_specs=[SMEM] + vmem(5),
        out_specs=vmem(3),
        out_shape=[
            sums_shape,
            jax.ShapeDtypeStruct((1, 128), F32),
            jax.ShapeDtypeStruct((5, 2 * blocks, 128), F32),
        ],
        scratch_shapes=scratch(),
        compiler_params=PARAMS,
        cost_estimate=cost,
        name="match_second",
    )(cell_ids, pose_line, everyone, source, margin_a, margin_b)
    everyone = exchange(sums)
    fitted, spread = pl.pallas_call(
        functools.partial(last_kernel, segs),
        in_specs=vmem(2),
        out_specs=vmem(2),
        out_shape=[jax.ShapeDtypeStruct((1, 12), F32), jax.ShapeDtypeStruct((1, 1), F32)],
        name="solve_last",
    )(pose_line, everyone)
    result = result.reshape(5, blocks, 2, 128).transpose(2, 0, 1, 3).reshape(1, 1, 2, 5, slots)
    return (result, fitted.reshape(12, 1), spread.reshape(1))


def solution(mesh):
    return jax.shard_map(
        functools.partial(on_device, mesh.shape["line"], mesh.shape["seg"]),
        mesh=mesh,
        in_specs=(
            P("line", "seg", None, None),
            P("line", "seg", None, None),
            P("line", "seg", None, None),
            P(None, "line"),
        ),
        out_specs=(P("line", "seg", None, None, None), P(None, "line"), P()),
        check_vma=False,
    )
```

time: 503 us -> 174 us (0.35)
  starting transfers between devices: 147 us -> 1.17 us
  local copies, waits for them, and re-layouts: 104 us -> 3.7 us
  Pallas kernels: 0 us -> 78.4 us
  matrix products: 53.8 us -> 0 us
  other arithmetic: 41.6 us -> 0.02 us
  loops' own time: 38.1 us -> 0 us
  blocking collectives: 105 us -> 89.3 us
  waiting for transfers between devices: 6.42 us -> 0.01 us
    ppermute x10 -> x2, starting transfers between devices: 147 us -> 1.17 us  [the longest x1 0.66 us: on_device(): lax.ppermute(margin_at(jnp.where(odd == 1, tail, 0)), 'line', pairs_b)]
    psum x4 -> x0, blocking collectives: 105 us -> none  [the longest x2 86.1 us: on_device(): energy_sum, share_sum = lax.psum((energy_part, share_part), ('line', 'seg'))]
    all_to_all x0 -> x2, blocking collectives: none -> 89.3 us  [exchange(): return lax.all_to_all(sums, ('line', 'seg'), 0, 0)]
    gather x146 -> x0, local copies, waits for them, and re-layouts: 81.8 us -> none
    pallas_call x0 -> x4, Pallas kernels: none -> 78.4 us  [the longest x1 36.3 us: on_device(): pl.pallas_call(functools.partial(second_kernel, lines, segs), in_specs=[S...]
    dot_general x20 -> x0, matrix products: 53 us -> none  [the longest x2 33.5 us: on_device(): jnp.dot(linear_part, own_points, precision=lax.Precision.HIGHEST, preferr...]
    another operation x38 -> x0, loops' own time: 38.1 us -> none  [the longest x24 21.8 us: one_turn(): return lax.cond(jnp.any(turn_cells >= 0), compute, skipped, 0)]
    reduce_sum x26 -> x0, other arithmetic: 17.7 us -> none  [the longest x12 8.99 us: match_block(): energy_row = jnp.sum(posterior * distance, axis=1)]
  transfers between devices with their start and end apart: 10 -> 2, of which waited for: 2 -> 0; matrix products, arithmetic and copies ran while one was open for 3% -> 0% of each run, Pallas kernels for 0% -> 3%
where the time goes in v1:
time: 174 us; the launch traced here: 173 us
  blocking collectives  89.3 us (51%)
  Pallas kernels  78.4 us (45%)
  local copies, waits for them, and re-layouts  3.7 us (2%)
    all_to_all x2, blocking collectives, exchange(): return lax.all_to_all(sums, ('line', 'seg'), 0, 0)  89.3 us
    pallas_call x1, Pallas kernels, on_device(): pl.pallas_call(functools.partial(second_kernel, lines, segs), in_specs=[S...  36.3 us
    pallas_call x1, Pallas kernels, on_device(): pl.pallas_call(first_kernel, in_specs=[SMEM] + vmem(4), out_specs=vmem(1)...  35.6 us
    pallas_call x1, Pallas kernels, gather(): pl.pallas_call(gather_kernel, grid=(1,), in_specs=[pl.BlockSpec((3, MROWS...  5.09 us
  transfers between devices with their start and end apart: 2, of which 0 were waited for; matrix products, arithmetic and copies ran while one was open for 0% of the time, Pallas kernels for 3%

profile of v1, /device:TPU:0, one launch (start us, length us, event | category | flops | bytes accessed | tf_op | source)
XLA Modules:
  0.0 173.2 jit_solution(13316114205635204103)
XLA Ops:
  0.6 0.0 copy-start.3
  0.6 0.6 copy-done.3
  1.3 1.0 constant_dynamic-slice_fusion
  2.3 0.5 collective-permute-start
  2.8 0.7 collective-permute-start.1
  3.5 5.1 %gather_sources.1.source_ref = f32[4,48,128]{2,1,0:T(8,128)} custom-call(f32[3,256,128]{2,1,0:T(8,128)} %bitcast.31, f32[3,256,128]{2,1,0:T(8,128)} %bitcast.32, s32[48,128]{1,0:T(8,128)} %bitcast.36), custom_call_target="tpu_custom_call" | custom-call | tf_op jit(solution)/shard_map/gather_sources/pallas_call | solution.py:79
  8.6 0.0 copy-start.2
  8.6 0.0 collective-permute-done.margin_a
  8.6 0.0 collective-permute-done.1.margin_b
  8.6 0.7 copy-done.2
  9.2 0.0 copy-start
  9.2 0.9 copy-done
  10.1 35.6 %match_first.1 = f32[32,128]{1,0:T(8,128)S(1)} custom-call(s32[2,24]{1,0:T(2,128)S(1)} %bitcast.28, f32[1,128]{1,0:T(1,128)S(1)} %pad.8.pose_ref, f32[4,48,128]{2,1,0:T(8,128)S(1)} %copy-done, f32[200,128]{1,0:T(8,128)S(1)} %collective-permute-done.margin_a, f32[200,128]{1,0:T(8,128)S(1)} %collective-permute-done.1.margin_b), custom_call_target="tpu_custom_call" | custom-call | flops 56623104 | bytes 1048576 | tf_op jit(solution)/shard_map/match_first/pallas_call | solution.py:362
  45.7 47.0 %all_to_all.22 = f32[32,1,128]{2,1,0:T(1,128)S(1)} all-to-all(f32[32,1,128]{2,1,0:T(1,128)S(1)} %bitcast.27), channel_id=1, replica_groups=mesh['line'=8,'seg'=4] {'line','seg'}, dimensions={0} | all-to-all | bytes 32768 | tf_op jit(solution)/shard_map/all_to_all | solution.py:334
  92.7 36.3 %match_second.1 = (f32[32,128]{1,0:T(8,128)S(1)}, f32[1,128]{1,0:T(1,128)S(1)}, f32[5,48,128]{2,1,0:T(8,128)}) custom-call(s32[2,24]{1,0:T(2,128)S(1)} %bitcast.29, f32[1,128]{1,0:T(1,128)S(1)} %pad.8.pose_ref, f32[32,128]{1,0:T(8,128)S(1)} %bitcast.25, f32[4,48,128]{2,1,0:T(8,128)S(1)} %copy-done, f32[200,128]{1,0:T(8,128)S(1)} %collective-permute-done.margin_a, ...), custom_call_target="tpu_custom_call" | custom-call | flops 56623104 | bytes 1048576 | tf_op jit(solution)/shard_map/match_second/pallas_call | solution.py:373
  129.0 0.0 copy-start.1
  129.0 0.5 copy-done.1
  129.6 42.3 %all_to_all.23 = f32[32,1,128]{2,1,0:T(1,128)} all-to-all(f32[32,1,128]{2,1,0:T(1,128)S(1)} %bitcast.26), channel_id=1, replica_groups=mesh['line'=8,'seg'=4] {'line','seg'}, dimensions={0} | all-to-all | bytes 32768 | tf_op jit(solution)/shard_map/all_to_all | solution.py:334
  171.8 1.4 solve_last.1
  (2 shorter events, 0.0 us)
Async XLA Ops:
  0.6 0.7 copy-start.3
  2.3 6.3 %collective-permute-start = (f32[200,128]{1,0:T(8,128)S(1)}, f32[200,128]{1,0:T(8,128)S(1)}, u32[]{:S(2)}, u32[]{:S(2)}) collective-permute-start(f32[200,128]{1,0:T(8,128)S(1)} %get-tuple-element.16), channel_id=1, source_target_pairs={{0,4},{4,0},{8,12},{12,8},{16,20},{20,16},{24,28},{28,24},{1,5},{5... | collective-permute-start | bytes 307208 | tf_op jit(solution)/shard_map/ppermute | solution.py:356
  2.8 5.8 %collective-permute-start.1 = (f32[200,128]{1,0:T(8,128)S(1)}, f32[200,128]{1,0:T(8,128)S(1)}, u32[]{:S(2)}, u32[]{:S(2)}) collective-permute-start(f32[200,128]{1,0:T(8,128)S(1)} %get-tuple-element.15), channel_id=1, source_target_pairs={{4,8},{8,4},{12,16},{16,12},{20,24},{24,20},{5,9},{9,5},{13,17},{1... | collective-permute-start | bytes 307208 | tf_op jit(solution)/shard_map/ppermute | solution.py:357
  8.6 0.7 copy-start.2
  9.2 0.9 copy-start
  129.0 0.5 copy-start.1

commit v2 on v1

--- a/solution.py
+++ b/solution.py
@@ -15,7 +15,8 @@
 MROWS = MARGIN // 128
 TILES = CT // 128
 GROUPS = BLOCK // 8
-UNROLL = 2
+UNROLL = 8
+QUICK_LIMIT = 1000.0
 
 OUTLIER_MASS = 1.0
 SPREAD_START = 0.05
@@ -25,6 +26,7 @@
 LOG2E = math.log2(math.e)
 
 F32 = jnp.float32
+BF16 = jnp.bfloat16
 TILE = (8, 128)
 ONE = 24
 SHARE = ONE + 3
@@ -100,7 +102,159 @@
     return out
 
 
-def match(own, nbrs, negc, dirs, cells_ref, source_ref, margin_refs, world_ref, moved_ref, column_ref, out_ref):
+def column(coefs, first, stride):
+    sub = iota(0)
+    out = jnp.zeros(TILE, F32)
+    for k in range(3):
+        out = jnp.where(sub == k, coefs[first + stride * k], out)
+    return out
+
+
+def columns(coefs):
+    return [column(coefs, k, 3) for k in range(3)] + [column(coefs, 9, 1)]
+
+
+def squared_length(value):
+    square = value * value
+    return spread_out(square[0:1, :]) + spread_out(square[1:2, :]) + spread_out(square[2:3, :])
+
+
+def three_parts(value):
+    high = value.astype(BF16).astype(F32)
+    rest = value - high
+    middle = rest.astype(BF16).astype(F32)
+    return high, middle, rest - middle
+
+
+def combine(cols, xyz):
+    return cols[0] * xyz[0] + cols[1] * xyz[1] + cols[2] * xyz[2]
+
+
+def prepare(near, margin_refs, phi_ref):
+    sub = iota(0)
+
+    def step(r, longest):
+        for side in range(2):
+            xyz = [spread_out(margin_refs[side][pl.ds(k * MROWS + r, 1), :]) for k in range(3)]
+            y = combine(near[side], xyz)
+            length = squared_length(y)
+            longest = jnp.maximum(longest, length)
+            high, middle, low = three_parts(jnp.where(sub == 3, length, jnp.where(sub == 4, 1.0, y)))
+            spot = pl.ds(pl.multiple_of(r * 128, 128), 128)
+            for i, pair in enumerate(((high, middle), (low, high), (middle, high))):
+                phi_ref[side, 16 * i : 16 * i + 16, spot] = jnp.concatenate(pair, axis=0).astype(BF16)
+        return longest
+
+    return lax.fori_loop(0, MROWS, step, jnp.zeros(TILE, F32), unroll=4)
+
+
+def longest_source(own, near, dirs, source_ref):
+    longest = jnp.zeros(TILE, F32)
+    for v in range(source_ref.shape[1] // 8):
+        rows = slice(8 * v, 8 * v + 8)
+        xyz = [source_ref[k, rows, :] for k in range(3)]
+        moved = apply_pose(own, xyz)
+        for side in range(2):
+            square = sum((moved[k] - near[side][9 + k]) ** 2 for k in range(3))
+            listed = (iota(0) & 1) == dirs[side]
+            longest = jnp.maximum(longest, jnp.where(listed, square * source_ref[3, rows, :], 0.0))
+    return longest
+
+
+def quick_block(negc, exact, own, near, phi_ref, source_ref, side, row, cell):
+    sub = iota(0)
+    xt = [spread_out(source_ref[k, pl.ds(row, 1), :]) for k in range(4)]
+    m = combine(own, xt) + (own[3] - near[side][3])
+    length = squared_length(m)
+    coef = jnp.where(sub == 3, negc, jnp.where(sub == 4, negc * length, (-2.0 * negc) * m))
+    high, middle, low = three_parts(coef)
+    stack = jnp.concatenate([high, high, high, middle, middle, low], axis=0)
+    phi = phi_ref[side, :, pl.ds(pl.multiple_of(jnp.maximum(cell, 0) * CT, CT), CT)]
+    power = jnp.dot(jnp.transpose(stack).astype(BF16), phi, preferred_element_type=F32)
+    weight = jnp.exp2(power)
+    top = weight.astype(BF16)
+    last = (((1,), (1,)), ((), ()))
+    sums = lax.dot_general(phi[:32], top, last, preferred_element_type=F32)
+    if exact:
+        rest = (weight - top.astype(F32)).astype(BF16)
+        sums = sums + lax.dot_general(phi[:32], rest, last, preferred_element_type=F32)
+    sums = sums[0:8] + sums[8:16] + sums[16:24]
+    total = spread_out(sums[4:5, :])
+    around = combine([spread_out(m[k : k + 1, :]) for k in range(3)], [spread_out(sums[k : k + 1, :]) for k in range(3)])
+    energy = spread_out(sums[3:4, :]) - 2.0 * around + length * total
+    raw = jnp.where(sub < 3, sums + near[side][3] * total, jnp.where(sub == 3, total, jnp.where(sub == 4, energy, 0.0)))
+    return raw * (xt[3] / (total + OUTLIER_MASS)), xt
+
+
+def match(exact, own, nbrs, negc, dirs, cells_ref, source_ref, margin_refs, scratch_refs, out_ref):
+    phi_ref, sums_ref, world_ref, moved_ref, column_ref = scratch_refs
+    own_cols, near_cols = columns(own), [columns(near) for near in nbrs]
+    size = prepare(near_cols, margin_refs, phi_ref) + longest_source(own, nbrs, dirs, source_ref)
+    quick = jnp.max(size * -negc) <= QUICK_LIMIT
+    if out_ref is not None:
+        out_ref[...] = jnp.zeros(out_ref.shape, F32)
+
+    @pl.when(quick)
+    def _():
+        def block(side, row, cell):
+            return quick_block(negc, exact, own_cols, near_cols, phi_ref, source_ref, side, row, cell)
+
+        run_blocks(block, UNROLL, dirs, cells_ref, sums_ref, out_ref)
+
+    @pl.when(jnp.logical_not(quick))
+    def _():
+        block = careful_setup(own, nbrs, negc, source_ref, margin_refs, world_ref, moved_ref, column_ref)
+        run_blocks(block, 1, dirs, cells_ref, sums_ref, out_ref)
+
+    return [sums_ref[n] for n in range(5)]
+
+
+def run_blocks(one_block, unroll, dirs, cells_ref, sums_ref, out_ref):
+    sub = iota(0)
+    x_left = (sub < 3).astype(F32)
+    y_left = ((sub == 3) | (sub == 4)).astype(F32)
+    z_left = (sub == 5).astype(F32)
+    x_right = (sub == 0).astype(F32)
+    y_right = ((sub == 1) | (sub == 3)).astype(F32)
+    z_right = ((sub == 2) | (sub == 4) | (sub == 5)).astype(F32)
+
+    def add_block(carry, row, result, xt):
+        if out_ref is not None:
+            for q in range(5):
+                out_ref[q, pl.ds(row, 1), :] = result[q : q + 1, :]
+        factor = combine([x_left, y_left, z_left], xt) * combine([x_right, y_right, z_right], xt)
+        share = spread_out(result[3:4, :])
+        return (
+            carry[0] + result * xt[0],
+            carry[1] + result * xt[1],
+            carry[2] + result * xt[2],
+            carry[3] + result,
+            carry[4] + share * factor,
+        )
+
+    carry = tuple(jnp.zeros(TILE, F32) for _ in range(5))
+    blocks = cells_ref.shape[1]
+    for side in range(2):
+        d = dirs[side]
+
+        def filled(b, n, d=d):
+            return n + (cells_ref[d, b] >= 0).astype(jnp.int32)
+
+        live_blocks = lax.fori_loop(0, blocks, filled, jnp.int32(0))
+
+        def step(i, carry, side=side, d=d):
+            places = [i * unroll + u for u in range(unroll)]
+            found = [one_block(side, 2 * b + d, cells_ref[d, b]) for b in places]
+            for b, (result, xt) in zip(places, found):
+                carry = add_block(carry, 2 * b + d, result, xt)
+            return carry
+
+        carry = lax.fori_loop(0, (live_blocks + unroll - 1) // unroll, step, carry)
+    for n in range(5):
+        sums_ref[n] = carry[n]
+
+
+def careful_setup(own, nbrs, negc, source_ref, margin_refs, world_ref, moved_ref, column_ref):
     slot_rows = source_ref.shape[1]
     for v in range(slot_rows // 8):
         xyz = [source_ref[k, 8 * v : 8 * v + 8, :] for k in range(3)]
@@ -113,9 +267,7 @@
             xyz = [margin_refs[side][k * MROWS + 8 * v : k * MROWS + 8 * v + 8, :] for k in range(3)]
             for k, value in enumerate(apply_pose(nbrs[side], xyz)):
                 world_ref[side, k, 8 * v : 8 * v + 8, :] = value
-    lane, sub = iota(1), iota(0)
-    if out_ref is not None:
-        out_ref[...] = jnp.zeros(out_ref.shape, F32)
+    lane = iota(1)
 
     def one_block(side, row, cell):
         first = jnp.maximum(cell, 0) * TILES
@@ -141,53 +293,10 @@
                 part = jnp.where(lane == q, jnp.sum(sums[q], axis=1, keepdims=True), part)
             parts.append(part)
         flat = jnp.transpose(jnp.concatenate(parts, axis=0))[:8, :]
-        result = flat * (1.0 / (spread_out(flat[3:4, :]) + OUTLIER_MASS))
         xt = [spread_out(source_ref[k, pl.ds(row, 1), :]) for k in range(4)]
-        result = result * xt[3]
-        return result, xt
-
-    x_left = (sub < 3).astype(F32)
-    y_left = ((sub == 3) | (sub == 4)).astype(F32)
-    z_left = (sub == 5).astype(F32)
-    x_right = (sub == 0).astype(F32)
-    y_right = ((sub == 1) | (sub == 3)).astype(F32)
-    z_right = ((sub == 2) | (sub == 4) | (sub == 5)).astype(F32)
-
-    def add_block(carry, side, row, cell):
-        result, xt = one_block(side, row, cell)
-        if out_ref is not None:
-            for q in range(5):
-                out_ref[q, pl.ds(row, 1), :] = result[q : q + 1, :]
-        factor = (x_left * xt[0] + y_left * xt[1] + z_left * xt[2]) * (
-            x_right * xt[0] + y_right * xt[1] + z_right * xt[2]
-        )
-        share = spread_out(result[3:4, :])
-        return (
-            carry[0] + result * xt[0],
-            carry[1] + result * xt[1],
-            carry[2] + result * xt[2],
-            carry[3] + result,
-            carry[4] + share * factor,
-        )
-
-    carry = tuple(jnp.zeros(TILE, F32) for _ in range(5))
-    blocks = cells_ref.shape[1]
-    for side in range(2):
-        d = dirs[side]
-
-        def filled(b, n, d=d):
-            return n + (cells_ref[d, b] >= 0).astype(jnp.int32)
-
-        live_blocks = lax.fori_loop(0, blocks, filled, jnp.int32(0))
-
-        def step(i, carry, side=side, d=d):
-            for u in range(UNROLL):
-                b = i * UNROLL + u
-                carry = add_block(carry, side, 2 * b + d, cells_ref[d, b])
-            return carry
-
-        carry = lax.fori_loop(0, (live_blocks + UNROLL - 1) // UNROLL, step, carry)
-    return carry
+        return flat * (xt[3] / (spread_out(flat[3:4, :]) + OUTLIER_MASS)), xt
+
+    return one_block
 
 
 def pack_sums(sums, out_ref):
@@ -208,13 +317,13 @@
     return [1 - odd, odd]
 
 
-def first_kernel(cells_ref, pose_ref, source_ref, margin_a, margin_b, sums_ref, world_ref, moved_ref, column_ref):
+def first_kernel(cells_ref, pose_ref, source_ref, margin_a, margin_b, sums_ref, *scratch_refs):
     line = lax.axis_index("line")
     own = pose_of_row(pose_ref[...])
     nbrs = [pose_of_row(margin[3 * MROWS : 3 * MROWS + 1, :]) for margin in (margin_a, margin_b)]
-    negc = F32(-LOG2E / (2.0 * SPREAD_START))
+    negc = jnp.full(TILE, -LOG2E / (2.0 * SPREAD_START), F32)
     sums = match(
-        own, nbrs, negc, sides_of(line), cells_ref, source_ref, (margin_a, margin_b), world_ref, moved_ref, column_ref, None
+        False, own, nbrs, negc, sides_of(line), cells_ref, source_ref, (margin_a, margin_b), scratch_refs, None
     )
     pack_sums(sums, sums_ref)
 
@@ -284,7 +393,7 @@
 
 def second_kernel(
     lines, segs, cells_ref, pose_ref, all_ref, source_ref, margin_a, margin_b,
-    sums_ref, pose_out_ref, out_ref, world_ref, moved_ref, column_ref,
+    sums_ref, pose_out_ref, out_ref, *scratch_refs,
 ):
     line = lax.axis_index("line")
     dirs = sides_of(line)
@@ -301,7 +410,7 @@
     own, near_a, near_b = [[spread_out(value[n : n + 1, :]) for value in new] for n in range(3)]
     pose_out_ref[...] = pose_row(new, 0)[:1, :]
     sums = match(
-        own, [near_a, near_b], negc, dirs, cells_ref, source_ref, (margin_a, margin_b), world_ref, moved_ref, column_ref, out_ref
+        True, own, [near_a, near_b], negc, dirs, cells_ref, source_ref, (margin_a, margin_b), scratch_refs, out_ref
     )
     pack_sums(sums, sums_ref)
 
@@ -324,6 +433,8 @@
 
 def scratch():
     return [
+        pltpu.VMEM((2, 48, MARGIN), BF16),
+        pltpu.VMEM((5, 8, 128), F32),
         pltpu.VMEM((2, 3, MROWS, 128), F32),
         pltpu.VMEM((3, 128, 128), F32),
         pltpu.VMEM((3, 128, 128), F32),

time: 174 us -> 55.2 us (0.32)
  Pallas kernels: 78.4 us -> 18.5 us
  blocking collectives: 89.3 us -> 30.7 us
    all_to_all x2, blocking collectives: 89.3 us -> 30.7 us  [exchange(): return lax.all_to_all(sums, ('line', 'seg'), 0, 0)]
    pallas_call x1, Pallas kernels: 35.6 us -> 4.99 us  [on_device(): pl.pallas_call(first_kernel, in_specs=[SMEM] + vmem(4), out_specs=vmem(1)...]
    pallas_call x1, Pallas kernels: 36.3 us -> 7.07 us  [on_device(): pl.pallas_call(functools.partial(second_kernel, lines, segs), in_specs=[S...]
  transfers between devices with their start and end apart: 2 -> 2, of which waited for: 0 -> 0; matrix products, arithmetic and copies ran while one was open for 0% -> 0% of each run, Pallas kernels for 3% -> 9%
where the time goes in v2:
time: 55.2 us; the launch traced here: 54.8 us
  blocking collectives  30.7 us (56%)
  Pallas kernels  18.5 us (34%)
  local copies, waits for them, and re-layouts  3.7 us (7%)
  starting transfers between devices  1.17 us (2%)
  between operations  0.68 us (1%)
    all_to_all x2, blocking collectives, exchange(): return lax.all_to_all(sums, ('line', 'seg'), 0, 0)  30.7 us
    pallas_call x1, Pallas kernels, on_device(): pl.pallas_call(functools.partial(second_kernel, lines, segs), in_specs=[S...  7.07 us
    pallas_call x1, Pallas kernels, gather(): pl.pallas_call(gather_kernel, grid=(1,), in_specs=[pl.BlockSpec((3, MROWS...  5.09 us
    pallas_call x1, Pallas kernels, on_device(): pl.pallas_call(first_kernel, in_specs=[SMEM] + vmem(4), out_specs=vmem(1)...  4.99 us
    unnamed x8, local copies, waits for them, and re-layouts  2.74 us
    pallas_call x1, Pallas kernels, on_device(): pl.pallas_call(functools.partial(last_kernel, segs), in_specs=vmem(2), ou...  1.39 us
  transfers between devices with their start and end apart: 2, of which 0 were waited for; matrix products, arithmetic and copies ran while one was open for 0% of the time, Pallas kernels for 9%

profile of v2, /device:TPU:0, one launch (start us, length us, event | category | flops | bytes accessed | tf_op | source)
XLA Modules:
  0.0 54.8 jit_solution(7201881260355706514)
XLA Ops:
  0.6 0.0 copy-start.3
  0.6 0.6 %copy-done.3 = f32[12,1]{0,1:T(1,128)S(1)} copy-done((f32[12,1]{0,1:T(1,128)S(1)}, f32[12,1]{0,1:T(1,128)}, u32[]{:S(2)}) %copy-start.3) | copy-done | bytes 72
  1.3 1.0 %constant_dynamic-slice_fusion = (f32[3,64,128]{2,1,0:T(8,128)S(1)}, f32[3,64,128]{2,1,0:T(8,128)S(1)}) fusion(f32[3,256,128]{2,1,0:T(8,128)} %bitcast.30, s32[]{:T(128)S(6)} %select_n.10, s32[]{:T(128)S(6)} %select_n.9), kind=kLoop, calls=%fused_computation.4 | loop fusion | bytes 393224 | tf_op jit(solution)/shard_map/dynamic_slice | solution.py:461
  2.3 0.5 collective-permute-start
  2.8 0.7 %collective-permute-start.1 = (f32[200,128]{1,0:T(8,128)S(1)}, f32[200,128]{1,0:T(8,128)S(1)}, u32[]{:S(2)}, u32[]{:S(2)}) collective-permute-start(f32[200,128]{1,0:T(8,128)S(1)} %get-tuple-element.15), channel_id=1, source_target_pairs={{4,8},{8,4},{12,16},{16,12},{20,24},{24,20},{5,9},{9,5},{13,17},{1... | collective-permute-start | bytes 307208 | tf_op jit(solution)/shard_map/ppermute | solution.py:468
  3.5 5.1 %gather_sources.1.source_ref = f32[4,48,128]{2,1,0:T(8,128)} custom-call(f32[3,256,128]{2,1,0:T(8,128)} %bitcast.31, f32[3,256,128]{2,1,0:T(8,128)} %bitcast.32, s32[48,128]{1,0:T(8,128)} %bitcast.36), custom_call_target="tpu_custom_call" | custom-call | tf_op jit(solution)/shard_map/gather_sources/pallas_call | solution.py:81
  8.6 0.0 copy-start.2
  8.6 0.0 collective-permute-done.margin_a
  8.6 0.0 collective-permute-done.1.margin_b
  8.6 0.7 %copy-done.2 = s32[1,1,2,24]{3,2,1,0:T(2,128)S(1)} copy-done((s32[1,1,2,24]{3,2,1,0:T(2,128)S(1)}, s32[1,1,2,24]{3,2,1,0:T(2,128)}, u32[]{:S(2)}) %copy-start.2) | copy-done | bytes 216
  9.2 0.0 copy-start
  9.2 0.9 %copy-done = f32[4,48,128]{2,1,0:T(8,128)S(1)} copy-done((f32[4,48,128]{2,1,0:T(8,128)S(1)}, f32[4,48,128]{2,1,0:T(8,128)}, u32[]{:S(2)}) %copy-start) | copy-done | bytes 98328
  10.1 5.0 %match_first.1 = f32[32,128]{1,0:T(8,128)S(1)} custom-call(s32[2,24]{1,0:T(2,128)S(1)} %bitcast.28, f32[1,128]{1,0:T(1,128)S(1)} %pad.8.pose_ref, f32[4,48,128]{2,1,0:T(8,128)S(1)} %copy-done, f32[200,128]{1,0:T(8,128)S(1)} %collective-permute-done.margin_a, f32[200,128]{1,0:T(8,128)S(1)} %collective-permute-done.1.margin_b), custom_call_target="tpu_custom_call" | custom-call | flops 56623104 | bytes 1048576 | tf_op jit(solution)/shard_map/match_first/pallas_call | solution.py:473
  15.1 18.4 %all_to_all.22 = f32[32,1,128]{2,1,0:T(1,128)S(1)} all-to-all(f32[32,1,128]{2,1,0:T(1,128)S(1)} %bitcast.27), channel_id=1, replica_groups=mesh['line'=8,'seg'=4] {'line','seg'}, dimensions={0} | all-to-all | bytes 32768 | tf_op jit(solution)/shard_map/all_to_all | solution.py:445
  33.5 7.1 %match_second.1 = (f32[32,128]{1,0:T(8,128)S(1)}, f32[1,128]{1,0:T(1,128)S(1)}, f32[5,48,128]{2,1,0:T(8,128)}) custom-call(s32[2,24]{1,0:T(2,128)S(1)} %bitcast.29, f32[1,128]{1,0:T(1,128)S(1)} %pad.8.pose_ref, f32[32,128]{1,0:T(8,128)S(1)} %bitcast.25, f32[4,48,128]{2,1,0:T(8,128)S(1)} %copy-done, f32[200,128]{1,0:T(8,128)S(1)} %collective-permute-done.margin_a, ...), custom_call_target="tpu_custom_call" | custom-call | flops 56623104 | bytes 1048576 | tf_op jit(solution)/shard_map/match_second/pallas_call | solution.py:484
  40.5 0.0 copy-start.1
  40.5 0.5 copy-done.1
  41.1 12.4 %all_to_all.23 = f32[32,1,128]{2,1,0:T(1,128)} all-to-all(f32[32,1,128]{2,1,0:T(1,128)S(1)} %bitcast.26), channel_id=1, replica_groups=mesh['line'=8,'seg'=4] {'line','seg'}, dimensions={0} | all-to-all | bytes 32768 | tf_op jit(solution)/shard_map/all_to_all | solution.py:445
  53.5 1.4 %solve_last.1 = (f32[1,12]{1,0:T(1,128)}, f32[1,1]{1,0:T(1,128)}) custom-call(f32[1,128]{1,0:T(1,128)} %copy-done.1, f32[32,128]{1,0:T(8,128)} %bitcast.35), custom_call_target="tpu_custom_call" | custom-call | tf_op jit(solution)/shard_map/solve_last/pallas_call | solution.py:499
  (2 shorter events, 0.0 us)
Async XLA Ops:
  0.6 0.7 %copy-start.3 = (f32[12,1]{0,1:T(1,128)S(1)}, f32[12,1]{0,1:T(1,128)}, u32[]{:S(2)}) copy-start(f32[12,1]{0,1:T(1,128)} %param.7) | copy-start | bytes 148
  2.3 6.3 %collective-permute-start = (f32[200,128]{1,0:T(8,128)S(1)}, f32[200,128]{1,0:T(8,128)S(1)}, u32[]{:S(2)}, u32[]{:S(2)}) collective-permute-start(f32[200,128]{1,0:T(8,128)S(1)} %get-tuple-element.16), channel_id=1, source_target_pairs={{0,4},{4,0},{8,12},{12,8},{16,20},{20,16},{24,28},{28,24},{1,5},{5... | collective-permute-start | bytes 307208 | tf_op jit(solution)/shard_map/ppermute | solution.py:467
  2.8 5.8 %collective-permute-start.1 = (f32[200,128]{1,0:T(8,128)S(1)}, f32[200,128]{1,0:T(8,128)S(1)}, u32[]{:S(2)}, u32[]{:S(2)}) collective-permute-start(f32[200,128]{1,0:T(8,128)S(1)} %get-tuple-element.15), channel_id=1, source_target_pairs={{4,8},{8,4},{12,16},{16,12},{20,24},{24,20},{5,9},{9,5},{13,17},{1... | collective-permute-start | bytes 307208 | tf_op jit(solution)/shard_map/ppermute | solution.py:468
  8.6 0.7 %copy-start.2 = (s32[1,1,2,24]{3,2,1,0:T(2,128)S(1)}, s32[1,1,2,24]{3,2,1,0:T(2,128)}, u32[]{:S(2)}) copy-start(s32[1,1,2,24]{3,2,1,0:T(2,128)} %param.6) | copy-start | bytes 580
  9.2 0.9 %copy-start = (f32[4,48,128]{2,1,0:T(8,128)S(1)}, f32[4,48,128]{2,1,0:T(8,128)}, u32[]{:S(2)}) copy-start(f32[4,48,128]{2,1,0:T(8,128)} %gather_sources.1.source_ref) | copy-start | bytes 294916
  40.5 0.5 copy-start.1

commit v3 on v2

--- a/solution.py
+++ b/solution.py
@@ -15,8 +15,9 @@
 MROWS = MARGIN // 128
 TILES = CT // 128
 GROUPS = BLOCK // 8
-UNROLL = 8
+UNROLL = 48
 QUICK_LIMIT = 1000.0
+ENERGY_LIMIT = 400.0
 
 OUTLIER_MASS = 1.0
 SPREAD_START = 0.05
@@ -161,7 +162,7 @@
     return longest
 
 
-def quick_block(negc, exact, own, near, phi_ref, source_ref, side, row, cell):
+def weigh(negc, own, near, phi_ref, source_ref, side, row, cell):
     sub = iota(0)
     xt = [spread_out(source_ref[k, pl.ds(row, 1), :]) for k in range(4)]
     m = combine(own, xt) + (own[3] - near[side][3])
@@ -169,16 +170,24 @@
     coef = jnp.where(sub == 3, negc, jnp.where(sub == 4, negc * length, (-2.0 * negc) * m))
     high, middle, low = three_parts(coef)
     stack = jnp.concatenate([high, high, high, middle, middle, low], axis=0)
-    phi = phi_ref[side, :, pl.ds(pl.multiple_of(jnp.maximum(cell, 0) * CT, CT), CT)]
-    power = jnp.dot(jnp.transpose(stack).astype(BF16), phi, preferred_element_type=F32)
+    spot = pl.ds(pl.multiple_of(jnp.maximum(cell, 0) * CT, CT), CT)
+    power = jnp.dot(jnp.transpose(stack).astype(BF16), phi_ref[side, :, spot], preferred_element_type=F32)
     weight = jnp.exp2(power)
     top = weight.astype(BF16)
+    rest = (weight - top.astype(F32)).astype(BF16)
+    return xt, m, length, spot, top, rest
+
+
+def weighted_sums(phi_ref, side, spot, top, rest):
     last = (((1,), (1,)), ((), ()))
-    sums = lax.dot_general(phi[:32], top, last, preferred_element_type=F32)
-    if exact:
-        rest = (weight - top.astype(F32)).astype(BF16)
-        sums = sums + lax.dot_general(phi[:32], rest, last, preferred_element_type=F32)
-    sums = sums[0:8] + sums[8:16] + sums[16:24]
+    features = phi_ref[side, :32, spot]
+    sums = lax.dot_general(features, top, last, preferred_element_type=F32)
+    sums = sums + lax.dot_general(features, rest, last, preferred_element_type=F32)
+    return sums[0:8] + sums[8:16] + sums[16:24]
+
+
+def finish(near, side, xt, m, length, sums):
+    sub = iota(0)
     total = spread_out(sums[4:5, :])
     around = combine([spread_out(m[k : k + 1, :]) for k in range(3)], [spread_out(sums[k : k + 1, :]) for k in range(3)])
     energy = spread_out(sums[3:4, :]) - 2.0 * around + length * total
@@ -186,72 +195,68 @@
     return raw * (xt[3] / (total + OUTLIER_MASS)), xt
 
 
-def match(exact, own, nbrs, negc, dirs, cells_ref, source_ref, margin_refs, scratch_refs, out_ref):
+def quick_blocks(negc, own, near, phi_ref, source_ref, places):
+    ahead = weigh(negc, own, near, phi_ref, source_ref, *places[0])
+    found = []
+    for n, (side, _, _) in enumerate(places):
+        xt, m, length, spot, top, rest = ahead
+        if n + 1 < len(places):
+            ahead = weigh(negc, own, near, phi_ref, source_ref, *places[n + 1])
+        found.append(finish(near, side, xt, m, length, weighted_sums(phi_ref, side, spot, top, rest)))
+    return found
+
+
+def match(own, nbrs, negc, dirs, cells_ref, source_ref, margin_refs, scratch_refs, out_ref):
     phi_ref, sums_ref, world_ref, moved_ref, column_ref = scratch_refs
+    blocks = cells_ref.shape[1]
     own_cols, near_cols = columns(own), [columns(near) for near in nbrs]
     size = prepare(near_cols, margin_refs, phi_ref) + longest_source(own, nbrs, dirs, source_ref)
-    quick = jnp.max(size * -negc) <= QUICK_LIMIT
-    if out_ref is not None:
-        out_ref[...] = jnp.zeros(out_ref.shape, F32)
-
-    @pl.when(quick)
-    def _():
-        def block(side, row, cell):
-            return quick_block(negc, exact, own_cols, near_cols, phi_ref, source_ref, side, row, cell)
-
-        run_blocks(block, UNROLL, dirs, cells_ref, sums_ref, out_ref)
-
-    @pl.when(jnp.logical_not(quick))
-    def _():
-        block = careful_setup(own, nbrs, negc, source_ref, margin_refs, world_ref, moved_ref, column_ref)
-        run_blocks(block, 1, dirs, cells_ref, sums_ref, out_ref)
-
-    return [sums_ref[n] for n in range(5)]
-
-
-def run_blocks(one_block, unroll, dirs, cells_ref, sums_ref, out_ref):
-    sub = iota(0)
-    x_left = (sub < 3).astype(F32)
-    y_left = ((sub == 3) | (sub == 4)).astype(F32)
-    z_left = (sub == 5).astype(F32)
-    x_right = (sub == 0).astype(F32)
-    y_right = ((sub == 1) | (sub == 3)).astype(F32)
-    z_right = ((sub == 2) | (sub == 4) | (sub == 5)).astype(F32)
-
-    def add_block(carry, row, result, xt):
-        if out_ref is not None:
-            for q in range(5):
-                out_ref[q, pl.ds(row, 1), :] = result[q : q + 1, :]
-        factor = combine([x_left, y_left, z_left], xt) * combine([x_right, y_right, z_right], xt)
-        share = spread_out(result[3:4, :])
-        return (
-            carry[0] + result * xt[0],
-            carry[1] + result * xt[1],
-            carry[2] + result * xt[2],
-            carry[3] + result,
-            carry[4] + share * factor,
-        )
-
-    carry = tuple(jnp.zeros(TILE, F32) for _ in range(5))
-    blocks = cells_ref.shape[1]
-    for side in range(2):
-        d = dirs[side]
-
-        def filled(b, n, d=d):
-            return n + (cells_ref[d, b] >= 0).astype(jnp.int32)
-
-        live_blocks = lax.fori_loop(0, blocks, filled, jnp.int32(0))
-
-        def step(i, carry, side=side, d=d):
-            places = [i * unroll + u for u in range(unroll)]
-            found = [one_block(side, 2 * b + d, cells_ref[d, b]) for b in places]
-            for b, (result, xt) in zip(places, found):
-                carry = add_block(carry, 2 * b + d, result, xt)
-            return carry
-
-        carry = lax.fori_loop(0, (live_blocks + unroll - 1) // unroll, step, carry)
+    places = [(side, 2 * b + dirs[side], cells_ref[dirs[side], b]) for side in range(2) for b in range(blocks)]
+    carry = [jnp.zeros(TILE, F32) for _ in range(5)]
+    for first in range(0, len(places), UNROLL):
+        chosen = places[first : first + UNROLL]
+        found = quick_blocks(negc, own_cols, near_cols, phi_ref, source_ref, chosen)
+        for (_, row, _), (result, xt) in zip(chosen, found):
+            carry = add_block(carry, row, result, xt, out_ref)
     for n in range(5):
         sums_ref[n] = carry[n]
+    share, energy = [jnp.sum(carry[3][q : q + 1, :]) for q in (3, 4)]
+    longest = jnp.max(size)
+    bad = (jnp.max(size * -negc) > QUICK_LIMIT) | (longest * share > ENERGY_LIMIT * energy)
+
+    @pl.when(bad)
+    def _():
+        one_block = careful_setup(own, nbrs, negc, source_ref, margin_refs, world_ref, moved_ref, column_ref)
+        carry = tuple(jnp.zeros(TILE, F32) for _ in range(5))
+        for side in range(2):
+            d = dirs[side]
+
+            def step(b, carry, side=side, d=d):
+                result, xt = one_block(side, 2 * b + d, cells_ref[d, b])
+                return tuple(add_block(carry, 2 * b + d, result, xt, out_ref))
+
+            carry = lax.fori_loop(0, blocks, step, carry)
+        for n in range(5):
+            sums_ref[n] = carry[n]
+
+    return [sums_ref[n] for n in range(5)]
+
+
+def add_block(carry, row, result, xt, out_ref):
+    sub = iota(0)
+    if out_ref is not None:
+        for q in range(5):
+            out_ref[q, pl.ds(row, 1), :] = result[q : q + 1, :]
+    left = jnp.where(sub < 3, xt[0], jnp.where(sub < 5, xt[1], xt[2]))
+    right = jnp.where(sub == 0, xt[0], jnp.where((sub == 1) | (sub == 3), xt[1], xt[2]))
+    share = spread_out(result[3:4, :])
+    return [
+        carry[0] + result * xt[0],
+        carry[1] + result * xt[1],
+        carry[2] + result * xt[2],
+        carry[3] + result,
+        carry[4] + share * (left * right),
+    ]
 
 
 def careful_setup(own, nbrs, negc, source_ref, margin_refs, world_ref, moved_ref, column_ref):
@@ -323,7 +328,7 @@
     nbrs = [pose_of_row(margin[3 * MROWS : 3 * MROWS + 1, :]) for margin in (margin_a, margin_b)]
     negc = jnp.full(TILE, -LOG2E / (2.0 * SPREAD_START), F32)
     sums = match(
-        False, own, nbrs, negc, sides_of(line), cells_ref, source_ref, (margin_a, margin_b), scratch_refs, None
+        own, nbrs, negc, sides_of(line), cells_ref, source_ref, (margin_a, margin_b), scratch_refs, None
     )
     pack_sums(sums, sums_ref)
 
@@ -410,7 +415,7 @@
     own, near_a, near_b = [[spread_out(value[n : n + 1, :]) for value in new] for n in range(3)]
     pose_out_ref[...] = pose_row(new, 0)[:1, :]
     sums = match(
-        True, own, [near_a, near_b], negc, dirs, cells_ref, source_ref, (margin_a, margin_b), scratch_refs, out_ref
+        own, [near_a, near_b], negc, dirs, cells_ref, source_ref, (margin_a, margin_b), scratch_refs, out_ref
     )
     pack_sums(sums, sums_ref)
 
@@ -439,6 +444,41 @@
         pltpu.VMEM((3, 128, 128), F32),
         pltpu.VMEM((3, 128, 128), F32),
     ]
+
+
+def pair_cost(cells):
+    pairs = cells.size * BLOCK * CT
+    return pl.CostEstimate(flops=400 * pairs, bytes_accessed=1 << 20, transcendentals=pairs)
+
+
+def first_call(cells, pose_line, source, margin_a, margin_b, devices):
+    return pl.pallas_call(
+        first_kernel,
+        in_specs=[SMEM] + vmem(4),
+        out_specs=vmem(1)[0],
+        out_shape=jax.ShapeDtypeStruct((devices, 128), F32),
+        scratch_shapes=scratch(),
+        compiler_params=PARAMS,
+        cost_estimate=pair_cost(cells),
+        name="match_first",
+    )(cells, pose_line, source, margin_a, margin_b)
+
+
+def second_call(cells, pose_line, everyone, source, margin_a, margin_b, lines, segs):
+    return pl.pallas_call(
+        functools.partial(second_kernel, lines, segs),
+        in_specs=[SMEM] + vmem(5),
+        out_specs=vmem(3),
+        out_shape=[
+            jax.ShapeDtypeStruct((lines * segs, 128), F32),
+            jax.ShapeDtypeStruct((1, 128), F32),
+            jax.ShapeDtypeStruct((5,) + source.shape[1:], F32),
+        ],
+        scratch_shapes=scratch(),
+        compiler_params=PARAMS,
+        cost_estimate=pair_cost(cells),
+        name="match_second",
+    )(cells, pose_line, everyone, source, margin_a, margin_b)
 
 
 def exchange(sums):
@@ -467,34 +507,9 @@
     margin_a = lax.ppermute(margin_at(jnp.where(odd == 1, 0, tail)), "line", pairs_a)
     margin_b = lax.ppermute(margin_at(jnp.where(odd == 1, tail, 0)), "line", pairs_b)
     source = gather(own_points, row_list)
-    sums_shape = jax.ShapeDtypeStruct((devices, 128), F32)
-    pair_ops = 2 * blocks * BLOCK * CT
-    cost = pl.CostEstimate(flops=18 * pair_ops, bytes_accessed=1 << 20, transcendentals=pair_ops)
-    sums = pl.pallas_call(
-        first_kernel,
-        in_specs=[SMEM] + vmem(4),
-        out_specs=vmem(1)[0],
-        out_shape=sums_shape,
-        scratch_shapes=scratch(),
-        compiler_params=PARAMS,
-        cost_estimate=cost,
-        name="match_first",
-    )(cell_ids, pose_line, source, margin_a, margin_b)
+    sums = first_call(cell_ids, pose_line, source, margin_a, margin_b, devices)
     everyone = exchange(sums)
-    sums, pose_line, result = pl.pallas_call(
-        functools.partial(second_kernel, lines, segs),
-        in_specs=[SMEM] + vmem(5),
-        out_specs=vmem(3),
-        out_shape=[
-            sums_shape,
-            jax.ShapeDtypeStruct((1, 128), F32),
-            jax.ShapeDtypeStruct((5, 2 * blocks, 128), F32),
-        ],
-        scratch_shapes=scratch(),
-        compiler_params=PARAMS,
-        cost_estimate=cost,
-        name="match_second",
-    )(cell_ids, pose_line, everyone, source, margin_a, margin_b)
+    sums, pose_line, result = second_call(cell_ids, pose_line, everyone, source, margin_a, margin_b, lines, segs)
     everyone = exchange(sums)
     fitted, spread = pl.pallas_call(
         functools.partial(last_kernel, segs),

time: 55.2 us -> 50.7 us (0.918)
  blocking collectives: 30.7 us -> 25.1 us
  Pallas kernels: 18.5 us -> 19.7 us
    all_to_all x2, blocking collectives: 30.7 us -> 25.1 us  [exchange(): return lax.all_to_all(sums, ('line', 'seg'), 0, 0)]
    pallas_call x2, Pallas kernels: 12.1 us -> 13.2 us  [the longest x1 6.9 us: second_call(): pl.pallas_call(functools.partial(second_kernel, lines, segs), in_specs=[S...]
  transfers between devices with their start and end apart: 2 -> 2, of which waited for: 0 -> 0; matrix products, arithmetic and copies ran while one was open for 0% -> 0% of each run, Pallas kernels for 9% -> 10%
where the time goes in v3:
time: 50.7 us; the launch traced here: 50.3 us
  blocking collectives  25.1 us (50%)
  Pallas kernels  19.7 us (39%)
  local copies, waits for them, and re-layouts  3.7 us (7%)
  starting transfers between devices  1.17 us (2%)
  between operations  0.68 us (1%)
    all_to_all x2, blocking collectives, exchange(): return lax.all_to_all(sums, ('line', 'seg'), 0, 0)  25.1 us
    pallas_call x1, Pallas kernels, second_call(): pl.pallas_call(functools.partial(second_kernel, lines, segs), in_specs=[S...  6.9 us
    pallas_call x1, Pallas kernels, first_call(): pl.pallas_call(first_kernel, in_specs=[SMEM] + vmem(4), out_specs=vmem(1)...  6.3 us
    pallas_call x1, Pallas kernels, gather(): pl.pallas_call(gather_kernel, grid=(1,), in_specs=[pl.BlockSpec((3, MROWS...  5.09 us
    unnamed x8, local copies, waits for them, and re-layouts  2.74 us
    pallas_call x1, Pallas kernels, on_device(): pl.pallas_call(functools.partial(last_kernel, segs), in_specs=vmem(2), ou...  1.39 us
  transfers between devices with their start and end apart: 2, of which 0 were waited for; matrix products, arithmetic and copies ran while one was open for 0% of the time, Pallas kernels for 10%

profile of v3, /device:TPU:0, one launch (start us, length us, event | category | flops | bytes accessed | tf_op | source)
XLA Modules:
  0.0 50.3 jit_solution(6630967247891928522)
XLA Ops:
  0.6 0.0 copy-start.3
  0.6 0.6 %copy-done.3 = f32[12,1]{0,1:T(1,128)S(1)} copy-done((f32[12,1]{0,1:T(1,128)S(1)}, f32[12,1]{0,1:T(1,128)}, u32[]{:S(2)}) %copy-start.3) | copy-done | bytes 72
  1.3 1.0 %constant_dynamic-slice_fusion = (f32[3,64,128]{2,1,0:T(8,128)S(1)}, f32[3,64,128]{2,1,0:T(8,128)S(1)}) fusion(f32[3,256,128]{2,1,0:T(8,128)} %bitcast.30, s32[]{:T(128)S(6)} %select_n.10, s32[]{:T(128)S(6)} %select_n.9), kind=kLoop, calls=%fused_computation.4 | loop fusion | bytes 393224 | tf_op jit(solution)/shard_map/dynamic_slice | solution.py:501
  2.3 0.5 %collective-permute-start = (f32[200,128]{1,0:T(8,128)S(1)}, f32[200,128]{1,0:T(8,128)S(1)}, u32[]{:S(2)}, u32[]{:S(2)}) collective-permute-start(f32[200,128]{1,0:T(8,128)S(1)} %get-tuple-element.16), channel_id=1, source_target_pairs={{0,4},{4,0},{8,12},{12,8},{16,20},{20,16},{24,28},{28,24},{1,5},{5... | collective-permute-start | bytes 307208 | tf_op jit(solution)/shard_map/ppermute | solution.py:507
  2.8 0.7 %collective-permute-start.1 = (f32[200,128]{1,0:T(8,128)S(1)}, f32[200,128]{1,0:T(8,128)S(1)}, u32[]{:S(2)}, u32[]{:S(2)}) collective-permute-start(f32[200,128]{1,0:T(8,128)S(1)} %get-tuple-element.15), channel_id=1, source_target_pairs={{4,8},{8,4},{12,16},{16,12},{20,24},{24,20},{5,9},{9,5},{13,17},{1... | collective-permute-start | bytes 307208 | tf_op jit(solution)/shard_map/ppermute | solution.py:508
  3.5 5.1 %gather_sources.1.source_ref = f32[4,48,128]{2,1,0:T(8,128)} custom-call(f32[3,256,128]{2,1,0:T(8,128)} %bitcast.31, f32[3,256,128]{2,1,0:T(8,128)} %bitcast.32, s32[48,128]{1,0:T(8,128)} %bitcast.36), custom_call_target="tpu_custom_call" | custom-call | tf_op jit(solution)/shard_map/gather_sources/pallas_call | solution.py:82
  8.6 0.0 copy-start.2
  8.6 0.0 collective-permute-done.margin_a
  8.6 0.0 collective-permute-done.1.margin_b
  8.6 0.7 %copy-done.2 = s32[1,1,2,24]{3,2,1,0:T(2,128)S(1)} copy-done((s32[1,1,2,24]{3,2,1,0:T(2,128)S(1)}, s32[1,1,2,24]{3,2,1,0:T(2,128)}, u32[]{:S(2)}) %copy-start.2) | copy-done | bytes 216
  9.2 0.0 copy-start
  9.2 0.9 %copy-done = f32[4,48,128]{2,1,0:T(8,128)S(1)} copy-done((f32[4,48,128]{2,1,0:T(8,128)S(1)}, f32[4,48,128]{2,1,0:T(8,128)}, u32[]{:S(2)}) %copy-start) | copy-done | bytes 98328
  10.1 6.3 %match_first.1 = f32[32,128]{1,0:T(8,128)S(1)} custom-call(s32[2,24]{1,0:T(2,128)S(1)} %bitcast.28, f32[1,128]{1,0:T(1,128)S(1)} %pad.8.pose_ref, f32[4,48,128]{2,1,0:T(8,128)S(1)} %copy-done, f32[200,128]{1,0:T(8,128)S(1)} %collective-permute-done.margin_a, f32[200,128]{1,0:T(8,128)S(1)} %collective-permute-done.1.margin_b), custom_call_target="tpu_custom_call" | custom-call | flops 1258291200 | bytes 1048576 | tf_op jit(solution)/shard_map/match_first/pallas_call | solution.py:455
  16.4 15.7 %all_to_all.22 = f32[32,1,128]{2,1,0:T(1,128)S(1)} all-to-all(f32[32,1,128]{2,1,0:T(1,128)S(1)} %bitcast.27), channel_id=1, replica_groups=mesh['line'=8,'seg'=4] {'line','seg'}, dimensions={0} | all-to-all | bytes 32768 | tf_op jit(solution)/shard_map/all_to_all | solution.py:485
  32.1 6.9 %match_second.1 = (f32[32,128]{1,0:T(8,128)S(1)}, f32[1,128]{1,0:T(1,128)S(1)}, f32[5,48,128]{2,1,0:T(8,128)}) custom-call(s32[2,24]{1,0:T(2,128)S(1)} %bitcast.29, f32[1,128]{1,0:T(1,128)S(1)} %pad.8.pose_ref, f32[32,128]{1,0:T(8,128)S(1)} %bitcast.25, f32[4,48,128]{2,1,0:T(8,128)S(1)} %copy-done, f32[200,128]{1,0:T(8,128)S(1)} %collective-permute-done.margin_a, ...), custom_call_target="tpu_custom_call" | custom-call | flops 1258291200 | bytes 1048576 | tf_op jit(solution)/shard_map/match_second/pallas_call | solution.py:468
  39.0 0.0 copy-start.1
  39.0 0.5 %copy-done.1 = f32[1,128]{1,0:T(1,128)} copy-done((f32[1,128]{1,0:T(1,128)}, f32[1,128]{1,0:T(1,128)S(1)}, u32[]{:S(2)}) %copy-start.1) | copy-done | bytes 536
  39.6 9.4 %all_to_all.23 = f32[32,1,128]{2,1,0:T(1,128)} all-to-all(f32[32,1,128]{2,1,0:T(1,128)S(1)} %bitcast.26), channel_id=1, replica_groups=mesh['line'=8,'seg'=4] {'line','seg'}, dimensions={0} | all-to-all | bytes 32768 | tf_op jit(solution)/shard_map/all_to_all | solution.py:485
  48.9 1.4 %solve_last.1 = (f32[1,12]{1,0:T(1,128)}, f32[1,1]{1,0:T(1,128)}) custom-call(f32[1,128]{1,0:T(1,128)} %copy-done.1, f32[32,128]{1,0:T(8,128)} %bitcast.35), custom_call_target="tpu_custom_call" | custom-call | tf_op jit(solution)/shard_map/solve_last/pallas_call | solution.py:514
  (2 shorter events, 0.0 us)
Async XLA Ops:
  0.6 0.7 %copy-start.3 = (f32[12,1]{0,1:T(1,128)S(1)}, f32[12,1]{0,1:T(1,128)}, u32[]{:S(2)}) copy-start(f32[12,1]{0,1:T(1,128)} %param.7) | copy-start | bytes 148
  2.3 6.3 %collective-permute-start = (f32[200,128]{1,0:T(8,128)S(1)}, f32[200,128]{1,0:T(8,128)S(1)}, u32[]{:S(2)}, u32[]{:S(2)}) collective-permute-start(f32[200,128]{1,0:T(8,128)S(1)} %get-tuple-element.16), channel_id=1, source_target_pairs={{0,4},{4,0},{8,12},{12,8},{16,20},{20,16},{24,28},{28,24},{1,5},{5... | collective-permute-start | bytes 307208 | tf_op jit(solution)/shard_map/ppermute | solution.py:507
  2.8 5.8 %collective-permute-start.1 = (f32[200,128]{1,0:T(8,128)S(1)}, f32[200,128]{1,0:T(8,128)S(1)}, u32[]{:S(2)}, u32[]{:S(2)}) collective-permute-start(f32[200,128]{1,0:T(8,128)S(1)} %get-tuple-element.15), channel_id=1, source_target_pairs={{4,8},{8,4},{12,16},{16,12},{20,24},{24,20},{5,9},{9,5},{13,17},{1... | collective-permute-start | bytes 307208 | tf_op jit(solution)/shard_map/ppermute | solution.py:508
  8.6 0.7 %copy-start.2 = (s32[1,1,2,24]{3,2,1,0:T(2,128)S(1)}, s32[1,1,2,24]{3,2,1,0:T(2,128)}, u32[]{:S(2)}) copy-start(s32[1,1,2,24]{3,2,1,0:T(2,128)} %param.6) | copy-start | bytes 580
  9.2 0.9 %copy-start = (f32[4,48,128]{2,1,0:T(8,128)S(1)}, f32[4,48,128]{2,1,0:T(8,128)}, u32[]{:S(2)}) copy-start(f32[4,48,128]{2,1,0:T(8,128)} %gather_sources.1.source_ref) | copy-start | bytes 294916
  39.0 0.5 %copy-start.1 = (f32[1,128]{1,0:T(1,128)}, f32[1,128]{1,0:T(1,128)S(1)}, u32[]{:S(2)}) copy-start(f32[1,128]{1,0:T(1,128)S(1)} %get-tuple-element.9.pose_ref) | copy-start | bytes 1540

commit v4 on v3

--- a/solution.py
+++ b/solution.py
@@ -15,7 +15,7 @@
 MROWS = MARGIN // 128
 TILES = CT // 128
 GROUPS = BLOCK // 8
-UNROLL = 48
+WIDE = 4
 QUICK_LIMIT = 1000.0
 ENERGY_LIMIT = 400.0
 
@@ -33,6 +33,7 @@
 SHARE = ONE + 3
 ENERGY = ONE + 4
 QUAD = 32
+POSE = 64
 
 
 def iota(axis):
@@ -43,54 +44,62 @@
     return jnp.broadcast_to(value, TILE)
 
 
-def gather_kernel(low_ref, up_ref, rows_ref, source_ref):
+def gather_kernel(points_ref, rows_ref, source_ref, table_ref, turned_ref, sems):
     slot_rows = rows_ref.shape[0]
-    count = slot_rows // 8
-    upward = (iota(0) & 1) == 1
-    high, low, live = [], [], []
-    for v in range(count):
-        row = rows_ref[8 * v : 8 * v + 8, :]
-        live.append((row >= 0).astype(F32))
-        spot = jnp.maximum(row, 0) & (MARGIN - 1)
-        high.append(spot >> 7)
-        low.append(spot & 127)
-
-    def step(r, carry):
-        table = []
+    blocks = slot_rows // 2
+    starts = [0, points_ref.shape[1] - MROWS]
+    copies = [
+        pltpu.make_async_copy(points_ref.at[:, pl.ds(starts[d], MROWS), :], table_ref.at[d], sems.at[d]) for d in range(2)
+    ]
+    for copy in copies:
+        copy.start()
+    for v in range(slot_rows // 8):
+        source_ref[3, 8 * v : 8 * v + 8, :] = (rows_ref[8 * v : 8 * v + 8, :] >= 0).astype(F32)
+    group = MROWS // 8
+    for d in range(2):
+        copies[d].wait()
         for k in range(3):
-            a = spread_out(low_ref[k, pl.ds(r, 1), :])
-            b = spread_out(up_ref[k, pl.ds(r, 1), :])
-            table.append(jnp.where(upward, b, a))
-        out = []
-        for v in range(count):
-            hit = high[v] == r
-            for k in range(3):
-                got = jnp.take_along_axis(table[k], low[v], axis=1, mode="promise_in_bounds")
-                out.append(jnp.where(hit, got, carry[3 * v + k]))
-        return tuple(out)
-
-    done = lax.fori_loop(0, MROWS, step, tuple(jnp.zeros(TILE, F32) for _ in range(3 * count)), unroll=4)
-    for v in range(count):
-        for k in range(3):
-            source_ref[k, 8 * v : 8 * v + 8, :] = done[3 * v + k]
-        source_ref[3, 8 * v : 8 * v + 8, :] = live[v]
+            parts = [three_parts(table_ref[d, k, 8 * v : 8 * v + 8, :]) for v in range(group)]
+            stack = jnp.concatenate([parts[v][p] for p in range(3) for v in range(group)], axis=0)
+            turned_ref[d, 128 * k : 128 * k + 128, :] = jnp.transpose(stack).astype(BF16)
+        for first in range(0, blocks, WIDE):
+            chosen = range(first, min(first + WIDE, blocks))
+            spots = [jnp.maximum(rows_ref[2 * b + d : 2 * b + d + 1, :], 0) & (MARGIN - 1) for b in chosen]
+            hits = []
+            for spot in spots:
+                high = spread_out(spot >> 7)
+                hits.append(
+                    jnp.concatenate([(high == iota(0) + 8 * v).astype(F32) for v in range(group)], axis=0).astype(BF16)
+                )
+            hit = jnp.concatenate(hits, axis=1)
+            picked = jnp.dot(turned_ref[d], jnp.concatenate([hit] * 3, axis=0), preferred_element_type=F32)
+            for n, b in enumerate(chosen):
+                low = spread_out(spots[n] & 127)
+                sums = [jnp.zeros(TILE, F32)] * 3
+                for v in range(16):
+                    here = low == iota(0) + 8 * v
+                    for k in range(3):
+                        part = picked[128 * k + 8 * v : 128 * k + 8 * v + 8, 128 * n : 128 * n + 128]
+                        sums[k] = jnp.where(here, part, sums[k])
+                for k in range(3):
+                    source_ref[k, 2 * b + d : 2 * b + d + 1, :] = jnp.sum(sums[k], axis=0, keepdims=True)
 
 
 def gather(points, rows):
-    last = points.shape[1] // MROWS - 1
     slot_rows = rows.shape[0]
     return pl.pallas_call(
         gather_kernel,
-        grid=(1,),
-        in_specs=[
-            pl.BlockSpec((3, MROWS, 128), lambda i: (0, 0, 0)),
-            pl.BlockSpec((3, MROWS, 128), lambda i: (0, last, 0)),
-            pl.BlockSpec((slot_rows, 128), lambda i: (0, 0)),
+        in_specs=[pl.BlockSpec(memory_space=pl.ANY)] + vmem(1),
+        out_specs=vmem(1)[0],
+        out_shape=jax.ShapeDtypeStruct((4, slot_rows, 128), F32),
+        scratch_shapes=[
+            pltpu.VMEM((2, 3, MROWS, 128), F32),
+            pltpu.VMEM((2, 3 * 128, 3 * MROWS), BF16),
+            pltpu.SemaphoreType.DMA((2,)),
         ],
-        out_specs=pl.BlockSpec((4, slot_rows, 128), lambda i: (0, 0, 0)),
-        out_shape=jax.ShapeDtypeStruct((4, slot_rows, 128), F32),
+        compiler_params=PARAMS,
         name="gather_sources",
-    )(points, points, rows)
+    )(points, rows)
 
 
 def apply_pose(coefs, xyz):
@@ -131,22 +140,14 @@
     return cols[0] * xyz[0] + cols[1] * xyz[1] + cols[2] * xyz[2]
 
 
-def prepare(near, margin_refs, phi_ref):
+def prepare(near, margin_ref, phi_ref, r):
     sub = iota(0)
-
-    def step(r, longest):
-        for side in range(2):
-            xyz = [spread_out(margin_refs[side][pl.ds(k * MROWS + r, 1), :]) for k in range(3)]
-            y = combine(near[side], xyz)
-            length = squared_length(y)
-            longest = jnp.maximum(longest, length)
-            high, middle, low = three_parts(jnp.where(sub == 3, length, jnp.where(sub == 4, 1.0, y)))
-            spot = pl.ds(pl.multiple_of(r * 128, 128), 128)
-            for i, pair in enumerate(((high, middle), (low, high), (middle, high))):
-                phi_ref[side, 16 * i : 16 * i + 16, spot] = jnp.concatenate(pair, axis=0).astype(BF16)
-        return longest
-
-    return lax.fori_loop(0, MROWS, step, jnp.zeros(TILE, F32), unroll=4)
+    y = combine(near, [spread_out(margin_ref[k * MROWS + r : k * MROWS + r + 1, :]) for k in range(3)])
+    length = squared_length(y)
+    high, middle, low = three_parts(jnp.where(sub == 3, length, jnp.where(sub == 4, 1.0, y)))
+    for i, pair in enumerate(((high, middle), (low, high), (middle, high))):
+        phi_ref[16 * i : 16 * i + 16, 128 * r : 128 * r + 128] = jnp.concatenate(pair, axis=0).astype(BF16)
+    return length
 
 
 def longest_source(own, near, dirs, source_ref):
@@ -162,7 +163,7 @@
     return longest
 
 
-def weigh(negc, own, near, phi_ref, source_ref, side, row, cell):
+def weigh(negc, own, near, phi_refs, source_ref, side, row, cell):
     sub = iota(0)
     xt = [spread_out(source_ref[k, pl.ds(row, 1), :]) for k in range(4)]
     m = combine(own, xt) + (own[3] - near[side][3])
@@ -171,16 +172,16 @@
     high, middle, low = three_parts(coef)
     stack = jnp.concatenate([high, high, high, middle, middle, low], axis=0)
     spot = pl.ds(pl.multiple_of(jnp.maximum(cell, 0) * CT, CT), CT)
-    power = jnp.dot(jnp.transpose(stack).astype(BF16), phi_ref[side, :, spot], preferred_element_type=F32)
+    power = jnp.dot(jnp.transpose(stack).astype(BF16), phi_refs[side][:, spot], preferred_element_type=F32)
     weight = jnp.exp2(power)
     top = weight.astype(BF16)
     rest = (weight - top.astype(F32)).astype(BF16)
     return xt, m, length, spot, top, rest
 
 
-def weighted_sums(phi_ref, side, spot, top, rest):
+def weighted_sums(phi_refs, side, spot, top, rest):
     last = (((1,), (1,)), ((), ()))
-    features = phi_ref[side, :32, spot]
+    features = phi_refs[side][:32, spot]
     sums = lax.dot_general(features, top, last, preferred_element_type=F32)
     sums = sums + lax.dot_general(features, rest, last, preferred_element_type=F32)
     return sums[0:8] + sums[8:16] + sums[16:24]
@@ -195,37 +196,49 @@
     return raw * (xt[3] / (total + OUTLIER_MASS)), xt
 
 
-def quick_blocks(negc, own, near, phi_ref, source_ref, places):
-    ahead = weigh(negc, own, near, phi_ref, source_ref, *places[0])
+def match(own, nbrs, negc, dirs, cells_hbm, source_ref, margin_refs, scratch_refs, sums_ref, pose_row, out):
+    phi_refs, (cells_ref, cells_sem, world_ref, moved_ref, column_ref) = scratch_refs[:2], scratch_refs[2:7]
+    blocks = cells_ref.shape[1]
+    fetch = pltpu.make_async_copy(cells_hbm, cells_ref, cells_sem)
+    fetch.start()
+    out_ref = None if out is None else out[1]
+    own_cols, near_cols = columns(own), [columns(near) for near in nbrs]
+    longest = jnp.zeros(TILE, F32)
+    for r in range(MROWS):
+        longest = jnp.maximum(longest, prepare(near_cols[0], margin_refs[0], phi_refs[0], r))
+    fetch.wait()
+    places = [(side, 2 * b + dirs[side], cells_ref[dirs[side], b]) for side in range(2) for b in range(blocks)]
+    later = list(range(MROWS))
+    each = -(-MROWS // max(1, blocks - 2))
+    carry = [jnp.zeros(TILE, F32) for _ in range(5)]
     found = []
-    for n, (side, _, _) in enumerate(places):
-        xt, m, length, spot, top, rest = ahead
+    ahead = None
+    for n in range(-1, len(places)):
+        block, ahead = ahead, None
         if n + 1 < len(places):
-            ahead = weigh(negc, own, near, phi_ref, source_ref, *places[n + 1])
-        found.append(finish(near, side, xt, m, length, weighted_sums(phi_ref, side, spot, top, rest)))
-    return found
-
-
-def match(own, nbrs, negc, dirs, cells_ref, source_ref, margin_refs, scratch_refs, out_ref):
-    phi_ref, sums_ref, world_ref, moved_ref, column_ref = scratch_refs
-    blocks = cells_ref.shape[1]
-    own_cols, near_cols = columns(own), [columns(near) for near in nbrs]
-    size = prepare(near_cols, margin_refs, phi_ref) + longest_source(own, nbrs, dirs, source_ref)
-    places = [(side, 2 * b + dirs[side], cells_ref[dirs[side], b]) for side in range(2) for b in range(blocks)]
-    carry = [jnp.zeros(TILE, F32) for _ in range(5)]
-    for first in range(0, len(places), UNROLL):
-        chosen = places[first : first + UNROLL]
-        found = quick_blocks(negc, own_cols, near_cols, phi_ref, source_ref, chosen)
-        for (_, row, _), (result, xt) in zip(chosen, found):
-            carry = add_block(carry, row, result, xt, out_ref)
-    for n in range(5):
-        sums_ref[n] = carry[n]
-    share, energy = [jnp.sum(carry[3][q : q + 1, :]) for q in (3, 4)]
-    longest = jnp.max(size)
-    bad = (jnp.max(size * -negc) > QUICK_LIMIT) | (longest * share > ENERGY_LIMIT * energy)
-
-    @pl.when(bad)
+            ahead = weigh(negc, own_cols, near_cols, phi_refs, source_ref, *places[n + 1])
+        for r in later[:each]:
+            longest = jnp.maximum(longest, prepare(near_cols[1], margin_refs[1], phi_refs[1], r))
+        later = later[each:]
+        if block is not None:
+            side, row, _ = places[n]
+            xt, m, length, spot, top, rest = block
+            found.append((row, *finish(near_cols, side, xt, m, length, weighted_sums(phi_refs, side, spot, top, rest))))
+    for row, result, xt in found:
+        carry = add_block(carry, row, result, xt, out_ref)
+    if out is not None:
+        save = pltpu.make_async_copy(out[1], out[0], out[2])
+        save.start()
+    pack_sums(carry, pose_row, sums_ref)
+    size = spread_out(jnp.max(longest)) + spread_out(jnp.max(longest_source(own, nbrs, dirs, source_ref)))
+    whole = jnp.sum(carry[3], axis=1, keepdims=True)
+    share, energy = [spread_out(whole[q : q + 1, :]) for q in (3, 4)]
+    bad = (size * -negc > QUICK_LIMIT) | (size * share > ENERGY_LIMIT * energy)
+
+    @pl.when(jnp.max(bad.astype(F32)) > 0.0)
     def _():
+        if out is not None:
+            save.wait()
         one_block = careful_setup(own, nbrs, negc, source_ref, margin_refs, world_ref, moved_ref, column_ref)
         carry = tuple(jnp.zeros(TILE, F32) for _ in range(5))
         for side in range(2):
@@ -236,10 +249,12 @@
                 return tuple(add_block(carry, 2 * b + d, result, xt, out_ref))
 
             carry = lax.fori_loop(0, blocks, step, carry)
-        for n in range(5):
-            sums_ref[n] = carry[n]
-
-    return [sums_ref[n] for n in range(5)]
+        pack_sums(carry, pose_row, sums_ref)
+        if out is not None:
+            save.start()
+
+    if out is not None:
+        save.wait()
 
 
 def add_block(carry, row, result, xt, out_ref):
@@ -304,13 +319,13 @@
     return one_block
 
 
-def pack_sums(sums, out_ref):
+def pack_sums(sums, pose_row, out_ref):
     lane, sub = iota(1), iota(0)
     total = jnp.zeros(TILE, F32)
     for c in range(5):
         total = total + jnp.where(lane == 8 * c + sub, jnp.sum(sums[c], axis=1, keepdims=True), 0.0)
     row = jnp.sum(total, axis=0, keepdims=True)
-    out_ref[...] = jnp.broadcast_to(row, out_ref.shape)
+    out_ref[...] = jnp.broadcast_to(row + pose_row, out_ref.shape)
 
 
 def pose_of_row(row):
@@ -322,15 +337,13 @@
     return [1 - odd, odd]
 
 
-def first_kernel(cells_ref, pose_ref, source_ref, margin_a, margin_b, sums_ref, *scratch_refs):
+def first_kernel(cells_hbm, pose_ref, source_ref, margin_a, margin_b, sums_ref, *scratch_refs):
     line = lax.axis_index("line")
     own = pose_of_row(pose_ref[...])
     nbrs = [pose_of_row(margin[3 * MROWS : 3 * MROWS + 1, :]) for margin in (margin_a, margin_b)]
     negc = jnp.full(TILE, -LOG2E / (2.0 * SPREAD_START), F32)
-    sums = match(
-        own, nbrs, negc, sides_of(line), cells_ref, source_ref, (margin_a, margin_b), scratch_refs, None
-    )
-    pack_sums(sums, sums_ref)
+    margins = (margin_a, margin_b)
+    match(own, nbrs, negc, sides_of(line), cells_hbm, source_ref, margins, scratch_refs, sums_ref, 0.0, None)
 
 
 def solve(totals, old):
@@ -388,17 +401,17 @@
     return top / (3.0 * spread_out(everything[:, SHARE : SHARE + 1]) + PRIOR_BOTTOM)
 
 
-def pose_row(new, sub):
-    lane = iota(1)
-    row = jnp.zeros(TILE, F32)
+def pose_row(new, first):
+    lane = lax.broadcasted_iota(jnp.int32, (1, 128), 1)
+    row = jnp.zeros((1, 128), F32)
     for j in range(12):
-        row = jnp.where(lane == j, spread_out(new[j][sub : sub + 1, :]), row)
+        row = jnp.where(lane == first + j, new[j][:1, :], row)
     return row
 
 
 def second_kernel(
-    lines, segs, cells_ref, pose_ref, all_ref, source_ref, margin_a, margin_b,
-    sums_ref, pose_out_ref, out_ref, *scratch_refs,
+    lines, segs, cells_hbm, pose_ref, all_ref, source_ref, margin_a, margin_b,
+    sums_ref, out_hbm, *scratch_refs,
 ):
     line = lax.axis_index("line")
     dirs = sides_of(line)
@@ -413,18 +426,20 @@
     new = solve(totals, old)
     negc = (-0.5 * LOG2E) / new_spread(all_ref)
     own, near_a, near_b = [[spread_out(value[n : n + 1, :]) for value in new] for n in range(3)]
-    pose_out_ref[...] = pose_row(new, 0)[:1, :]
-    sums = match(
-        own, [near_a, near_b], negc, dirs, cells_ref, source_ref, (margin_a, margin_b), scratch_refs, out_ref
+    margins = (margin_a, margin_b)
+    out_ref, out_sem = scratch_refs[7:9]
+    match(
+        own, [near_a, near_b], negc, dirs, cells_hbm, source_ref, margins, scratch_refs, sums_ref,
+        pose_row(new, POSE), (out_hbm, out_ref, out_sem),
     )
-    pack_sums(sums, sums_ref)
-
-
-def last_kernel(segs, pose_ref, all_ref, fitted_ref, spread_ref):
+
+
+def last_kernel(segs, all_ref, fitted_ref, spread_ref):
     line = lax.axis_index("line")
     totals = spread_out(line_sum(all_ref, line, segs))
-    new = solve(totals, spread_out(pose_ref[...]))
-    fitted_ref[...] = pose_row(new, 0)[:1, :12]
+    old = all_ref[pl.ds(line * segs, 1), :][:, POSE : POSE + 12]
+    new = solve(totals, jnp.broadcast_to(old, (8, 12)))
+    fitted_ref[...] = pose_row(new, 0)[:, :12]
     spread_ref[...] = new_spread(all_ref)[:1, :1]
 
 
@@ -432,14 +447,16 @@
     return [pl.BlockSpec(memory_space=pltpu.VMEM)] * count
 
 
-SMEM = pl.BlockSpec(memory_space=pltpu.SMEM)
+ANY = pl.BlockSpec(memory_space=pl.ANY)
 PARAMS = pltpu.CompilerParams(vmem_limit_bytes=32 * 1024 * 1024)
 
 
-def scratch():
+def scratch(cells):
     return [
-        pltpu.VMEM((2, 48, MARGIN), BF16),
-        pltpu.VMEM((5, 8, 128), F32),
+        pltpu.VMEM((48, MARGIN), BF16),
+        pltpu.VMEM((48, MARGIN), BF16),
+        pltpu.SMEM(cells.shape, jnp.int32),
+        pltpu.SemaphoreType.DMA,
         pltpu.VMEM((2, 3, MROWS, 128), F32),
         pltpu.VMEM((3, 128, 128), F32),
         pltpu.VMEM((3, 128, 128), F32),
@@ -454,10 +471,10 @@
 def first_call(cells, pose_line, source, margin_a, margin_b, devices):
     return pl.pallas_call(
         first_kernel,
-        in_specs=[SMEM] + vmem(4),
+        in_specs=[ANY] + vmem(4),
         out_specs=vmem(1)[0],
         out_shape=jax.ShapeDtypeStruct((devices, 128), F32),
-        scratch_shapes=scratch(),
+        scratch_shapes=scratch(cells),
         compiler_params=PARAMS,
         cost_estimate=pair_cost(cells),
         name="match_first",
@@ -465,16 +482,13 @@
 
 
 def second_call(cells, pose_line, everyone, source, margin_a, margin_b, lines, segs):
+    result = (5,) + source.shape[1:]
     return pl.pallas_call(
         functools.partial(second_kernel, lines, segs),
-        in_specs=[SMEM] + vmem(5),
-        out_specs=vmem(3),
-        out_shape=[
-            jax.ShapeDtypeStruct((lines * segs, 128), F32),
-            jax.ShapeDtypeStruct((1, 128), F32),
-            jax.ShapeDtypeStruct((5,) + source.shape[1:], F32),
-        ],
-        scratch_shapes=scratch(),
+        in_specs=[ANY] + vmem(5),
+        out_specs=vmem(1) + [ANY],
+        out_shape=[jax.ShapeDtypeStruct((lines * segs, 128), F32), jax.ShapeDtypeStruct(result, F32)],
+        scratch_shapes=scratch(cells) + [pltpu.VMEM(result, F32), pltpu.SemaphoreType.DMA],
         compiler_params=PARAMS,
         cost_estimate=pair_cost(cells),
         name="match_second",
@@ -509,15 +523,16 @@
     source = gather(own_points, row_list)
     sums = first_call(cell_ids, pose_line, source, margin_a, margin_b, devices)
     everyone = exchange(sums)
-    sums, pose_line, result = second_call(cell_ids, pose_line, everyone, source, margin_a, margin_b, lines, segs)
+    sums, result = second_call(cell_ids, pose_line, everyone, source, margin_a, margin_b, lines, segs)
     everyone = exchange(sums)
     fitted, spread = pl.pallas_call(
         functools.partial(last_kernel, segs),
-        in_specs=vmem(2),
+        in_specs=vmem(1),
         out_specs=vmem(2),
         out_shape=[jax.ShapeDtypeStruct((1, 12), F32), jax.ShapeDtypeStruct((1, 1), F32)],
+        compiler_params=PARAMS,
         name="solve_last",
-    )(pose_line, everyone)
+    )(everyone)
     result = result.reshape(5, blocks, 2, 128).transpose(2, 0, 1, 3).reshape(1, 1, 2, 5, slots)
     return (result, fitted.reshape(12, 1), spread.reshape(1))
 

time: 50.7 us -> 45 us (0.89)
  Pallas kernels: 19.7 us -> 14.4 us
  local copies, waits for them, and re-layouts: 3.7 us -> 2.32 us
  blocking collectives: 25.1 us -> 26.1 us
    pallas_call x4, Pallas kernels: 19.7 us -> 14.4 us  [the longest x1 6.15 us: second_call(): pl.pallas_call(functools.partial(second_kernel, lines, segs), in_specs=[A...]
    unnamed x8, local copies, waits for them, and re-layouts: 2.74 us -> 1.31 us
    all_to_all x2, blocking collectives: 25.1 us -> 26.1 us  [exchange(): return lax.all_to_all(sums, ('line', 'seg'), 0, 0)]
  transfers between devices with their start and end apart: 2 -> 2, of which waited for: 0 -> 0; matrix products, arithmetic and copies ran while one was open for 0% -> 0% of each run, Pallas kernels for 10% -> 4%
where the time goes in v4:
time: 45 us; the launch traced here: 44.8 us
  blocking collectives  26.1 us (58%)
  Pallas kernels  14.4 us (32%)
  local copies, waits for them, and re-layouts  2.32 us (5%)
  starting transfers between devices  1.17 us (3%)
  between operations  0.74 us (2%)
    all_to_all x2, blocking collectives, exchange(): return lax.all_to_all(sums, ('line', 'seg'), 0, 0)  26.1 us
    pallas_call x1, Pallas kernels, second_call(): pl.pallas_call(functools.partial(second_kernel, lines, segs), in_specs=[A...  6.15 us
    pallas_call x1, Pallas kernels, first_call(): pl.pallas_call(first_kernel, in_specs=[ANY] + vmem(4), out_specs=vmem(1)[...  5.62 us
    pallas_call x1, Pallas kernels, gather(): pl.pallas_call(gather_kernel, in_specs=[pl.BlockSpec(memory_space=pl.ANY)...  1.96 us
    unnamed x8, local copies, waits for them, and re-layouts  1.31 us
    dynamic_slice x1, local copies, waits for them, and re-layouts, margin_at(): part = lax.dynamic_slice_in_dim(own_points, first, MROWS, 1)  1.01 us
  transfers between devices with their start and end apart: 2, of which 0 were waited for; matrix products, arithmetic and copies ran while one was open for 0% of the time, Pallas kernels for 4%

profile of v4, /device:TPU:0, one launch (start us, length us, event | category | flops | bytes accessed | tf_op | source)
XLA Modules:
  0.0 44.8 jit_solution(9145657191648132303)
XLA Ops:
  0.6 0.0 copy-start.3
  0.6 0.6 %copy-done.3 = f32[12,1]{0,1:T(1,128)S(1)} copy-done((f32[12,1]{0,1:T(1,128)S(1)}, f32[12,1]{0,1:T(1,128)}, u32[]{:S(2)}) %copy-start.3) | copy-done | bytes 72
  1.3 0.0 copy-start
  1.3 1.0 %constant_dynamic-slice_fusion = (f32[3,64,128]{2,1,0:T(8,128)S(1)}, f32[3,64,128]{2,1,0:T(8,128)S(1)}) fusion(f32[3,256,128]{2,1,0:T(8,128)} %bitcast.25, s32[]{:T(128)S(6)} %select_n.10, s32[]{:T(128)S(6)} %select_n.9), kind=kLoop, calls=%fused_computation.4 | loop fusion | bytes 393224 | tf_op jit(solution)/shard_map/dynamic_slice | solution.py:515
  2.3 0.0 copy-start.1
  2.3 0.5 %collective-permute-start = (f32[200,128]{1,0:T(8,128)S(1)}, f32[200,128]{1,0:T(8,128)S(1)}, u32[]{:S(2)}, u32[]{:S(2)}) collective-permute-start(f32[200,128]{1,0:T(8,128)S(1)} %get-tuple-element.14), channel_id=1, source_target_pairs={{0,4},{4,0},{8,12},{12,8},{16,20},{20,16},{24,28},{28,24},{1,5},{5... | collective-permute-start | bytes 307208 | tf_op jit(solution)/shard_map/ppermute | solution.py:521
  2.9 0.7 %collective-permute-start.1 = (f32[200,128]{1,0:T(8,128)S(1)}, f32[200,128]{1,0:T(8,128)S(1)}, u32[]{:S(2)}, u32[]{:S(2)}) collective-permute-start(f32[200,128]{1,0:T(8,128)S(1)} %get-tuple-element.13), channel_id=1, source_target_pairs={{4,8},{8,4},{12,16},{16,12},{20,24},{24,20},{5,9},{9,5},{13,17},{1... | collective-permute-start | bytes 307208 | tf_op jit(solution)/shard_map/ppermute | solution.py:522
  3.5 0.0 copy-done
  3.5 0.0 copy-done.1
  3.6 2.0 %gather_sources.1.source_ref = f32[4,48,128]{2,1,0:T(8,128)S(1)} custom-call(f32[3,256,128]{2,1,0:T(8,128)S(1)} %bitcast.26, s32[48,128]{1,0:T(8,128)S(1)} %bitcast.28), custom_call_target="tpu_custom_call" | custom-call | tf_op jit(solution)/shard_map/gather_sources/pallas_call | solution.py:90
  5.5 0.0 copy-start.2
  5.5 0.0 collective-permute-done.margin_a
  5.5 0.0 collective-permute-done.1.margin_b
  5.6 0.6 %copy-done.2 = s32[1,1,2,24]{3,2,1,0:T(2,128)S(1)} copy-done((s32[1,1,2,24]{3,2,1,0:T(2,128)S(1)}, s32[1,1,2,24]{3,2,1,0:T(2,128)}, u32[]{:S(2)}) %copy-start.2) | copy-done | bytes 216
  6.2 5.6 %match_first.1 = f32[32,128]{1,0:T(8,128)S(1)} custom-call(s32[2,24]{1,0:T(2,128)S(1)} %bitcast.32, f32[1,128]{1,0:T(1,128)S(1)} %pad.8.pose_ref, f32[4,48,128]{2,1,0:T(8,128)S(1)} %gather_sources.1.source_ref, f32[200,128]{1,0:T(8,128)S(1)} %collective-permute-done.margin_a, f32[200,128]{1,0:T(8,128)S(1)} %collective-permute-done.1.margin_b), custom_call_target="tpu_custom_call" | custom-call | flops 1258291200 | bytes 1048576 | tf_op jit(solution)/shard_map/match_first/pallas_call | solution.py:472
  11.8 17.3 %all_to_all.22 = f32[32,1,128]{2,1,0:T(1,128)S(1)} all-to-all(f32[32,1,128]{2,1,0:T(1,128)S(1)} %bitcast.31), channel_id=1, replica_groups=mesh['line'=8,'seg'=4] {'line','seg'}, dimensions={0} | all-to-all | bytes 32768 | tf_op jit(solution)/shard_map/all_to_all | solution.py:499
  29.1 6.1 %match_second.1 = (f32[32,128]{1,0:T(8,128)S(1)}, f32[5,48,128]{2,1,0:T(8,128)}) custom-call(s32[2,24]{1,0:T(2,128)S(1)} %bitcast.33, f32[1,128]{1,0:T(1,128)S(1)} %pad.8.pose_ref, f32[32,128]{1,0:T(8,128)S(1)} %bitcast.29, f32[4,48,128]{2,1,0:T(8,128)S(1)} %gather_sources.1.source_ref, f32[200,128]{1,0:T(8,128)S(1)} %collective-permute-done.margin_a, ...), custom_call_target="tpu_custom_call" | custom-call | flops 1258291200 | bytes 1048576 | tf_op jit(solution)/shard_map/match_second/pallas_call | solution.py:486
  35.2 8.9 %all_to_all.23 = f32[32,1,128]{2,1,0:T(1,128)S(1)} all-to-all(f32[32,1,128]{2,1,0:T(1,128)S(1)} %bitcast.30), channel_id=1, replica_groups=mesh['line'=8,'seg'=4] {'line','seg'}, dimensions={0} | all-to-all | bytes 32768 | tf_op jit(solution)/shard_map/all_to_all | solution.py:499
  44.1 0.7 %solve_last.1 = (f32[1,12]{1,0:T(1,128)}, f32[1,1]{1,0:T(1,128)}) custom-call(f32[32,128]{1,0:T(8,128)S(1)} %bitcast.27), custom_call_target="tpu_custom_call" | custom-call | tf_op jit(solution)/shard_map/solve_last/pallas_call | solution.py:528
  (2 shorter events, 0.0 us)
Async XLA Ops:
  0.6 0.7 %copy-start.3 = (f32[12,1]{0,1:T(1,128)S(1)}, f32[12,1]{0,1:T(1,128)}, u32[]{:S(2)}) copy-start(f32[12,1]{0,1:T(1,128)} %param.7) | copy-start | bytes 148
  1.3 2.2 %copy-start = (f32[1,1,3,32768]{3,1,2,0:T(1,128)S(1)}, f32[1,1,3,32768]{3,1,2,0:T(1,128)}, u32[]{:S(2)}) copy-start(f32[1,1,3,32768]{3,1,2,0:T(1,128)} %param.4) | copy-start | bytes 1179652
  2.3 1.2 %copy-start.1 = (s32[1,1,2,3072]{3,2,1,0:T(2,128)S(1)}, s32[1,1,2,3072]{3,2,1,0:T(2,128)}, u32[]{:S(2)}) copy-start(s32[1,1,2,3072]{3,2,1,0:T(2,128)} %param.5) | copy-start | bytes 73732
  2.3 3.2 %collective-permute-start = (f32[200,128]{1,0:T(8,128)S(1)}, f32[200,128]{1,0:T(8,128)S(1)}, u32[]{:S(2)}, u32[]{:S(2)}) collective-permute-start(f32[200,128]{1,0:T(8,128)S(1)} %get-tuple-element.14), channel_id=1, source_target_pairs={{0,4},{4,0},{8,12},{12,8},{16,20},{20,16},{24,28},{28,24},{1,5},{5... | collective-permute-start | bytes 307208 | tf_op jit(solution)/shard_map/ppermute | solution.py:521
  2.9 2.7 %collective-permute-start.1 = (f32[200,128]{1,0:T(8,128)S(1)}, f32[200,128]{1,0:T(8,128)S(1)}, u32[]{:S(2)}, u32[]{:S(2)}) collective-permute-start(f32[200,128]{1,0:T(8,128)S(1)} %get-tuple-element.13), channel_id=1, source_target_pairs={{4,8},{8,4},{12,16},{16,12},{20,24},{24,20},{5,9},{9,5},{13,17},{1... | collective-permute-start | bytes 307208 | tf_op jit(solution)/shard_map/ppermute | solution.py:522
  5.5 0.7 %copy-start.2 = (s32[1,1,2,24]{3,2,1,0:T(2,128)S(1)}, s32[1,1,2,24]{3,2,1,0:T(2,128)}, u32[]{:S(2)}) copy-start(s32[1,1,2,24]{3,2,1,0:T(2,128)} %param.6) | copy-start | bytes 580

commit v5 on v4

--- a/solution.py
+++ b/solution.py
@@ -44,62 +44,72 @@
     return jnp.broadcast_to(value, TILE)
 
 
-def gather_kernel(points_ref, rows_ref, source_ref, table_ref, turned_ref, sems):
-    slot_rows = rows_ref.shape[0]
-    blocks = slot_rows // 2
-    starts = [0, points_ref.shape[1] - MROWS]
+def pack_kernel(points_hbm, pose_hbm, cells_hbm, sent_a, sent_b, cells_ref, pose_ref, sems):
+    odd = lax.axis_index("line") & 1
+    tail = points_hbm.shape[1] - MROWS
     copies = [
-        pltpu.make_async_copy(points_ref.at[:, pl.ds(starts[d], MROWS), :], table_ref.at[d], sems.at[d]) for d in range(2)
+        pltpu.make_async_copy(pose_hbm, pose_ref, sems.at[6]),
+        pltpu.make_async_copy(cells_hbm, cells_ref, sems.at[7]),
     ]
+    for n, (sent, first) in enumerate(((sent_a, (1 - odd) * tail), (sent_b, odd * tail))):
+        spot = pl.ds(pl.multiple_of(first, MROWS), MROWS)
+        for k in range(3):
+            copies.append(
+                pltpu.make_async_copy(points_hbm.at[k, spot, :], sent.at[pl.ds(MROWS * k, MROWS), :], sems.at[3 * n + k])
+            )
     for copy in copies:
         copy.start()
-    for v in range(slot_rows // 8):
-        source_ref[3, 8 * v : 8 * v + 8, :] = (rows_ref[8 * v : 8 * v + 8, :] >= 0).astype(F32)
+    for sent in (sent_a, sent_b):
+        sent[3 * MROWS :, :] = jnp.zeros(TILE, F32)
+    copies[0].wait()
+    for sent in (sent_a, sent_b):
+        sent[3 * MROWS : 3 * MROWS + 1, :12] = pose_ref[...]
+    for copy in copies[1:]:
+        copy.wait()
+
+
+def pack_call(points, pose, cells):
+    return pl.pallas_call(
+        pack_kernel,
+        in_specs=[HBM] * 3,
+        out_specs=vmem(3),
+        out_shape=[jax.ShapeDtypeStruct((3 * MROWS + 8, 128), F32)] * 2 + [jax.ShapeDtypeStruct(cells.shape, jnp.int32)],
+        scratch_shapes=[pltpu.VMEM((1, 12), F32), pltpu.SemaphoreType.DMA((8,))],
+        compiler_params=PARAMS,
+        name="pack_margins",
+    )(points, pose, cells)
+
+
+def turn_margin(margin_ref, turned_ref):
     group = MROWS // 8
-    for d in range(2):
-        copies[d].wait()
+    for k in range(3):
+        parts = [three_parts(margin_ref[MROWS * k + 8 * v : MROWS * k + 8 * v + 8, :]) for v in range(group)]
+        stack = jnp.concatenate([parts[v][p] for p in range(3) for v in range(group)], axis=0)
+        turned_ref[128 * k : 128 * k + 128, :] = jnp.transpose(stack).astype(BF16)
+
+
+def pick_rows(rows_ref, turned_ref, rows):
+    spots = [jnp.maximum(rows_ref[pl.ds(row, 1), :], 0) & (MARGIN - 1) for row in rows]
+    hits = []
+    for spot in spots:
+        high = spread_out(spot >> 7)
+        hit = [(high == iota(0) + 8 * v).astype(F32) for v in range(MROWS // 8)]
+        hits.append(jnp.concatenate(hit, axis=0).astype(BF16))
+    hit = jnp.concatenate(hits, axis=1)
+    return spots, jnp.dot(turned_ref[...], jnp.concatenate([hit] * 3, axis=0), preferred_element_type=F32)
+
+
+def pick_lanes(source_ref, rows, spots, picked):
+    for n, row in enumerate(rows):
+        low = spread_out(spots[n] & 127)
+        sums = [jnp.zeros(TILE, F32)] * 3
+        for v in range(16):
+            here = low == iota(0) + 8 * v
+            for k in range(3):
+                part = picked[128 * k + 8 * v : 128 * k + 8 * v + 8, 128 * n : 128 * n + 128]
+                sums[k] = jnp.where(here, part, sums[k])
         for k in range(3):
-            parts = [three_parts(table_ref[d, k, 8 * v : 8 * v + 8, :]) for v in range(group)]
-            stack = jnp.concatenate([parts[v][p] for p in range(3) for v in range(group)], axis=0)
-            turned_ref[d, 128 * k : 128 * k + 128, :] = jnp.transpose(stack).astype(BF16)
-        for first in range(0, blocks, WIDE):
-            chosen = range(first, min(first + WIDE, blocks))
-            spots = [jnp.maximum(rows_ref[2 * b + d : 2 * b + d + 1, :], 0) & (MARGIN - 1) for b in chosen]
-            hits = []
-            for spot in spots:
-                high = spread_out(spot >> 7)
-                hits.append(
-                    jnp.concatenate([(high == iota(0) + 8 * v).astype(F32) for v in range(group)], axis=0).astype(BF16)
-                )
-            hit = jnp.concatenate(hits, axis=1)
-            picked = jnp.dot(turned_ref[d], jnp.concatenate([hit] * 3, axis=0), preferred_element_type=F32)
-            for n, b in enumerate(chosen):
-                low = spread_out(spots[n] & 127)
-                sums = [jnp.zeros(TILE, F32)] * 3
-                for v in range(16):
-                    here = low == iota(0) + 8 * v
-                    for k in range(3):
-                        part = picked[128 * k + 8 * v : 128 * k + 8 * v + 8, 128 * n : 128 * n + 128]
-                        sums[k] = jnp.where(here, part, sums[k])
-                for k in range(3):
-                    source_ref[k, 2 * b + d : 2 * b + d + 1, :] = jnp.sum(sums[k], axis=0, keepdims=True)
-
-
-def gather(points, rows):
-    slot_rows = rows.shape[0]
-    return pl.pallas_call(
-        gather_kernel,
-        in_specs=[pl.BlockSpec(memory_space=pl.ANY)] + vmem(1),
-        out_specs=vmem(1)[0],
-        out_shape=jax.ShapeDtypeStruct((4, slot_rows, 128), F32),
-        scratch_shapes=[
-            pltpu.VMEM((2, 3, MROWS, 128), F32),
-            pltpu.VMEM((2, 3 * 128, 3 * MROWS), BF16),
-            pltpu.SemaphoreType.DMA((2,)),
-        ],
-        compiler_params=PARAMS,
-        name="gather_sources",
-    )(points, rows)
+            source_ref[k, pl.ds(row, 1), :] = jnp.sum(sums[k], axis=0, keepdims=True)
 
 
 def apply_pose(coefs, xyz):
@@ -196,41 +206,55 @@
     return raw * (xt[3] / (total + OUTLIER_MASS)), xt
 
 
-def match(own, nbrs, negc, dirs, cells_hbm, source_ref, margin_refs, scratch_refs, sums_ref, pose_row, out):
-    phi_refs, (cells_ref, cells_sem, world_ref, moved_ref, column_ref) = scratch_refs[:2], scratch_refs[2:7]
-    blocks = cells_ref.shape[1]
-    fetch = pltpu.make_async_copy(cells_hbm, cells_ref, cells_sem)
-    fetch.start()
-    out_ref = None if out is None else out[1]
+class Lists:
+    def __init__(self, dirs, cells_hbm, source_ref, scratch_refs):
+        self.dirs = dirs
+        self.source_ref = source_ref
+        self.cells_ref, cells_sem = scratch_refs[:2]
+        self.phi_refs = scratch_refs[2:4]
+        self.world_ref, self.moved_ref, self.column_ref = scratch_refs[4:7]
+        self.fetch = pltpu.make_async_copy(cells_hbm, self.cells_ref, cells_sem)
+        self.fetch.start()
+
+    def places(self, side):
+        d = self.dirs[side]
+        return [(side, 2 * b + d, self.cells_ref[d, b]) for b in range(self.cells_ref.shape[1])]
+
+
+def quick(lists, own, nbrs, negc, places, side_work, carry, out_ref):
     own_cols, near_cols = columns(own), [columns(near) for near in nbrs]
-    longest = jnp.zeros(TILE, F32)
-    for r in range(MROWS):
-        longest = jnp.maximum(longest, prepare(near_cols[0], margin_refs[0], phi_refs[0], r))
-    fetch.wait()
-    places = [(side, 2 * b + dirs[side], cells_ref[dirs[side], b]) for side in range(2) for b in range(blocks)]
-    later = list(range(MROWS))
-    each = -(-MROWS // max(1, blocks - 2))
-    carry = [jnp.zeros(TILE, F32) for _ in range(5)]
+    near_cols += [near_cols[0]] * (2 - len(near_cols))
+    phi_refs = lists.phi_refs
     found = []
     ahead = None
+    each = -(-len(side_work) // max(1, lists.cells_ref.shape[1] - 2))
     for n in range(-1, len(places)):
         block, ahead = ahead, None
         if n + 1 < len(places):
-            ahead = weigh(negc, own_cols, near_cols, phi_refs, source_ref, *places[n + 1])
-        for r in later[:each]:
-            longest = jnp.maximum(longest, prepare(near_cols[1], margin_refs[1], phi_refs[1], r))
-        later = later[each:]
+            ahead = weigh(negc, own_cols, near_cols, phi_refs, lists.source_ref, *places[n + 1])
+        for work in side_work[:each]:
+            work()
+        side_work = side_work[each:]
         if block is not None:
             side, row, _ = places[n]
             xt, m, length, spot, top, rest = block
             found.append((row, *finish(near_cols, side, xt, m, length, weighted_sums(phi_refs, side, spot, top, rest))))
     for row, result, xt in found:
         carry = add_block(carry, row, result, xt, out_ref)
+    return carry
+
+
+def no_sums():
+    return [jnp.zeros(TILE, F32) for _ in range(5)]
+
+
+def close(lists, own, nbrs, negc, margin_refs, carry, longest, pose_row, sums_ref, out):
+    out_ref = None if out is None else out[1]
     if out is not None:
         save = pltpu.make_async_copy(out[1], out[0], out[2])
         save.start()
     pack_sums(carry, pose_row, sums_ref)
-    size = spread_out(jnp.max(longest)) + spread_out(jnp.max(longest_source(own, nbrs, dirs, source_ref)))
+    size = spread_out(jnp.max(longest)) + spread_out(jnp.max(longest_source(own, nbrs, lists.dirs, lists.source_ref)))
     whole = jnp.sum(carry[3], axis=1, keepdims=True)
     share, energy = [spread_out(whole[q : q + 1, :]) for q in (3, 4)]
     bad = (size * -negc > QUICK_LIMIT) | (size * share > ENERGY_LIMIT * energy)
@@ -239,16 +263,18 @@
     def _():
         if out is not None:
             save.wait()
-        one_block = careful_setup(own, nbrs, negc, source_ref, margin_refs, world_ref, moved_ref, column_ref)
-        carry = tuple(jnp.zeros(TILE, F32) for _ in range(5))
+        one_block = careful_setup(
+            own, nbrs, negc, lists.source_ref, margin_refs, lists.world_ref, lists.moved_ref, lists.column_ref
+        )
+        carry = tuple(no_sums())
         for side in range(2):
-            d = dirs[side]
+            d = lists.dirs[side]
 
             def step(b, carry, side=side, d=d):
-                result, xt = one_block(side, 2 * b + d, cells_ref[d, b])
+                result, xt = one_block(side, 2 * b + d, lists.cells_ref[d, b])
                 return tuple(add_block(carry, 2 * b + d, result, xt, out_ref))
 
-            carry = lax.fori_loop(0, blocks, step, carry)
+            carry = lax.fori_loop(0, lists.cells_ref.shape[1], step, carry)
         pack_sums(carry, pose_row, sums_ref)
         if out is not None:
             save.start()
@@ -337,13 +363,68 @@
     return [1 - odd, odd]
 
 
-def first_kernel(cells_hbm, pose_ref, source_ref, margin_a, margin_b, sums_ref, *scratch_refs):
-    line = lax.axis_index("line")
-    own = pose_of_row(pose_ref[...])
-    nbrs = [pose_of_row(margin[3 * MROWS : 3 * MROWS + 1, :]) for margin in (margin_a, margin_b)]
-    negc = jnp.full(TILE, -LOG2E / (2.0 * SPREAD_START), F32)
-    margins = (margin_a, margin_b)
-    match(own, nbrs, negc, sides_of(line), cells_hbm, source_ref, margins, scratch_refs, sums_ref, 0.0, None)
+def features(near, margin_ref, phi_ref, longest):
+    cols = columns(near)
+
+    def make(r):
+        longest[0] = jnp.maximum(longest[0], prepare(cols, margin_ref, phi_ref, r))
+
+    return [functools.partial(make, r) for r in range(MROWS)]
+
+
+def first_negc():
+    return jnp.full(TILE, -LOG2E / (2.0 * SPREAD_START), F32)
+
+
+def pose_in(margin_ref):
+    return pose_of_row(margin_ref[3 * MROWS : 3 * MROWS + 1, :])
+
+
+def partner_kernel(
+    cells_hbm, rows_ref, sent_a, sent_b, margin_a, source_ref, part_ref, turned_a, turned_b, *scratch_refs
+):
+    dirs = sides_of(lax.axis_index("line"))
+    lists = Lists(dirs, cells_hbm, source_ref, scratch_refs)
+    own, near = pose_in(sent_a), pose_in(margin_a)
+    slot_rows = rows_ref.shape[0]
+    blocks = slot_rows // 2
+    for v in range(slot_rows // 8):
+        source_ref[3, 8 * v : 8 * v + 8, :] = (rows_ref[8 * v : 8 * v + 8, :] >= 0).astype(F32)
+
+    def gather_tasks(side, turned_ref):
+        tasks = []
+        for first in range(0, blocks, WIDE):
+            rows = [2 * b + dirs[side] for b in range(first, min(first + WIDE, blocks))]
+            held = []
+            tasks.append(lambda rows=rows, held=held: held.extend(pick_rows(rows_ref, turned_ref, rows)))
+            tasks.append(lambda rows=rows, held=held: pick_lanes(source_ref, rows, *held))
+        return tasks
+
+    turn_margin(sent_a, turned_a)
+    turn_margin(sent_b, turned_b)
+    longest = [jnp.zeros(TILE, F32)]
+    tasks = gather_tasks(0, turned_a)
+    for n in range(0, len(tasks) + 2, 2):
+        for task in tasks[n : n + 1] + tasks[max(n - 1, 0) : n]:
+            task()
+    for task in features(near, margin_a, lists.phi_refs[0], longest):
+        task()
+    lists.fetch.wait()
+    carry = quick(lists, own, [near], first_negc(), lists.places(0), gather_tasks(1, turned_b), no_sums(), None)
+    for n, value in enumerate(carry + longest):
+        part_ref[n] = value
+
+
+def other_kernel(cells_hbm, sent_a, source_ref, part_ref, margin_a, margin_b, sums_ref, *scratch_refs):
+    lists = Lists(sides_of(lax.axis_index("line")), cells_hbm, source_ref, scratch_refs)
+    own = pose_in(sent_a)
+    nbrs = [pose_in(margin) for margin in (margin_a, margin_b)]
+    longest = [part_ref[5]]
+    for task in features(nbrs[1], margin_b, lists.phi_refs[1], longest):
+        task()
+    lists.fetch.wait()
+    carry = quick(lists, own, nbrs, first_negc(), lists.places(1), [], [part_ref[n] for n in range(5)], None)
+    close(lists, own, nbrs, first_negc(), (margin_a, margin_b), carry, longest[0], 0.0, sums_ref, None)
 
 
 def solve(totals, old):
@@ -410,11 +491,12 @@
 
 
 def second_kernel(
-    lines, segs, cells_hbm, pose_ref, all_ref, source_ref, margin_a, margin_b,
-    sums_ref, out_hbm, *scratch_refs,
+    lines, segs, cells_hbm, sent_a, all_ref, source_ref, margin_a, margin_b,
+    sums_ref, out_hbm, out_ref, out_sem, *scratch_refs,
 ):
     line = lax.axis_index("line")
     dirs = sides_of(line)
+    lists = Lists(dirs, cells_hbm, source_ref, scratch_refs)
     partner = [jnp.clip(line + 2 * d - 1, 0, lines - 1) for d in dirs]
     sub = iota(0)
 
@@ -422,16 +504,19 @@
         return jnp.where(sub == 0, spread_out(a), jnp.where(sub == 1, spread_out(b), spread_out(c)))
 
     totals = stacked(*[line_sum(all_ref, n, segs) for n in (line, partner[0], partner[1])])
-    old = stacked(pose_ref[...], margin_a[3 * MROWS : 3 * MROWS + 1, :], margin_b[3 * MROWS : 3 * MROWS + 1, :])
+    old = stacked(*[ref[3 * MROWS : 3 * MROWS + 1, :] for ref in (sent_a, margin_a, margin_b)])
     new = solve(totals, old)
     negc = (-0.5 * LOG2E) / new_spread(all_ref)
-    own, near_a, near_b = [[spread_out(value[n : n + 1, :]) for value in new] for n in range(3)]
+    own, *nbrs = [[spread_out(value[n : n + 1, :]) for value in new] for n in range(3)]
+    longest = [jnp.zeros(TILE, F32)]
+    for task in features(nbrs[0], margin_a, lists.phi_refs[0], longest):
+        task()
+    lists.fetch.wait()
+    places = lists.places(0) + lists.places(1)
+    later = features(nbrs[1], margin_b, lists.phi_refs[1], longest)
+    carry = quick(lists, own, nbrs, negc, places, later, no_sums(), out_ref)
     margins = (margin_a, margin_b)
-    out_ref, out_sem = scratch_refs[7:9]
-    match(
-        own, [near_a, near_b], negc, dirs, cells_hbm, source_ref, margins, scratch_refs, sums_ref,
-        pose_row(new, POSE), (out_hbm, out_ref, out_sem),
-    )
+    close(lists, own, nbrs, negc, margins, carry, longest[0], pose_row(new, POSE), sums_ref, (out_hbm, out_ref, out_sem))
 
 
 def last_kernel(segs, all_ref, fitted_ref, spread_ref):
@@ -448,51 +533,72 @@
 
 
 ANY = pl.BlockSpec(memory_space=pl.ANY)
+HBM = pl.BlockSpec(memory_space=pltpu.HBM)
 PARAMS = pltpu.CompilerParams(vmem_limit_bytes=32 * 1024 * 1024)
 
 
 def scratch(cells):
     return [
+        pltpu.SMEM(cells.shape, jnp.int32),
+        pltpu.SemaphoreType.DMA,
         pltpu.VMEM((48, MARGIN), BF16),
         pltpu.VMEM((48, MARGIN), BF16),
-        pltpu.SMEM(cells.shape, jnp.int32),
-        pltpu.SemaphoreType.DMA,
         pltpu.VMEM((2, 3, MROWS, 128), F32),
         pltpu.VMEM((3, 128, 128), F32),
         pltpu.VMEM((3, 128, 128), F32),
     ]
 
 
-def pair_cost(cells):
-    pairs = cells.size * BLOCK * CT
+def in_hbm(value):
+    return pltpu.with_memory_space_constraint(value, pltpu.HBM)
+
+
+def pair_cost(cells, sides):
+    pairs = cells.size // 2 * sides * BLOCK * CT
     return pl.CostEstimate(flops=400 * pairs, bytes_accessed=1 << 20, transcendentals=pairs)
 
 
-def first_call(cells, pose_line, source, margin_a, margin_b, devices):
+def partner_call(cells, rows, sent_a, sent_b, margin_a):
     return pl.pallas_call(
-        first_kernel,
+        partner_kernel,
         in_specs=[ANY] + vmem(4),
+        out_specs=vmem(2),
+        out_shape=[
+            jax.ShapeDtypeStruct((4,) + rows.shape, F32),
+            jax.ShapeDtypeStruct((6,) + TILE, F32),
+        ],
+        scratch_shapes=[pltpu.VMEM((3 * 128, 3 * MROWS), BF16)] * 2 + scratch(cells),
+        compiler_params=PARAMS,
+        cost_estimate=pair_cost(cells, 1),
+        name="match_partner",
+    )(cells, rows, sent_a, sent_b, margin_a)
+
+
+def other_call(cells, sent_a, source, part, margin_a, margin_b, devices):
+    return pl.pallas_call(
+        other_kernel,
+        in_specs=[ANY] + vmem(5),
         out_specs=vmem(1)[0],
         out_shape=jax.ShapeDtypeStruct((devices, 128), F32),
         scratch_shapes=scratch(cells),
         compiler_params=PARAMS,
-        cost_estimate=pair_cost(cells),
-        name="match_first",
-    )(cells, pose_line, source, margin_a, margin_b)
-
-
-def second_call(cells, pose_line, everyone, source, margin_a, margin_b, lines, segs):
+        cost_estimate=pair_cost(cells, 1),
+        name="match_other",
+    )(cells, sent_a, source, part, margin_a, margin_b)
+
+
+def second_call(cells, sent_a, everyone, source, margin_a, margin_b, lines, segs):
     result = (5,) + source.shape[1:]
     return pl.pallas_call(
         functools.partial(second_kernel, lines, segs),
         in_specs=[ANY] + vmem(5),
         out_specs=vmem(1) + [ANY],
         out_shape=[jax.ShapeDtypeStruct((lines * segs, 128), F32), jax.ShapeDtypeStruct(result, F32)],
-        scratch_shapes=scratch(cells) + [pltpu.VMEM(result, F32), pltpu.SemaphoreType.DMA],
+        scratch_shapes=[pltpu.VMEM(result, F32), pltpu.SemaphoreType.DMA] + scratch(cells),
         compiler_params=PARAMS,
-        cost_estimate=pair_cost(cells),
+        cost_estimate=pair_cost(cells, 2),
         name="match_second",
-    )(cells, pose_line, everyone, source, margin_a, margin_b)
+    )(cells, sent_a, everyone, source, margin_a, margin_b)
 
 
 def exchange(sums):
@@ -505,25 +611,15 @@
     blocks = slots // BLOCK
     row_list = rows.reshape(2, blocks, 128).transpose(1, 0, 2).reshape(2 * blocks, 128)
     cell_ids = cells.reshape(2, blocks)
-    devices = lines * segs
-    odd = lax.axis_index("line") & 1
-    tail = own_points.shape[1] - MROWS
-    pose_line = jnp.pad(pose.reshape(1, 12), ((0, 0), (0, 116)))
-    pose_tile = jnp.pad(pose_line, ((0, 7), (0, 0)))
-
-    def margin_at(first):
-        part = lax.dynamic_slice_in_dim(own_points, first, MROWS, 1)
-        return jnp.concatenate([part.reshape(3 * MROWS, 128), pose_tile], axis=0)
-
-    pairs_a = [(i, i ^ 1) for i in range(lines) if i ^ 1 < lines]
-    pairs_b = [(i, ((i + 1) ^ 1) - 1) for i in range(lines)]
-    pairs_b = [(i, j) for i, j in pairs_b if 0 <= j < lines]
-    margin_a = lax.ppermute(margin_at(jnp.where(odd == 1, 0, tail)), "line", pairs_a)
-    margin_b = lax.ppermute(margin_at(jnp.where(odd == 1, tail, 0)), "line", pairs_b)
-    source = gather(own_points, row_list)
-    sums = first_call(cell_ids, pose_line, source, margin_a, margin_b, devices)
+    sent_a, sent_b, cell_ids = pack_call(in_hbm(own_points), in_hbm(pose.reshape(1, 12)), in_hbm(cell_ids))
+    pairs_a = [(i, i ^ 1) for i in range(lines)]
+    pairs_b = [(i, (((i + 1) ^ 1) - 1) % lines) for i in range(lines)]
+    margin_a = lax.ppermute(sent_a, "line", pairs_a)
+    margin_b = lax.ppermute(sent_b, "line", pairs_b)
+    source, part = partner_call(cell_ids, row_list, sent_a, sent_b, margin_a)
+    sums = other_call(cell_ids, sent_a, source, part, margin_a, margin_b, lines * segs)
     everyone = exchange(sums)
-    sums, result = second_call(cell_ids, pose_line, everyone, source, margin_a, margin_b, lines, segs)
+    sums, result = second_call(cell_ids, sent_a, everyone, source, margin_a, margin_b, lines, segs)
     everyone = exchange(sums)
     fitted, spread = pl.pallas_call(
         functools.partial(last_kernel, segs),

time: 45 us -> 41.7 us (0.927)
  blocking collectives: 26.1 us -> 20.4 us
  starting transfers between devices: 1.17 us -> 4.07 us
  local copies, waits for them, and re-layouts: 2.32 us -> 0.01 us
  Pallas kernels: 14.4 us -> 16.3 us
    all_to_all x2, blocking collectives: 26.1 us -> 20.4 us  [exchange(): return lax.all_to_all(sums, ('line', 'seg'), 0, 0)]
    ppermute x2, starting transfers between devices: 1.17 us -> 4.07 us  [the longest x1 3.56 us: on_device(): margin_b = lax.ppermute(sent_b, 'line', pairs_b)]
    pallas_call x2 -> x3, Pallas kernels: 7.58 us -> 9.47 us  [the longest x1 5.15 us: partner_call(): pl.pallas_call(partner_kernel, in_specs=[ANY] + vmem(4), out_specs=vmem(2...]
    unnamed x8 -> x2, local copies, waits for them, and re-layouts: 1.31 us -> 0.01 us
    dynamic_slice x1 -> x0, local copies, waits for them, and re-layouts: 1.01 us -> none  [margin_at(): part = lax.dynamic_slice_in_dim(own_points, first, MROWS, 1)]
  transfers between devices with their start and end apart: 2 -> 2, of which waited for: 0 -> 0; matrix products, arithmetic and copies ran while one was open for 0% -> 0% of each run, Pallas kernels for 4% -> 12%
where the time goes in v5:
time: 41.7 us; the launch traced here: 41.5 us
  blocking collectives  20.4 us (49%)
  Pallas kernels  16.3 us (39%)
  starting transfers between devices  4.07 us (10%)
  between operations  0.68 us (2%)
    all_to_all x2, blocking collectives, exchange(): return lax.all_to_all(sums, ('line', 'seg'), 0, 0)  20.4 us
    pallas_call x1, Pallas kernels, second_call(): pl.pallas_call(functools.partial(second_kernel, lines, segs), in_specs=[A...  6.15 us
    pallas_call x1, Pallas kernels, partner_call(): pl.pallas_call(partner_kernel, in_specs=[ANY] + vmem(4), out_specs=vmem(2...  5.15 us
    ppermute x1, starting transfers between devices, on_device(): margin_b = lax.ppermute(sent_b, 'line', pairs_b)  3.56 us
    pallas_call x1, Pallas kernels, other_call(): pl.pallas_call(other_kernel, in_specs=[ANY] + vmem(5), out_specs=vmem(1)[...  3.37 us
    pallas_call x1, Pallas kernels, pack_call(): pl.pallas_call(pack_kernel, in_specs=[HBM] * 3, out_specs=vmem(3), out_sh...  0.95 us
  transfers between devices with their start and end apart: 2, of which 0 were waited for; matrix products, arithmetic and copies ran while one was open for 0% of the time, Pallas kernels for 12%

profile of v5, /device:TPU:0, one launch (start us, length us, event | category | flops | bytes accessed | tf_op | source)
XLA Modules:
  0.0 41.5 jit_solution(12958306775068469246)
XLA Ops:
  0.6 0.0 copy-start
  0.6 0.9 %pack_margins.1 = (f32[200,128]{1,0:T(8,128)S(1)}, f32[200,128]{1,0:T(8,128)S(1)}, s32[2,24]{1,0:T(2,128)S(1)}) custom-call(f32[3,256,128]{2,1,0:T(8,128)} %bitcast.28, f32[1,12]{1,0:T(1,128)} %bitcast.30, s32[2,24]{1,0:T(2,128)} %bitcast.29), custom_call_target="tpu_custom_call" | custom-call | tf_op jit(solution)/shard_map/pack_margins/pallas_call | solution.py:72
  1.6 0.5 %collective-permute-start = (f32[200,128]{1,0:T(8,128)S(1)}, f32[200,128]{1,0:T(8,128)S(1)}, u32[]{:S(2)}, u32[]{:S(2)}) collective-permute-start(f32[200,128]{1,0:T(8,128)S(1)} %get-tuple-element.13.sent_a), channel_id=1, source_target_pairs={{0,4},{4,0},{8,12},{12,8},{16,20},{20,16},{24,28},{28,24},{1,5},{5... | collective-permute-start | bytes 307208 | tf_op jit(solution)/shard_map/ppermute | solution.py:617
  2.1 3.6 %collective-permute-start.1 = (f32[200,128]{1,0:T(8,128)S(1)}, f32[200,128]{1,0:T(8,128)S(1)}, u32[]{:S(2)}, u32[]{:S(2)}) collective-permute-start(f32[200,128]{1,0:T(8,128)S(1)} %get-tuple-element.14.sent_b), channel_id=1, source_target_pairs={{0,28},{4,8},{8,4},{12,16},{16,12},{20,24},{24,20},{28,0},{1,29},{... | collective-permute-start | bytes 307208 | tf_op jit(solution)/shard_map/ppermute | solution.py:618
  5.7 0.0 collective-permute-done.margin_a
  5.7 0.0 copy-done
  5.7 5.2 %match_partner.1 = (f32[4,48,128]{2,1,0:T(8,128)S(1)}, f32[6,8,128]{2,1,0:T(8,128)S(1)}) custom-call(s32[2,24]{1,0:T(2,128)S(1)} %get-tuple-element.12.cells_hbm, s32[48,128]{1,0:T(8,128)S(1)} %bitcast.27, f32[200,128]{1,0:T(8,128)S(1)} %get-tuple-element.13.sent_a, f32[200,128]{1,0:T(8,128)S(1)} %get-tuple-element.14.sent_b, ...), custom_call_target="tpu_custom_call" | custom-call | flops 629145600 | bytes 1048576 | tf_op jit(solution)/shard_map/match_partner/pallas_call | solution.py:562
  10.8 0.0 collective-permute-done.1.margin_b
  10.8 3.4 %match_other.1 = f32[32,128]{1,0:T(8,128)S(1)} custom-call(s32[2,24]{1,0:T(2,128)S(1)} %get-tuple-element.12.cells_hbm, f32[200,128]{1,0:T(8,128)S(1)} %get-tuple-element.13.sent_a, f32[4,48,128]{2,1,0:T(8,128)S(1)} %get-tuple-element.15.source_ref, f32[6,8,128]{2,1,0:T(8,128)S(1)} %get-tuple-element.16.part_ref, ...), custom_call_target="tpu_custom_call" | custom-call | flops 629145600 | bytes 1048576 | tf_op jit(solution)/shard_map/match_other/pallas_call | solution.py:578
  14.2 11.6 %all_to_all.22 = f32[32,1,128]{2,1,0:T(1,128)S(1)} all-to-all(f32[32,1,128]{2,1,0:T(1,128)S(1)} %bitcast.26), channel_id=1, replica_groups=mesh['line'=8,'seg'=4] {'line','seg'}, dimensions={0} | all-to-all | bytes 32768 | tf_op jit(solution)/shard_map/all_to_all | solution.py:605
  25.8 6.2 %match_second.1 = (f32[32,128]{1,0:T(8,128)S(1)}, f32[5,48,128]{2,1,0:T(8,128)}) custom-call(s32[2,24]{1,0:T(2,128)S(1)} %get-tuple-element.12.cells_hbm, f32[200,128]{1,0:T(8,128)S(1)} %get-tuple-element.13.sent_a, f32[32,128]{1,0:T(8,128)S(1)} %bitcast.24, f32[4,48,128]{2,1,0:T(8,128)S(1)} %get-tuple-element.15.source_ref, ...), custom_call_target="tpu_custom_call" | custom-call | flops 1258291200 | bytes 1048576 | tf_op jit(solution)/shard_map/match_second/pallas_call | solution.py:592
  32.0 8.9 %all_to_all.23 = f32[32,1,128]{2,1,0:T(1,128)S(1)} all-to-all(f32[32,1,128]{2,1,0:T(1,128)S(1)} %bitcast.25), channel_id=1, replica_groups=mesh['line'=8,'seg'=4] {'line','seg'}, dimensions={0} | all-to-all | bytes 32768 | tf_op jit(solution)/shard_map/all_to_all | solution.py:605
  40.8 0.7 %solve_last.1 = (f32[1,12]{1,0:T(1,128)}, f32[1,1]{1,0:T(1,128)}) custom-call(f32[32,128]{1,0:T(8,128)S(1)} %bitcast.23), custom_call_target="tpu_custom_call" | custom-call | tf_op jit(solution)/shard_map/solve_last/pallas_call | solution.py:624
Async XLA Ops:
  0.6 5.0 %copy-start = (s32[1,1,2,3072]{3,2,1,0:T(2,128)S(1)}, s32[1,1,2,3072]{3,2,1,0:T(2,128)}, u32[]{:S(2)}) copy-start(s32[1,1,2,3072]{3,2,1,0:T(2,128)} %param.5) | copy-start | bytes 73732
  1.6 4.1 %collective-permute-start = (f32[200,128]{1,0:T(8,128)S(1)}, f32[200,128]{1,0:T(8,128)S(1)}, u32[]{:S(2)}, u32[]{:S(2)}) collective-permute-start(f32[200,128]{1,0:T(8,128)S(1)} %get-tuple-element.13.sent_a), channel_id=1, source_target_pairs={{0,4},{4,0},{8,12},{12,8},{16,20},{20,16},{24,28},{28,24},{1,5},{5... | collective-permute-start | bytes 307208 | tf_op jit(solution)/shard_map/ppermute | solution.py:617
  2.1 8.7 %collective-permute-start.1 = (f32[200,128]{1,0:T(8,128)S(1)}, f32[200,128]{1,0:T(8,128)S(1)}, u32[]{:S(2)}, u32[]{:S(2)}) collective-permute-start(f32[200,128]{1,0:T(8,128)S(1)} %get-tuple-element.14.sent_b), channel_id=1, source_target_pairs={{0,28},{4,8},{8,4},{12,16},{16,12},{20,24},{24,20},{28,0},{1,29},{... | collective-permute-start | bytes 307208 | tf_op jit(solution)/shard_map/ppermute | solution.py:618

commit v6 on v5

--- a/solution.py
+++ b/solution.py
@@ -173,7 +173,8 @@
     return longest
 
 
-def weigh(negc, own, near, phi_refs, source_ref, side, row, cell):
+def coefficients(negc, own, near, source_ref, place):
+    side, row, _ = place
     sub = iota(0)
     xt = [spread_out(source_ref[k, pl.ds(row, 1), :]) for k in range(4)]
     m = combine(own, xt) + (own[3] - near[side][3])
@@ -181,19 +182,22 @@
     coef = jnp.where(sub == 3, negc, jnp.where(sub == 4, negc * length, (-2.0 * negc) * m))
     high, middle, low = three_parts(coef)
     stack = jnp.concatenate([high, high, high, middle, middle, low], axis=0)
+    return jnp.transpose(stack).astype(BF16), xt, m, length
+
+
+def weigh(phi_refs, place, coef):
+    side, _, cell = place
     spot = pl.ds(pl.multiple_of(jnp.maximum(cell, 0) * CT, CT), CT)
-    power = jnp.dot(jnp.transpose(stack).astype(BF16), phi_refs[side][:, spot], preferred_element_type=F32)
-    weight = jnp.exp2(power)
+    power = jnp.dot(coef, phi_refs[side][:, spot], preferred_element_type=F32)
+    weight = jnp.transpose(jnp.exp2(power))
     top = weight.astype(BF16)
     rest = (weight - top.astype(F32)).astype(BF16)
-    return xt, m, length, spot, top, rest
-
-
-def weighted_sums(phi_refs, side, spot, top, rest):
-    last = (((1,), (1,)), ((), ()))
-    features = phi_refs[side][:32, spot]
-    sums = lax.dot_general(features, top, last, preferred_element_type=F32)
-    sums = sums + lax.dot_general(features, rest, last, preferred_element_type=F32)
+    return phi_refs[side][:32, spot], jnp.concatenate([top, rest], axis=1)
+
+
+def weighted_sums(features, weights):
+    sums = jnp.dot(features, weights, preferred_element_type=F32)
+    sums = sums[:, :BLOCK] + sums[:, BLOCK:]
     return sums[0:8] + sums[8:16] + sums[16:24]
 
 
@@ -207,9 +211,10 @@
 
 
 class Lists:
-    def __init__(self, dirs, cells_hbm, source_ref, scratch_refs):
-        self.dirs = dirs
+    def __init__(self, cells_hbm, source_ref, margin_refs, scratch_refs):
+        self.dirs = sides_of(lax.axis_index("line"))
         self.source_ref = source_ref
+        self.margin_refs = margin_refs
         self.cells_ref, cells_sem = scratch_refs[:2]
         self.phi_refs = scratch_refs[2:4]
         self.world_ref, self.moved_ref, self.column_ref = scratch_refs[4:7]
@@ -221,34 +226,41 @@
         return [(side, 2 * b + d, self.cells_ref[d, b]) for b in range(self.cells_ref.shape[1])]
 
 
-def quick(lists, own, nbrs, negc, places, side_work, carry, out_ref):
-    own_cols, near_cols = columns(own), [columns(near) for near in nbrs]
-    near_cols += [near_cols[0]] * (2 - len(near_cols))
-    phi_refs = lists.phi_refs
+def quick(lists, own, nbrs, negc, sides, carry, longest, out_ref):
+    own_cols, near_cols = columns(own), {side: columns(nbrs[side]) for side in sides}
+    longest = [longest]
+
+    def features(side, rows):
+        for r in rows:
+            length = prepare(near_cols[side], lists.margin_refs[side], lists.phi_refs[side], r)
+            longest[0] = jnp.maximum(longest[0], length)
+
+    features(sides[0], range(MROWS))
+    lists.fetch.wait()
+    places = [place for side in sides for place in lists.places(side)]
+    each = -(-MROWS // max(1, len(places) // len(sides) - 2))
+    coefs = [coefficients(negc, own_cols, near_cols, lists.source_ref, place) for place in places]
     found = []
     ahead = None
-    each = -(-len(side_work) // max(1, lists.cells_ref.shape[1] - 2))
     for n in range(-1, len(places)):
         block, ahead = ahead, None
         if n + 1 < len(places):
-            ahead = weigh(negc, own_cols, near_cols, phi_refs, lists.source_ref, *places[n + 1])
-        for work in side_work[:each]:
-            work()
-        side_work = side_work[each:]
+            ahead = weigh(lists.phi_refs, places[n + 1], coefs[n + 1][0])
+        for side in sides[1:]:
+            features(side, range(min((n + 1) * each, MROWS), min((n + 2) * each, MROWS)))
         if block is not None:
-            side, row, _ = places[n]
-            xt, m, length, spot, top, rest = block
-            found.append((row, *finish(near_cols, side, xt, m, length, weighted_sums(phi_refs, side, spot, top, rest))))
-    for row, result, xt in found:
+            found.append(weighted_sums(*block))
+    for (side, row, _), (_, xt, m, length), sums in zip(places, coefs, found):
+        result, xt = finish(near_cols, side, xt, m, length, sums)
         carry = add_block(carry, row, result, xt, out_ref)
-    return carry
+    return carry, longest[0]
 
 
 def no_sums():
     return [jnp.zeros(TILE, F32) for _ in range(5)]
 
 
-def close(lists, own, nbrs, negc, margin_refs, carry, longest, pose_row, sums_ref, out):
+def close(lists, own, nbrs, negc, carry, longest, pose_row, sums_ref, out):
     out_ref = None if out is None else out[1]
     if out is not None:
         save = pltpu.make_async_copy(out[1], out[0], out[2])
@@ -264,7 +276,7 @@
         if out is not None:
             save.wait()
         one_block = careful_setup(
-            own, nbrs, negc, lists.source_ref, margin_refs, lists.world_ref, lists.moved_ref, lists.column_ref
+            own, nbrs, negc, lists.source_ref, lists.margin_refs, lists.world_ref, lists.moved_ref, lists.column_ref
         )
         carry = tuple(no_sums())
         for side in range(2):
@@ -363,68 +375,48 @@
     return [1 - odd, odd]
 
 
-def features(near, margin_ref, phi_ref, longest):
-    cols = columns(near)
-
-    def make(r):
-        longest[0] = jnp.maximum(longest[0], prepare(cols, margin_ref, phi_ref, r))
-
-    return [functools.partial(make, r) for r in range(MROWS)]
-
-
-def first_negc():
-    return jnp.full(TILE, -LOG2E / (2.0 * SPREAD_START), F32)
-
-
 def pose_in(margin_ref):
     return pose_of_row(margin_ref[3 * MROWS : 3 * MROWS + 1, :])
 
 
-def partner_kernel(
-    cells_hbm, rows_ref, sent_a, sent_b, margin_a, source_ref, part_ref, turned_a, turned_b, *scratch_refs
-):
+def gather_kernel(rows_ref, sent_a, sent_b, source_ref, turned_a, turned_b):
     dirs = sides_of(lax.axis_index("line"))
-    lists = Lists(dirs, cells_hbm, source_ref, scratch_refs)
-    own, near = pose_in(sent_a), pose_in(margin_a)
     slot_rows = rows_ref.shape[0]
     blocks = slot_rows // 2
     for v in range(slot_rows // 8):
         source_ref[3, 8 * v : 8 * v + 8, :] = (rows_ref[8 * v : 8 * v + 8, :] >= 0).astype(F32)
-
-    def gather_tasks(side, turned_ref):
-        tasks = []
+    turn_margin(sent_a, turned_a)
+    turn_margin(sent_b, turned_b)
+    last = None
+    for side, turned_ref in enumerate((turned_a, turned_b)):
         for first in range(0, blocks, WIDE):
             rows = [2 * b + dirs[side] for b in range(first, min(first + WIDE, blocks))]
-            held = []
-            tasks.append(lambda rows=rows, held=held: held.extend(pick_rows(rows_ref, turned_ref, rows)))
-            tasks.append(lambda rows=rows, held=held: pick_lanes(source_ref, rows, *held))
-        return tasks
-
-    turn_margin(sent_a, turned_a)
-    turn_margin(sent_b, turned_b)
-    longest = [jnp.zeros(TILE, F32)]
-    tasks = gather_tasks(0, turned_a)
-    for n in range(0, len(tasks) + 2, 2):
-        for task in tasks[n : n + 1] + tasks[max(n - 1, 0) : n]:
-            task()
-    for task in features(near, margin_a, lists.phi_refs[0], longest):
-        task()
-    lists.fetch.wait()
-    carry = quick(lists, own, [near], first_negc(), lists.places(0), gather_tasks(1, turned_b), no_sums(), None)
-    for n, value in enumerate(carry + longest):
+            found = rows, *pick_rows(rows_ref, turned_ref, rows)
+            if last is not None:
+                pick_lanes(source_ref, *last)
+            last = found
+    pick_lanes(source_ref, *last)
+
+
+def partner_kernel(cells_hbm, sent_a, source_ref, margin_a, part_ref, *scratch_refs):
+    lists = Lists(cells_hbm, source_ref, (margin_a, None), scratch_refs)
+    nothing = jnp.zeros(TILE, F32)
+    carry, longest = quick(lists, pose_in(sent_a), [pose_in(margin_a)], first_negc(), [0], no_sums(), nothing, None)
+    for n, value in enumerate(carry + [longest]):
         part_ref[n] = value
 
 
 def other_kernel(cells_hbm, sent_a, source_ref, part_ref, margin_a, margin_b, sums_ref, *scratch_refs):
-    lists = Lists(sides_of(lax.axis_index("line")), cells_hbm, source_ref, scratch_refs)
+    lists = Lists(cells_hbm, source_ref, (margin_a, margin_b), scratch_refs)
     own = pose_in(sent_a)
     nbrs = [pose_in(margin) for margin in (margin_a, margin_b)]
-    longest = [part_ref[5]]
-    for task in features(nbrs[1], margin_b, lists.phi_refs[1], longest):
-        task()
-    lists.fetch.wait()
-    carry = quick(lists, own, nbrs, first_negc(), lists.places(1), [], [part_ref[n] for n in range(5)], None)
-    close(lists, own, nbrs, first_negc(), (margin_a, margin_b), carry, longest[0], 0.0, sums_ref, None)
+    part = [part_ref[n] for n in range(6)]
+    carry, longest = quick(lists, own, nbrs, first_negc(), [1], part[:5], part[5], None)
+    close(lists, own, nbrs, first_negc(), carry, longest, 0.0, sums_ref, None)
+
+
+def first_negc():
+    return jnp.full(TILE, -LOG2E / (2.0 * SPREAD_START), F32)
 
 
 def solve(totals, old):
@@ -495,9 +487,8 @@
     sums_ref, out_hbm, out_ref, out_sem, *scratch_refs,
 ):
     line = lax.axis_index("line")
-    dirs = sides_of(line)
-    lists = Lists(dirs, cells_hbm, source_ref, scratch_refs)
-    partner = [jnp.clip(line + 2 * d - 1, 0, lines - 1) for d in dirs]
+    lists = Lists(cells_hbm, source_ref, (margin_a, margin_b), scratch_refs)
+    partner = [jnp.clip(line + 2 * d - 1, 0, lines - 1) for d in lists.dirs]
     sub = iota(0)
 
     def stacked(a, b, c):
@@ -508,15 +499,8 @@
     new = solve(totals, old)
     negc = (-0.5 * LOG2E) / new_spread(all_ref)
     own, *nbrs = [[spread_out(value[n : n + 1, :]) for value in new] for n in range(3)]
-    longest = [jnp.zeros(TILE, F32)]
-    for task in features(nbrs[0], margin_a, lists.phi_refs[0], longest):
-        task()
-    lists.fetch.wait()
-    places = lists.places(0) + lists.places(1)
-    later = features(nbrs[1], margin_b, lists.phi_refs[1], longest)
-    carry = quick(lists, own, nbrs, negc, places, later, no_sums(), out_ref)
-    margins = (margin_a, margin_b)
-    close(lists, own, nbrs, negc, margins, carry, longest[0], pose_row(new, POSE), sums_ref, (out_hbm, out_ref, out_sem))
+    carry, longest = quick(lists, own, nbrs, negc, [0, 1], no_sums(), jnp.zeros(TILE, F32), out_ref)
+    close(lists, own, nbrs, negc, carry, longest, pose_row(new, POSE), sums_ref, (out_hbm, out_ref, out_sem))
 
 
 def last_kernel(segs, all_ref, fitted_ref, spread_ref):
@@ -558,20 +542,30 @@
     return pl.CostEstimate(flops=400 * pairs, bytes_accessed=1 << 20, transcendentals=pairs)
 
 
-def partner_call(cells, rows, sent_a, sent_b, margin_a):
+def gather_call(rows, sent_a, sent_b):
+    return pl.pallas_call(
+        gather_kernel,
+        in_specs=vmem(3),
+        out_specs=vmem(1)[0],
+        out_shape=jax.ShapeDtypeStruct((4,) + rows.shape, F32),
+        scratch_shapes=[pltpu.VMEM((3 * 128, 3 * MROWS), BF16)] * 2,
+        compiler_params=PARAMS,
+        cost_estimate=pl.CostEstimate(flops=10**9, bytes_accessed=1 << 20, transcendentals=0),
+        name="gather_sources",
+    )(rows, sent_a, sent_b)
+
+
+def partner_call(cells, sent_a, source, margin_a):
     return pl.pallas_call(
         partner_kernel,
-        in_specs=[ANY] + vmem(4),
-        out_specs=vmem(2),
-        out_shape=[
-            jax.ShapeDtypeStruct((4,) + rows.shape, F32),
-            jax.ShapeDtypeStruct((6,) + TILE, F32),
-        ],
-        scratch_shapes=[pltpu.VMEM((3 * 128, 3 * MROWS), BF16)] * 2 + scratch(cells),
+        in_specs=[ANY] + vmem(3),
+        out_specs=vmem(1)[0],
+        out_shape=jax.ShapeDtypeStruct((6,) + TILE, F32),
+        scratch_shapes=scratch(cells),
         compiler_params=PARAMS,
         cost_estimate=pair_cost(cells, 1),
         name="match_partner",
-    )(cells, rows, sent_a, sent_b, margin_a)
+    )(cells, sent_a, source, margin_a)
 
 
 def other_call(cells, sent_a, source, part, margin_a, margin_b, devices):
@@ -616,7 +610,8 @@
     pairs_b = [(i, (((i + 1) ^ 1) - 1) % lines) for i in range(lines)]
     margin_a = lax.ppermute(sent_a, "line", pairs_a)
     margin_b = lax.ppermute(sent_b, "line", pairs_b)
-    source, part = partner_call(cell_ids, row_list, sent_a, sent_b, margin_a)
+    source = gather_call(row_list, sent_a, sent_b)
+    part = partner_call(cell_ids, sent_a, source, margin_a)
     sums = other_call(cell_ids, sent_a, source, part, margin_a, margin_b, lines * segs)
     everyone = exchange(sums)
     sums, result = second_call(cell_ids, sent_a, everyone, source, margin_a, margin_b, lines, segs)

time: 41.7 us -> 39.4 us (0.945)
  Pallas kernels: 16.3 us -> 14.5 us
  blocking collectives: 20.4 us -> 19.8 us
    pallas_call x1 -> x2, Pallas kernels: 5.15 us -> 4.46 us  [the longest x1 2.77 us: partner_call(): pl.pallas_call(partner_kernel, in_specs=[ANY] + vmem(3), out_specs=vmem(1...]
    pallas_call x1, Pallas kernels: 6.15 us -> 5.47 us  [second_call(): pl.pallas_call(functools.partial(second_kernel, lines, segs), in_specs=[A...]
    all_to_all x2, blocking collectives: 20.4 us -> 19.8 us  [exchange(): return lax.all_to_all(sums, ('line', 'seg'), 0, 0)]
  transfers between devices with their start and end apart: 2 -> 2, of which waited for: 0 -> 0; matrix products, arithmetic and copies ran while one was open for 0% -> 0% of each run, Pallas kernels for 12% -> 11%
where the time goes in v6:
time: 39.4 us; the launch traced here: 39.1 us
  blocking collectives  19.8 us (50%)
  Pallas kernels  14.5 us (37%)
  starting transfers between devices  4.07 us (10%)
  between operations  0.7 us (2%)
    all_to_all x2, blocking collectives, exchange(): return lax.all_to_all(sums, ('line', 'seg'), 0, 0)  19.8 us
    pallas_call x1, Pallas kernels, second_call(): pl.pallas_call(functools.partial(second_kernel, lines, segs), in_specs=[A...  5.47 us
    ppermute x1, starting transfers between devices, on_device(): margin_b = lax.ppermute(sent_b, 'line', pairs_b)  3.56 us
    pallas_call x1, Pallas kernels, other_call(): pl.pallas_call(other_kernel, in_specs=[ANY] + vmem(5), out_specs=vmem(1)[...  3 us
    pallas_call x1, Pallas kernels, partner_call(): pl.pallas_call(partner_kernel, in_specs=[ANY] + vmem(3), out_specs=vmem(1...  2.77 us
    pallas_call x1, Pallas kernels, gather_call(): pl.pallas_call(gather_kernel, in_specs=vmem(3), out_specs=vmem(1)[0], out...  1.69 us
    pallas_call x1, Pallas kernels, pack_call(): pl.pallas_call(pack_kernel, in_specs=[HBM] * 3, out_specs=vmem(3), out_sh...  0.95 us
  transfers between devices with their start and end apart: 2, of which 0 were waited for; matrix products, arithmetic and copies ran while one was open for 0% of the time, Pallas kernels for 11%

profile of v6, /device:TPU:0, one launch (start us, length us, event | category | flops | bytes accessed | tf_op | source)
XLA Modules:
  0.0 39.1 jit_solution(965938545912822603)
XLA Ops:
  0.6 0.0 copy-start
  0.6 0.9 %pack_margins.1 = (f32[200,128]{1,0:T(8,128)S(1)}, f32[200,128]{1,0:T(8,128)S(1)}, s32[2,24]{1,0:T(2,128)S(1)}) custom-call(f32[3,256,128]{2,1,0:T(8,128)} %bitcast.28, f32[1,12]{1,0:T(1,128)} %bitcast.30, s32[2,24]{1,0:T(2,128)} %bitcast.29), custom_call_target="tpu_custom_call" | custom-call | tf_op jit(solution)/shard_map/pack_margins/pallas_call | solution.py:72
  1.6 0.5 %collective-permute-start = (f32[200,128]{1,0:T(8,128)S(1)}, f32[200,128]{1,0:T(8,128)S(1)}, u32[]{:S(2)}, u32[]{:S(2)}) collective-permute-start(f32[200,128]{1,0:T(8,128)S(1)} %get-tuple-element.11.sent_a), channel_id=1, source_target_pairs={{0,4},{4,0},{8,12},{12,8},{16,20},{20,16},{24,28},{28,24},{1,5},{5... | collective-permute-start | bytes 307208 | tf_op jit(solution)/shard_map/ppermute | solution.py:611
  2.1 3.6 %collective-permute-start.1 = (f32[200,128]{1,0:T(8,128)S(1)}, f32[200,128]{1,0:T(8,128)S(1)}, u32[]{:S(2)}, u32[]{:S(2)}) collective-permute-start(f32[200,128]{1,0:T(8,128)S(1)} %get-tuple-element.12.sent_b), channel_id=1, source_target_pairs={{0,28},{4,8},{8,4},{12,16},{16,12},{20,24},{24,20},{28,0},{1,29},{... | collective-permute-start | bytes 307208 | tf_op jit(solution)/shard_map/ppermute | solution.py:612
  5.7 0.0 copy-done
  5.7 1.7 %gather_sources.1.source_ref = f32[4,48,128]{2,1,0:T(8,128)S(1)} custom-call(s32[48,128]{1,0:T(8,128)S(1)} %bitcast.27, f32[200,128]{1,0:T(8,128)S(1)} %get-tuple-element.11.sent_a, f32[200,128]{1,0:T(8,128)S(1)} %get-tuple-element.12.sent_b), custom_call_target="tpu_custom_call" | custom-call | flops 1000000000 | bytes 1048576 | tf_op jit(solution)/shard_map/gather_sources/pallas_call | solution.py:546
  7.4 0.0 collective-permute-done.margin_a
  7.4 2.8 %match_partner.1.part_ref = f32[6,8,128]{2,1,0:T(8,128)S(1)} custom-call(s32[2,24]{1,0:T(2,128)S(1)} %get-tuple-element.10.cells_hbm, f32[200,128]{1,0:T(8,128)S(1)} %get-tuple-element.11.sent_a, f32[4,48,128]{2,1,0:T(8,128)S(1)} %gather_sources.1.source_ref, f32[200,128]{1,0:T(8,128)S(1)} %collective-permute-done.margin_a), custom_call_target="tpu_custom_call" | custom-call | flops 629145600 | bytes 1048576 | tf_op jit(solution)/shard_map/match_partner/pallas_call | solution.py:559
  10.2 0.0 collective-permute-done.1.margin_b
  10.2 3.0 %match_other.1 = f32[32,128]{1,0:T(8,128)S(1)} custom-call(s32[2,24]{1,0:T(2,128)S(1)} %get-tuple-element.10.cells_hbm, f32[200,128]{1,0:T(8,128)S(1)} %get-tuple-element.11.sent_a, f32[4,48,128]{2,1,0:T(8,128)S(1)} %gather_sources.1.source_ref, f32[6,8,128]{2,1,0:T(8,128)S(1)} %match_partner.1.part_ref, f32[200,128]{1,0:T(8,128)S(1)} %collective-permute-done.margin_a, ...), custom_call_target="tpu_custom_call" | custom-call | flops 629145600 | bytes 1048576 | tf_op jit(solution)/shard_map/match_other/pallas_call | solution.py:572
  13.2 10.9 %all_to_all.22 = f32[32,1,128]{2,1,0:T(1,128)S(1)} all-to-all(f32[32,1,128]{2,1,0:T(1,128)S(1)} %bitcast.26), channel_id=1, replica_groups=mesh['line'=8,'seg'=4] {'line','seg'}, dimensions={0} | all-to-all | bytes 32768 | tf_op jit(solution)/shard_map/all_to_all | solution.py:599
  24.1 5.5 %match_second.1 = (f32[32,128]{1,0:T(8,128)S(1)}, f32[5,48,128]{2,1,0:T(8,128)}) custom-call(s32[2,24]{1,0:T(2,128)S(1)} %get-tuple-element.10.cells_hbm, f32[200,128]{1,0:T(8,128)S(1)} %get-tuple-element.11.sent_a, f32[32,128]{1,0:T(8,128)S(1)} %bitcast.24, f32[4,48,128]{2,1,0:T(8,128)S(1)} %gather_sources.1.source_ref, ...), custom_call_target="tpu_custom_call" | custom-call | flops 1258291200 | bytes 1048576 | tf_op jit(solution)/shard_map/match_second/pallas_call | solution.py:586
  29.6 8.9 %all_to_all.23 = f32[32,1,128]{2,1,0:T(1,128)S(1)} all-to-all(f32[32,1,128]{2,1,0:T(1,128)S(1)} %bitcast.25), channel_id=1, replica_groups=mesh['line'=8,'seg'=4] {'line','seg'}, dimensions={0} | all-to-all | bytes 32768 | tf_op jit(solution)/shard_map/all_to_all | solution.py:599
  38.5 0.7 %solve_last.1 = (f32[1,12]{1,0:T(1,128)}, f32[1,1]{1,0:T(1,128)}) custom-call(f32[32,128]{1,0:T(8,128)S(1)} %bitcast.23), custom_call_target="tpu_custom_call" | custom-call | tf_op jit(solution)/shard_map/solve_last/pallas_call | solution.py:619
Async XLA Ops:
  0.6 5.0 %copy-start = (s32[1,1,2,3072]{3,2,1,0:T(2,128)S(1)}, s32[1,1,2,3072]{3,2,1,0:T(2,128)}, u32[]{:S(2)}) copy-start(s32[1,1,2,3072]{3,2,1,0:T(2,128)} %param.5) | copy-start | bytes 73732
  1.6 5.8 %collective-permute-start = (f32[200,128]{1,0:T(8,128)S(1)}, f32[200,128]{1,0:T(8,128)S(1)}, u32[]{:S(2)}, u32[]{:S(2)}) collective-permute-start(f32[200,128]{1,0:T(8,128)S(1)} %get-tuple-element.11.sent_a), channel_id=1, source_target_pairs={{0,4},{4,0},{8,12},{12,8},{16,20},{20,16},{24,28},{28,24},{1,5},{5... | collective-permute-start | bytes 307208 | tf_op jit(solution)/shard_map/ppermute | solution.py:611
  2.1 8.0 %collective-permute-start.1 = (f32[200,128]{1,0:T(8,128)S(1)}, f32[200,128]{1,0:T(8,128)S(1)}, u32[]{:S(2)}, u32[]{:S(2)}) collective-permute-start(f32[200,128]{1,0:T(8,128)S(1)} %get-tuple-element.12.sent_b), channel_id=1, source_target_pairs={{0,28},{4,8},{8,4},{12,16},{16,12},{20,24},{24,20},{28,0},{1,29},{... | collective-permute-start | bytes 307208 | tf_op jit(solution)/shard_map/ppermute | solution.py:612

commit v7 on v6

--- a/solution.py
+++ b/solution.py
@@ -15,6 +15,8 @@
 MROWS = MARGIN // 128
 TILES = CT // 128
 GROUPS = BLOCK // 8
+LEAD = 48
+LAG = 3
 WIDE = 4
 QUICK_LIMIT = 1000.0
 ENERGY_LIMIT = 400.0
@@ -72,42 +74,34 @@
     return pl.pallas_call(
         pack_kernel,
         in_specs=[HBM] * 3,
-        out_specs=vmem(3),
-        out_shape=[jax.ShapeDtypeStruct((3 * MROWS + 8, 128), F32)] * 2 + [jax.ShapeDtypeStruct(cells.shape, jnp.int32)],
+        out_specs=vmem(2) + [SMEM],
+        out_shape=[jax.ShapeDtypeStruct((3 * MROWS + 8, 128), F32)] * 2 + [pltpu.SMEM(cells.shape, jnp.int32)],
         scratch_shapes=[pltpu.VMEM((1, 12), F32), pltpu.SemaphoreType.DMA((8,))],
         compiler_params=PARAMS,
         name="pack_margins",
     )(points, pose, cells)
 
 
-def turn_margin(margin_ref, turned_ref):
-    group = MROWS // 8
-    for k in range(3):
-        parts = [three_parts(margin_ref[MROWS * k + 8 * v : MROWS * k + 8 * v + 8, :]) for v in range(group)]
-        stack = jnp.concatenate([parts[v][p] for p in range(3) for v in range(group)], axis=0)
-        turned_ref[128 * k : 128 * k + 128, :] = jnp.transpose(stack).astype(BF16)
-
-
-def pick_rows(rows_ref, turned_ref, rows):
+def pick_columns(rows_ref, margin_parts, rows):
     spots = [jnp.maximum(rows_ref[pl.ds(row, 1), :], 0) & (MARGIN - 1) for row in rows]
     hits = []
     for spot in spots:
-        high = spread_out(spot >> 7)
-        hit = [(high == iota(0) + 8 * v).astype(F32) for v in range(MROWS // 8)]
+        low = spread_out(spot & 127)
+        hit = [(low == iota(0) + 8 * v).astype(F32) for v in range(16)]
         hits.append(jnp.concatenate(hit, axis=0).astype(BF16))
     hit = jnp.concatenate(hits, axis=1)
-    return spots, jnp.dot(turned_ref[...], jnp.concatenate([hit] * 3, axis=0), preferred_element_type=F32)
-
-
-def pick_lanes(source_ref, rows, spots, picked):
+    return spots, jnp.dot(margin_parts, jnp.concatenate([hit] * 3, axis=0), preferred_element_type=F32)
+
+
+def pick_rows(source_ref, rows, spots, picked):
     for n, row in enumerate(rows):
-        low = spread_out(spots[n] & 127)
+        high = spread_out(spots[n] >> 7)
         sums = [jnp.zeros(TILE, F32)] * 3
-        for v in range(16):
-            here = low == iota(0) + 8 * v
+        for v in range(MROWS // 8):
+            here = high == iota(0) + 8 * v
             for k in range(3):
-                part = picked[128 * k + 8 * v : 128 * k + 8 * v + 8, 128 * n : 128 * n + 128]
-                sums[k] = jnp.where(here, part, sums[k])
+                first = MROWS * k + 8 * v
+                sums[k] = jnp.where(here, picked[first : first + 8, 128 * n : 128 * n + 128], sums[k])
         for k in range(3):
             source_ref[k, pl.ds(row, 1), :] = jnp.sum(sums[k], axis=0, keepdims=True)
 
@@ -185,8 +179,7 @@
     return jnp.transpose(stack).astype(BF16), xt, m, length
 
 
-def weigh(phi_refs, place, coef):
-    side, _, cell = place
+def weigh(phi_refs, side, cell, coef):
     spot = pl.ds(pl.multiple_of(jnp.maximum(cell, 0) * CT, CT), CT)
     power = jnp.dot(coef, phi_refs[side][:, spot], preferred_element_type=F32)
     weight = jnp.transpose(jnp.exp2(power))
@@ -211,19 +204,20 @@
 
 
 class Lists:
-    def __init__(self, cells_hbm, source_ref, margin_refs, scratch_refs):
+    def __init__(self, cells_ref, source_ref, margin_refs, scratch_refs):
         self.dirs = sides_of(lax.axis_index("line"))
         self.source_ref = source_ref
         self.margin_refs = margin_refs
-        self.cells_ref, cells_sem = scratch_refs[:2]
-        self.phi_refs = scratch_refs[2:4]
-        self.world_ref, self.moved_ref, self.column_ref = scratch_refs[4:7]
-        self.fetch = pltpu.make_async_copy(cells_hbm, self.cells_ref, cells_sem)
-        self.fetch.start()
+        self.cells_ref = cells_ref
+        self.phi_refs = scratch_refs[:2]
+        self.world_ref, self.moved_ref, self.column_ref = scratch_refs[2:5]
 
     def places(self, side):
-        d = self.dirs[side]
-        return [(side, 2 * b + d, self.cells_ref[d, b]) for b in range(self.cells_ref.shape[1])]
+        return [(side, 2 * b + self.dirs[side], b) for b in range(self.cells_ref.shape[1])]
+
+    def cell(self, place):
+        side, _, b = place
+        return self.cells_ref[self.dirs[side], b]
 
 
 def quick(lists, own, nbrs, negc, sides, carry, longest, out_ref):
@@ -236,23 +230,24 @@
             longest[0] = jnp.maximum(longest[0], length)
 
     features(sides[0], range(MROWS))
-    lists.fetch.wait()
     places = [place for side in sides for place in lists.places(side)]
     each = -(-MROWS // max(1, len(places) // len(sides) - 2))
-    coefs = [coefficients(negc, own_cols, near_cols, lists.source_ref, place) for place in places]
-    found = []
+    coefs, found = {}, {}
     ahead = None
-    for n in range(-1, len(places)):
+    for n in range(-1, len(places) + LAG):
         block, ahead = ahead, None
+        for later in range(0 if n < 0 else n + 1 + LEAD, min(n + 2 + LEAD, len(places))):
+            coefs[later] = coefficients(negc, own_cols, near_cols, lists.source_ref, places[later])
         if n + 1 < len(places):
-            ahead = weigh(lists.phi_refs, places[n + 1], coefs[n + 1][0])
+            ahead = weigh(lists.phi_refs, places[n + 1][0], lists.cell(places[n + 1]), coefs[n + 1][0])
         for side in sides[1:]:
             features(side, range(min((n + 1) * each, MROWS), min((n + 2) * each, MROWS)))
         if block is not None:
-            found.append(weighted_sums(*block))
-    for (side, row, _), (_, xt, m, length), sums in zip(places, coefs, found):
-        result, xt = finish(near_cols, side, xt, m, length, sums)
-        carry = add_block(carry, row, result, xt, out_ref)
+            found[n] = weighted_sums(*block)
+        if n >= LAG:
+            side, row, _ = places[n - LAG]
+            result, xt = finish(near_cols, side, *coefs[n - LAG][1:], found[n - LAG])
+            carry = add_block(carry, row, result, xt, out_ref)
     return carry, longest[0]
 
 
@@ -266,12 +261,11 @@
         save = pltpu.make_async_copy(out[1], out[0], out[2])
         save.start()
     pack_sums(carry, pose_row, sums_ref)
-    size = spread_out(jnp.max(longest)) + spread_out(jnp.max(longest_source(own, nbrs, lists.dirs, lists.source_ref)))
-    whole = jnp.sum(carry[3], axis=1, keepdims=True)
-    share, energy = [spread_out(whole[q : q + 1, :]) for q in (3, 4)]
-    bad = (size * -negc > QUICK_LIMIT) | (size * share > ENERGY_LIMIT * energy)
-
-    @pl.when(jnp.max(bad.astype(F32)) > 0.0)
+    size = jnp.max(longest) + jnp.max(longest_source(own, nbrs, lists.dirs, lists.source_ref))
+    share, energy = [jnp.sum(carry[3][q : q + 1, :]) for q in (3, 4)]
+    bad = (size * jnp.max(-negc) > QUICK_LIMIT) | (size * share > ENERGY_LIMIT * energy)
+
+    @pl.when(bad)
     def _():
         if out is not None:
             save.wait()
@@ -379,23 +373,22 @@
     return pose_of_row(margin_ref[3 * MROWS : 3 * MROWS + 1, :])
 
 
-def gather_kernel(rows_ref, sent_a, sent_b, source_ref, turned_a, turned_b):
+def gather_kernel(rows_ref, sent_a, sent_b, source_ref):
     dirs = sides_of(lax.axis_index("line"))
     slot_rows = rows_ref.shape[0]
     blocks = slot_rows // 2
     for v in range(slot_rows // 8):
         source_ref[3, 8 * v : 8 * v + 8, :] = (rows_ref[8 * v : 8 * v + 8, :] >= 0).astype(F32)
-    turn_margin(sent_a, turned_a)
-    turn_margin(sent_b, turned_b)
     last = None
-    for side, turned_ref in enumerate((turned_a, turned_b)):
+    for side, sent in enumerate((sent_a, sent_b)):
+        parts = jnp.concatenate(three_parts(sent[: 3 * MROWS, :]), axis=1).astype(BF16)
         for first in range(0, blocks, WIDE):
             rows = [2 * b + dirs[side] for b in range(first, min(first + WIDE, blocks))]
-            found = rows, *pick_rows(rows_ref, turned_ref, rows)
+            found = rows, *pick_columns(rows_ref, parts, rows)
             if last is not None:
-                pick_lanes(source_ref, *last)
+                pick_rows(source_ref, *last)
             last = found
-    pick_lanes(source_ref, *last)
+    pick_rows(source_ref, *last)
 
 
 def partner_kernel(cells_hbm, sent_a, source_ref, margin_a, part_ref, *scratch_refs):
@@ -518,13 +511,12 @@
 
 ANY = pl.BlockSpec(memory_space=pl.ANY)
 HBM = pl.BlockSpec(memory_space=pltpu.HBM)
+SMEM = pl.BlockSpec(memory_space=pltpu.SMEM)
 PARAMS = pltpu.CompilerParams(vmem_limit_bytes=32 * 1024 * 1024)
 
 
-def scratch(cells):
+def scratch():
     return [
-        pltpu.SMEM(cells.shape, jnp.int32),
-        pltpu.SemaphoreType.DMA,
         pltpu.VMEM((48, MARGIN), BF16),
         pltpu.VMEM((48, MARGIN), BF16),
         pltpu.VMEM((2, 3, MROWS, 128), F32),
@@ -548,7 +540,6 @@
         in_specs=vmem(3),
         out_specs=vmem(1)[0],
         out_shape=jax.ShapeDtypeStruct((4,) + rows.shape, F32),
-        scratch_shapes=[pltpu.VMEM((3 * 128, 3 * MROWS), BF16)] * 2,
         compiler_params=PARAMS,
         cost_estimate=pl.CostEstimate(flops=10**9, bytes_accessed=1 << 20, transcendentals=0),
         name="gather_sources",
@@ -558,10 +549,10 @@
 def partner_call(cells, sent_a, source, margin_a):
     return pl.pallas_call(
         partner_kernel,
-        in_specs=[ANY] + vmem(3),
+        in_specs=[SMEM] + vmem(3),
         out_specs=vmem(1)[0],
         out_shape=jax.ShapeDtypeStruct((6,) + TILE, F32),
-        scratch_shapes=scratch(cells),
+        scratch_shapes=scratch(),
         compiler_params=PARAMS,
         cost_estimate=pair_cost(cells, 1),
         name="match_partner",
@@ -571,10 +562,10 @@
 def other_call(cells, sent_a, source, part, margin_a, margin_b, devices):
     return pl.pallas_call(
         other_kernel,
-        in_specs=[ANY] + vmem(5),
+        in_specs=[SMEM] + vmem(5),
         out_specs=vmem(1)[0],
         out_shape=jax.ShapeDtypeStruct((devices, 128), F32),
-        scratch_shapes=scratch(cells),
+        scratch_shapes=scratch(),
         compiler_params=PARAMS,
         cost_estimate=pair_cost(cells, 1),
         name="match_other",
@@ -585,10 +576,10 @@
     result = (5,) + source.shape[1:]
     return pl.pallas_call(
         functools.partial(second_kernel, lines, segs),
-        in_specs=[ANY] + vmem(5),
+        in_specs=[SMEM] + vmem(5),
         out_specs=vmem(1) + [ANY],
         out_shape=[jax.ShapeDtypeStruct((lines * segs, 128), F32), jax.ShapeDtypeStruct(result, F32)],
-        scratch_shapes=[pltpu.VMEM(result, F32), pltpu.SemaphoreType.DMA] + scratch(cells),
+        scratch_shapes=[pltpu.VMEM(result, F32), pltpu.SemaphoreType.DMA] + scratch(),
         compiler_params=PARAMS,
         cost_estimate=pair_cost(cells, 2),
         name="match_second",
@@ -606,6 +597,7 @@
     row_list = rows.reshape(2, blocks, 128).transpose(1, 0, 2).reshape(2 * blocks, 128)
     cell_ids = cells.reshape(2, blocks)
     sent_a, sent_b, cell_ids = pack_call(in_hbm(own_points), in_hbm(pose.reshape(1, 12)), in_hbm(cell_ids))
+    cell_ids = pltpu.with_memory_space_constraint(cell_ids, pltpu.SMEM)
     pairs_a = [(i, i ^ 1) for i in range(lines)]
     pairs_b = [(i, (((i + 1) ^ 1) - 1) % lines) for i in range(lines)]
     margin_a = lax.ppermute(sent_a, "line", pairs_a)

time: 39.4 us -> 38.5 us (0.977)
  Pallas kernels: 14.5 us -> 13.3 us
  blocking collectives: 19.8 us -> 20.2 us
    pallas_call x4, Pallas kernels: 12.2 us -> 11.1 us  [the longest x1 5.11 us: second_call(): pl.pallas_call(functools.partial(second_kernel, lines, segs), in_specs=[S...]
  transfers between devices with their start and end apart: 2 -> 2, of which waited for: 0 -> 0; matrix products, arithmetic and copies ran while one was open for 0% -> 0% of each run, Pallas kernels for 11% -> 10%
where the time goes in v7:
time: 38.5 us; the launch traced here: 38.3 us
  blocking collectives  20.2 us (52%)
  Pallas kernels  13.3 us (35%)
  starting transfers between devices  4.07 us (11%)
  between operations  0.7 us (2%)
    all_to_all x2, blocking collectives, exchange(): return lax.all_to_all(sums, ('line', 'seg'), 0, 0)  20.2 us
    pallas_call x1, Pallas kernels, second_call(): pl.pallas_call(functools.partial(second_kernel, lines, segs), in_specs=[S...  5.11 us
    ppermute x1, starting transfers between devices, on_device(): margin_b = lax.ppermute(sent_b, 'line', pairs_b)  3.56 us
    pallas_call x1, Pallas kernels, other_call(): pl.pallas_call(other_kernel, in_specs=[SMEM] + vmem(5), out_specs=vmem(1)...  2.65 us
    pallas_call x1, Pallas kernels, partner_call(): pl.pallas_call(partner_kernel, in_specs=[SMEM] + vmem(3), out_specs=vmem(...  2.45 us
    pallas_call x1, Pallas kernels, gather_call(): pl.pallas_call(gather_kernel, in_specs=vmem(3), out_specs=vmem(1)[0], out...  1.53 us
    pallas_call x1, Pallas kernels, pack_call(): pl.pallas_call(pack_kernel, in_specs=[HBM] * 3, out_specs=vmem(2) + [SMEM...  0.93 us
  transfers between devices with their start and end apart: 2, of which 0 were waited for; matrix products, arithmetic and copies ran while one was open for 0% of the time, Pallas kernels for 10%

profile of v7, /device:TPU:0, one launch (start us, length us, event | category | flops | bytes accessed | tf_op | source)
XLA Modules:
  0.0 38.3 jit_solution(17318679412167906638)
XLA Ops:
  0.6 0.0 copy-start
  0.6 0.9 %pack_margins.1 = (f32[200,128]{1,0:T(8,128)S(1)}, f32[200,128]{1,0:T(8,128)S(1)}, s32[2,24]{1,0:T(2,128)S(4)}) custom-call(f32[3,256,128]{2,1,0:T(8,128)} %bitcast.28, f32[1,12]{1,0:T(1,128)} %bitcast.30, s32[2,24]{1,0:T(2,128)} %bitcast.29), custom_call_target="tpu_custom_call" | custom-call | tf_op jit(solution)/shard_map/pack_margins/pallas_call | solution.py:74
  1.6 0.5 %collective-permute-start = (f32[200,128]{1,0:T(8,128)S(1)}, f32[200,128]{1,0:T(8,128)S(1)}, u32[]{:S(2)}, u32[]{:S(2)}) collective-permute-start(f32[200,128]{1,0:T(8,128)S(1)} %get-tuple-element.11.sent_a), channel_id=1, source_target_pairs={{0,4},{4,0},{8,12},{12,8},{16,20},{20,16},{24,28},{28,24},{1,5},{5... | collective-permute-start | bytes 307208 | tf_op jit(solution)/shard_map/ppermute | solution.py:603
  2.1 3.6 %collective-permute-start.1 = (f32[200,128]{1,0:T(8,128)S(1)}, f32[200,128]{1,0:T(8,128)S(1)}, u32[]{:S(2)}, u32[]{:S(2)}) collective-permute-start(f32[200,128]{1,0:T(8,128)S(1)} %get-tuple-element.12.sent_b), channel_id=1, source_target_pairs={{0,28},{4,8},{8,4},{12,16},{16,12},{20,24},{24,20},{28,0},{1,29},{... | collective-permute-start | bytes 307208 | tf_op jit(solution)/shard_map/ppermute | solution.py:604
  5.7 0.0 copy-done
  5.7 1.5 %gather_sources.1.source_ref = f32[4,48,128]{2,1,0:T(8,128)S(1)} custom-call(s32[48,128]{1,0:T(8,128)S(1)} %bitcast.27, f32[200,128]{1,0:T(8,128)S(1)} %get-tuple-element.11.sent_a, f32[200,128]{1,0:T(8,128)S(1)} %get-tuple-element.12.sent_b), custom_call_target="tpu_custom_call" | custom-call | flops 1000000000 | bytes 1048576 | tf_op jit(solution)/shard_map/gather_sources/pallas_call | solution.py:538
  7.2 0.0 collective-permute-done.margin_a
  7.2 2.5 %match_partner.1.part_ref = f32[6,8,128]{2,1,0:T(8,128)S(1)} custom-call(s32[2,24]{1,0:T(2,128)S(4)} %get-tuple-element.10.cells_hbm, f32[200,128]{1,0:T(8,128)S(1)} %get-tuple-element.11.sent_a, f32[4,48,128]{2,1,0:T(8,128)S(1)} %gather_sources.1.source_ref, f32[200,128]{1,0:T(8,128)S(1)} %collective-permute-done.margin_a), custom_call_target="tpu_custom_call" | custom-call | flops 629145600 | bytes 1048576 | tf_op jit(solution)/shard_map/match_partner/pallas_call | solution.py:550
  9.7 0.0 collective-permute-done.1.margin_b
  9.7 2.7 %match_other.1 = f32[32,128]{1,0:T(8,128)S(1)} custom-call(s32[2,24]{1,0:T(2,128)S(4)} %get-tuple-element.10.cells_hbm, f32[200,128]{1,0:T(8,128)S(1)} %get-tuple-element.11.sent_a, f32[4,48,128]{2,1,0:T(8,128)S(1)} %gather_sources.1.source_ref, f32[6,8,128]{2,1,0:T(8,128)S(1)} %match_partner.1.part_ref, f32[200,128]{1,0:T(8,128)S(1)} %collective-permute-done.margin_a, ...), custom_call_target="tpu_custom_call" | custom-call | flops 629145600 | bytes 1048576 | tf_op jit(solution)/shard_map/match_other/pallas_call | solution.py:563
  12.3 11.3 %all_to_all.22 = f32[32,1,128]{2,1,0:T(1,128)S(1)} all-to-all(f32[32,1,128]{2,1,0:T(1,128)S(1)} %bitcast.26), channel_id=1, replica_groups=mesh['line'=8,'seg'=4] {'line','seg'}, dimensions={0} | all-to-all | bytes 32768 | tf_op jit(solution)/shard_map/all_to_all | solution.py:590
  23.7 5.1 %match_second.1 = (f32[32,128]{1,0:T(8,128)S(1)}, f32[5,48,128]{2,1,0:T(8,128)}) custom-call(s32[2,24]{1,0:T(2,128)S(4)} %get-tuple-element.10.cells_hbm, f32[200,128]{1,0:T(8,128)S(1)} %get-tuple-element.11.sent_a, f32[32,128]{1,0:T(8,128)S(1)} %bitcast.24, f32[4,48,128]{2,1,0:T(8,128)S(1)} %gather_sources.1.source_ref, ...), custom_call_target="tpu_custom_call" | custom-call | flops 1258291200 | bytes 1048576 | tf_op jit(solution)/shard_map/match_second/pallas_call | solution.py:577
  28.8 8.9 %all_to_all.23 = f32[32,1,128]{2,1,0:T(1,128)S(1)} all-to-all(f32[32,1,128]{2,1,0:T(1,128)S(1)} %bitcast.25), channel_id=1, replica_groups=mesh['line'=8,'seg'=4] {'line','seg'}, dimensions={0} | all-to-all | bytes 32768 | tf_op jit(solution)/shard_map/all_to_all | solution.py:590
  37.7 0.7 %solve_last.1 = (f32[1,12]{1,0:T(1,128)}, f32[1,1]{1,0:T(1,128)}) custom-call(f32[32,128]{1,0:T(8,128)S(1)} %bitcast.23), custom_call_target="tpu_custom_call" | custom-call | tf_op jit(solution)/shard_map/solve_last/pallas_call | solution.py:611
Async XLA Ops:
  0.6 5.0 %copy-start = (s32[1,1,2,3072]{3,2,1,0:T(2,128)S(1)}, s32[1,1,2,3072]{3,2,1,0:T(2,128)}, u32[]{:S(2)}) copy-start(s32[1,1,2,3072]{3,2,1,0:T(2,128)} %param.5) | copy-start | bytes 73732
  1.6 5.6 %collective-permute-start = (f32[200,128]{1,0:T(8,128)S(1)}, f32[200,128]{1,0:T(8,128)S(1)}, u32[]{:S(2)}, u32[]{:S(2)}) collective-permute-start(f32[200,128]{1,0:T(8,128)S(1)} %get-tuple-element.11.sent_a), channel_id=1, source_target_pairs={{0,4},{4,0},{8,12},{12,8},{16,20},{20,16},{24,28},{28,24},{1,5},{5... | collective-permute-start | bytes 307208 | tf_op jit(solution)/shard_map/ppermute | solution.py:603
  2.1 7.6 %collective-permute-start.1 = (f32[200,128]{1,0:T(8,128)S(1)}, f32[200,128]{1,0:T(8,128)S(1)}, u32[]{:S(2)}, u32[]{:S(2)}) collective-permute-start(f32[200,128]{1,0:T(8,128)S(1)} %get-tuple-element.12.sent_b), channel_id=1, source_target_pairs={{0,28},{4,8},{8,4},{12,16},{16,12},{20,24},{24,20},{28,0},{1,29},{... | collective-permute-start | bytes 307208 | tf_op jit(solution)/shard_map/ppermute | solution.py:604

commit v8 on v7

--- a/solution.py
+++ b/solution.py
@@ -16,6 +16,7 @@
 TILES = CT // 128
 GROUPS = BLOCK // 8
 LEAD = 48
+NEAR = 1
 LAG = 3
 WIDE = 4
 QUICK_LIMIT = 1000.0
@@ -144,14 +145,17 @@
     return cols[0] * xyz[0] + cols[1] * xyz[1] + cols[2] * xyz[2]
 
 
-def prepare(near, margin_ref, phi_ref, r):
+def features_of(near, margin_ref, cell):
     sub = iota(0)
-    y = combine(near, [spread_out(margin_ref[k * MROWS + r : k * MROWS + r + 1, :]) for k in range(3)])
-    length = squared_length(y)
-    high, middle, low = three_parts(jnp.where(sub == 3, length, jnp.where(sub == 4, 1.0, y)))
-    for i, pair in enumerate(((high, middle), (low, high), (middle, high))):
-        phi_ref[16 * i : 16 * i + 16, 128 * r : 128 * r + 128] = jnp.concatenate(pair, axis=0).astype(BF16)
-    return length
+    tiles, longest = [], None
+    for t in range(TILES):
+        row = cell * TILES + t
+        y = combine(near, [spread_out(margin_ref[pl.ds(k * MROWS + row, 1), :]) for k in range(3)])
+        length = squared_length(y)
+        longest = length if longest is None else jnp.maximum(longest, length)
+        high, middle, low = three_parts(jnp.where(sub == 3, length, jnp.where(sub == 4, 1.0, y)))
+        tiles.append(jnp.concatenate([high, middle, low, high, middle, high], axis=0).astype(BF16))
+    return jnp.concatenate(tiles, axis=1), longest
 
 
 def longest_source(own, near, dirs, source_ref):
@@ -179,13 +183,12 @@
     return jnp.transpose(stack).astype(BF16), xt, m, length
 
 
-def weigh(phi_refs, side, cell, coef):
-    spot = pl.ds(pl.multiple_of(jnp.maximum(cell, 0) * CT, CT), CT)
-    power = jnp.dot(coef, phi_refs[side][:, spot], preferred_element_type=F32)
+def weigh(features, coef):
+    power = jnp.dot(coef, features, preferred_element_type=F32)
     weight = jnp.transpose(jnp.exp2(power))
     top = weight.astype(BF16)
     rest = (weight - top.astype(F32)).astype(BF16)
-    return phi_refs[side][:32, spot], jnp.concatenate([top, rest], axis=1)
+    return features[:32], jnp.concatenate([top, rest], axis=1)
 
 
 def weighted_sums(features, weights):
@@ -209,8 +212,7 @@
         self.source_ref = source_ref
         self.margin_refs = margin_refs
         self.cells_ref = cells_ref
-        self.phi_refs = scratch_refs[:2]
-        self.world_ref, self.moved_ref, self.column_ref = scratch_refs[2:5]
+        self.world_ref, self.moved_ref, self.column_ref = scratch_refs
 
     def places(self, side):
         return [(side, 2 * b + self.dirs[side], b) for b in range(self.cells_ref.shape[1])]
@@ -222,33 +224,27 @@
 
 def quick(lists, own, nbrs, negc, sides, carry, longest, out_ref):
     own_cols, near_cols = columns(own), {side: columns(nbrs[side]) for side in sides}
-    longest = [longest]
-
-    def features(side, rows):
-        for r in rows:
-            length = prepare(near_cols[side], lists.margin_refs[side], lists.phi_refs[side], r)
-            longest[0] = jnp.maximum(longest[0], length)
-
-    features(sides[0], range(MROWS))
     places = [place for side in sides for place in lists.places(side)]
-    each = -(-MROWS // max(1, len(places) // len(sides) - 2))
-    coefs, found = {}, {}
+    coefs, feats, found = {}, {}, {}
     ahead = None
     for n in range(-1, len(places) + LAG):
         block, ahead = ahead, None
         for later in range(0 if n < 0 else n + 1 + LEAD, min(n + 2 + LEAD, len(places))):
             coefs[later] = coefficients(negc, own_cols, near_cols, lists.source_ref, places[later])
+        for later in range(0 if n < 0 else n + 1 + NEAR, min(n + 2 + NEAR, len(places))):
+            side = places[later][0]
+            cell = jnp.maximum(lists.cell(places[later]), 0)
+            feats[later], length = features_of(near_cols[side], lists.margin_refs[side], cell)
+            longest = jnp.maximum(longest, length)
         if n + 1 < len(places):
-            ahead = weigh(lists.phi_refs, places[n + 1][0], lists.cell(places[n + 1]), coefs[n + 1][0])
-        for side in sides[1:]:
-            features(side, range(min((n + 1) * each, MROWS), min((n + 2) * each, MROWS)))
+            ahead = weigh(feats.pop(n + 1), coefs[n + 1][0])
         if block is not None:
             found[n] = weighted_sums(*block)
         if n >= LAG:
             side, row, _ = places[n - LAG]
             result, xt = finish(near_cols, side, *coefs[n - LAG][1:], found[n - LAG])
             carry = add_block(carry, row, result, xt, out_ref)
-    return carry, longest[0]
+    return carry, longest
 
 
 def no_sums():
@@ -517,8 +513,6 @@
 
 def scratch():
     return [
-        pltpu.VMEM((48, MARGIN), BF16),
-        pltpu.VMEM((48, MARGIN), BF16),
         pltpu.VMEM((2, 3, MROWS, 128), F32),
         pltpu.VMEM((3, 128, 128), F32),
         pltpu.VMEM((3, 128, 128), F32),

time: 38.5 us -> 38.2 us (level)
  Pallas kernels: 13.3 us -> 12.9 us
where the time goes in v8:
time: 38.2 us; the launch traced here: 38 us
  blocking collectives  20.4 us (53%)
  Pallas kernels  12.9 us (34%)
  starting transfers between devices  4.07 us (11%)
  between operations  0.7 us (2%)
    all_to_all x2, blocking collectives, exchange(): return lax.all_to_all(sums, ('line', 'seg'), 0, 0)  20.4 us
    pallas_call x1, Pallas kernels, second_call(): pl.pallas_call(functools.partial(second_kernel, lines, segs), in_specs=[S...  4.92 us
    ppermute x1, starting transfers between devices, on_device(): margin_b = lax.ppermute(sent_b, 'line', pairs_b)  3.56 us
    pallas_call x1, Pallas kernels, other_call(): pl.pallas_call(other_kernel, in_specs=[SMEM] + vmem(5), out_specs=vmem(1)...  2.5 us
    pallas_call x1, Pallas kernels, partner_call(): pl.pallas_call(partner_kernel, in_specs=[SMEM] + vmem(3), out_specs=vmem(...  2.3 us
    pallas_call x1, Pallas kernels, gather_call(): pl.pallas_call(gather_kernel, in_specs=vmem(3), out_specs=vmem(1)[0], out...  1.53 us
    pallas_call x1, Pallas kernels, pack_call(): pl.pallas_call(pack_kernel, in_specs=[HBM] * 3, out_specs=vmem(2) + [SMEM...  0.93 us
  transfers between devices with their start and end apart: 2, of which 0 were waited for; matrix products, arithmetic and copies ran while one was open for 0% of the time, Pallas kernels for 10%

profile of v8, /device:TPU:0, one launch (start us, length us, event | category | flops | bytes accessed | tf_op | source)
XLA Modules:
  0.0 38.0 jit_solution(16928775587819626936)
XLA Ops:
  0.6 0.0 copy-start
  0.6 0.9 %pack_margins.1 = (f32[200,128]{1,0:T(8,128)S(1)}, f32[200,128]{1,0:T(8,128)S(1)}, s32[2,24]{1,0:T(2,128)S(4)}) custom-call(f32[3,256,128]{2,1,0:T(8,128)} %bitcast.28, f32[1,12]{1,0:T(1,128)} %bitcast.30, s32[2,24]{1,0:T(2,128)} %bitcast.29), custom_call_target="tpu_custom_call" | custom-call | tf_op jit(solution)/shard_map/pack_margins/pallas_call | solution.py:75
  1.6 0.5 %collective-permute-start = (f32[200,128]{1,0:T(8,128)S(1)}, f32[200,128]{1,0:T(8,128)S(1)}, u32[]{:S(2)}, u32[]{:S(2)}) collective-permute-start(f32[200,128]{1,0:T(8,128)S(1)} %get-tuple-element.11.sent_a), channel_id=1, source_target_pairs={{0,4},{4,0},{8,12},{12,8},{16,20},{20,16},{24,28},{28,24},{1,5},{5... | collective-permute-start | bytes 307208 | tf_op jit(solution)/shard_map/ppermute | solution.py:597
  2.1 3.6 %collective-permute-start.1 = (f32[200,128]{1,0:T(8,128)S(1)}, f32[200,128]{1,0:T(8,128)S(1)}, u32[]{:S(2)}, u32[]{:S(2)}) collective-permute-start(f32[200,128]{1,0:T(8,128)S(1)} %get-tuple-element.12.sent_b), channel_id=1, source_target_pairs={{0,28},{4,8},{8,4},{12,16},{16,12},{20,24},{24,20},{28,0},{1,29},{... | collective-permute-start | bytes 307208 | tf_op jit(solution)/shard_map/ppermute | solution.py:598
  5.7 0.0 copy-done
  5.7 1.5 %gather_sources.1.source_ref = f32[4,48,128]{2,1,0:T(8,128)S(1)} custom-call(s32[48,128]{1,0:T(8,128)S(1)} %bitcast.27, f32[200,128]{1,0:T(8,128)S(1)} %get-tuple-element.11.sent_a, f32[200,128]{1,0:T(8,128)S(1)} %get-tuple-element.12.sent_b), custom_call_target="tpu_custom_call" | custom-call | flops 1000000000 | bytes 1048576 | tf_op jit(solution)/shard_map/gather_sources/pallas_call | solution.py:532
  7.2 0.0 collective-permute-done.margin_a
  7.2 2.3 %match_partner.1.part_ref = f32[6,8,128]{2,1,0:T(8,128)S(1)} custom-call(s32[2,24]{1,0:T(2,128)S(4)} %get-tuple-element.10.cells_hbm, f32[200,128]{1,0:T(8,128)S(1)} %get-tuple-element.11.sent_a, f32[4,48,128]{2,1,0:T(8,128)S(1)} %gather_sources.1.source_ref, f32[200,128]{1,0:T(8,128)S(1)} %collective-permute-done.margin_a), custom_call_target="tpu_custom_call" | custom-call | flops 629145600 | bytes 1048576 | tf_op jit(solution)/shard_map/match_partner/pallas_call | solution.py:544
  9.5 0.0 collective-permute-done.1.margin_b
  9.5 2.5 %match_other.1 = f32[32,128]{1,0:T(8,128)S(1)} custom-call(s32[2,24]{1,0:T(2,128)S(4)} %get-tuple-element.10.cells_hbm, f32[200,128]{1,0:T(8,128)S(1)} %get-tuple-element.11.sent_a, f32[4,48,128]{2,1,0:T(8,128)S(1)} %gather_sources.1.source_ref, f32[6,8,128]{2,1,0:T(8,128)S(1)} %match_partner.1.part_ref, f32[200,128]{1,0:T(8,128)S(1)} %collective-permute-done.margin_a, ...), custom_call_target="tpu_custom_call" | custom-call | flops 629145600 | bytes 1048576 | tf_op jit(solution)/shard_map/match_other/pallas_call | solution.py:557
  12.0 11.5 %all_to_all.22 = f32[32,1,128]{2,1,0:T(1,128)S(1)} all-to-all(f32[32,1,128]{2,1,0:T(1,128)S(1)} %bitcast.26), channel_id=1, replica_groups=mesh['line'=8,'seg'=4] {'line','seg'}, dimensions={0} | all-to-all | bytes 32768 | tf_op jit(solution)/shard_map/all_to_all | solution.py:584
  23.5 4.9 %match_second.1 = (f32[32,128]{1,0:T(8,128)S(1)}, f32[5,48,128]{2,1,0:T(8,128)}) custom-call(s32[2,24]{1,0:T(2,128)S(4)} %get-tuple-element.10.cells_hbm, f32[200,128]{1,0:T(8,128)S(1)} %get-tuple-element.11.sent_a, f32[32,128]{1,0:T(8,128)S(1)} %bitcast.24, f32[4,48,128]{2,1,0:T(8,128)S(1)} %gather_sources.1.source_ref, ...), custom_call_target="tpu_custom_call" | custom-call | flops 1258291200 | bytes 1048576 | tf_op jit(solution)/shard_map/match_second/pallas_call | solution.py:571
  28.5 8.9 %all_to_all.23 = f32[32,1,128]{2,1,0:T(1,128)S(1)} all-to-all(f32[32,1,128]{2,1,0:T(1,128)S(1)} %bitcast.25), channel_id=1, replica_groups=mesh['line'=8,'seg'=4] {'line','seg'}, dimensions={0} | all-to-all | bytes 32768 | tf_op jit(solution)/shard_map/all_to_all | solution.py:584
  37.3 0.7 %solve_last.1 = (f32[1,12]{1,0:T(1,128)}, f32[1,1]{1,0:T(1,128)}) custom-call(f32[32,128]{1,0:T(8,128)S(1)} %bitcast.23), custom_call_target="tpu_custom_call" | custom-call | tf_op jit(solution)/shard_map/solve_last/pallas_call | solution.py:605
Async XLA Ops:
  0.6 5.0 %copy-start = (s32[1,1,2,3072]{3,2,1,0:T(2,128)S(1)}, s32[1,1,2,3072]{3,2,1,0:T(2,128)}, u32[]{:S(2)}) copy-start(s32[1,1,2,3072]{3,2,1,0:T(2,128)} %param.5) | copy-start | bytes 73732
  1.6 5.6 %collective-permute-start = (f32[200,128]{1,0:T(8,128)S(1)}, f32[200,128]{1,0:T(8,128)S(1)}, u32[]{:S(2)}, u32[]{:S(2)}) collective-permute-start(f32[200,128]{1,0:T(8,128)S(1)} %get-tuple-element.11.sent_a), channel_id=1, source_target_pairs={{0,4},{4,0},{8,12},{12,8},{16,20},{20,16},{24,28},{28,24},{1,5},{5... | collective-permute-start | bytes 307208 | tf_op jit(solution)/shard_map/ppermute | solution.py:597
  2.1 7.4 %collective-permute-start.1 = (f32[200,128]{1,0:T(8,128)S(1)}, f32[200,128]{1,0:T(8,128)S(1)}, u32[]{:S(2)}, u32[]{:S(2)}) collective-permute-start(f32[200,128]{1,0:T(8,128)S(1)} %get-tuple-element.12.sent_b), channel_id=1, source_target_pairs={{0,28},{4,8},{8,4},{12,16},{16,12},{20,24},{24,20},{28,0},{1,29},{... | collective-permute-start | bytes 307208 | tf_op jit(solution)/shard_map/ppermute | solution.py:598

commit v9 on v8

--- a/solution.py
+++ b/solution.py
@@ -535,7 +535,7 @@
         out_specs=vmem(1)[0],
         out_shape=jax.ShapeDtypeStruct((4,) + rows.shape, F32),
         compiler_params=PARAMS,
-        cost_estimate=pl.CostEstimate(flops=10**9, bytes_accessed=1 << 20, transcendentals=0),
+        cost_estimate=pl.CostEstimate(flops=10**11, bytes_accessed=1 << 20, transcendentals=0),
         name="gather_sources",
     )(rows, sent_a, sent_b)
 

time: 38.2 us -> 38.2 us (level)
  blocking collectives: 20.4 us -> 21.1 us
  starting transfers between devices: 4.07 us -> 3.4 us
    all_to_all x2, blocking collectives: 20.4 us -> 21.1 us  [exchange(): return lax.all_to_all(sums, ('line', 'seg'), 0, 0)]
    ppermute x1, starting transfers between devices: 0.52 us -> 0.01 us  [on_device(): margin_a = lax.ppermute(sent_a, 'line', pairs_a)]
where the time goes in v9:
time: 38.2 us; the launch traced here: 38 us
  blocking collectives  21.1 us (55%)
  Pallas kernels  12.8 us (34%)
  starting transfers between devices  3.4 us (9%)
  between operations  0.7 us (2%)
    all_to_all x2, blocking collectives, exchange(): return lax.all_to_all(sums, ('line', 'seg'), 0, 0)  21.1 us
    pallas_call x1, Pallas kernels, second_call(): pl.pallas_call(functools.partial(second_kernel, lines, segs), in_specs=[S...  4.91 us
    ppermute x1, starting transfers between devices, on_device(): margin_b = lax.ppermute(sent_b, 'line', pairs_b)  3.4 us
    pallas_call x1, Pallas kernels, other_call(): pl.pallas_call(other_kernel, in_specs=[SMEM] + vmem(5), out_specs=vmem(1)...  2.49 us
    pallas_call x1, Pallas kernels, partner_call(): pl.pallas_call(partner_kernel, in_specs=[SMEM] + vmem(3), out_specs=vmem(...  2.3 us
    pallas_call x1, Pallas kernels, gather_call(): pl.pallas_call(gather_kernel, in_specs=vmem(3), out_specs=vmem(1)[0], out...  1.53 us
    pallas_call x1, Pallas kernels, pack_call(): pl.pallas_call(pack_kernel, in_specs=[HBM] * 3, out_specs=vmem(2) + [SMEM...  0.93 us
  transfers between devices with their start and end apart: 2, of which 0 were waited for; matrix products, arithmetic and copies ran while one was open for 0% of the time, Pallas kernels for 10%

profile of v9, /device:TPU:0, one launch (start us, length us, event | category | flops | bytes accessed | tf_op | source)
XLA Modules:
  0.0 38.0 jit_solution(4640119658858238712)
XLA Ops:
  0.6 0.0 copy-start
  0.6 0.9 %pack_margins.1 = (f32[200,128]{1,0:T(8,128)S(1)}, f32[200,128]{1,0:T(8,128)S(1)}, s32[2,24]{1,0:T(2,128)S(4)}) custom-call(f32[3,256,128]{2,1,0:T(8,128)} %bitcast.28, f32[1,12]{1,0:T(1,128)} %bitcast.30, s32[2,24]{1,0:T(2,128)} %bitcast.29), custom_call_target="tpu_custom_call" | custom-call | tf_op jit(solution)/shard_map/pack_margins/pallas_call | solution.py:75
  1.6 3.4 %collective-permute-start.1 = (f32[200,128]{1,0:T(8,128)S(1)}, f32[200,128]{1,0:T(8,128)S(1)}, u32[]{:S(2)}, u32[]{:S(2)}) collective-permute-start(f32[200,128]{1,0:T(8,128)S(1)} %get-tuple-element.12.sent_b), channel_id=1, source_target_pairs={{0,28},{4,8},{8,4},{12,16},{16,12},{20,24},{24,20},{28,0},{1,29},{... | collective-permute-start | bytes 307208 | tf_op jit(solution)/shard_map/ppermute | solution.py:598
  5.0 0.0 collective-permute-start
  5.0 0.0 copy-done
  5.0 1.5 %gather_sources.1.source_ref = f32[4,48,128]{2,1,0:T(8,128)S(1)} custom-call(s32[48,128]{1,0:T(8,128)S(1)} %bitcast.27, f32[200,128]{1,0:T(8,128)S(1)} %get-tuple-element.11.sent_a, f32[200,128]{1,0:T(8,128)S(1)} %get-tuple-element.12.sent_b), custom_call_target="tpu_custom_call" | custom-call | flops 99999997952 | bytes 1048576 | tf_op jit(solution)/shard_map/gather_sources/pallas_call | solution.py:532
  6.5 0.0 collective-permute-done.margin_a
  6.5 2.3 %match_partner.1.part_ref = f32[6,8,128]{2,1,0:T(8,128)S(1)} custom-call(s32[2,24]{1,0:T(2,128)S(4)} %get-tuple-element.10.cells_hbm, f32[200,128]{1,0:T(8,128)S(1)} %get-tuple-element.11.sent_a, f32[4,48,128]{2,1,0:T(8,128)S(1)} %gather_sources.1.source_ref, f32[200,128]{1,0:T(8,128)S(1)} %collective-permute-done.margin_a), custom_call_target="tpu_custom_call" | custom-call | flops 629145600 | bytes 1048576 | tf_op jit(solution)/shard_map/match_partner/pallas_call | solution.py:544
  8.8 0.0 collective-permute-done.1.margin_b
  8.9 2.5 %match_other.1 = f32[32,128]{1,0:T(8,128)S(1)} custom-call(s32[2,24]{1,0:T(2,128)S(4)} %get-tuple-element.10.cells_hbm, f32[200,128]{1,0:T(8,128)S(1)} %get-tuple-element.11.sent_a, f32[4,48,128]{2,1,0:T(8,128)S(1)} %gather_sources.1.source_ref, f32[6,8,128]{2,1,0:T(8,128)S(1)} %match_partner.1.part_ref, f32[200,128]{1,0:T(8,128)S(1)} %collective-permute-done.margin_a, ...), custom_call_target="tpu_custom_call" | custom-call | flops 629145600 | bytes 1048576 | tf_op jit(solution)/shard_map/match_other/pallas_call | solution.py:557
  11.4 12.2 %all_to_all.22 = f32[32,1,128]{2,1,0:T(1,128)S(1)} all-to-all(f32[32,1,128]{2,1,0:T(1,128)S(1)} %bitcast.26), channel_id=1, replica_groups=mesh['line'=8,'seg'=4] {'line','seg'}, dimensions={0} | all-to-all | bytes 32768 | tf_op jit(solution)/shard_map/all_to_all | solution.py:584
  23.6 4.9 %match_second.1 = (f32[32,128]{1,0:T(8,128)S(1)}, f32[5,48,128]{2,1,0:T(8,128)}) custom-call(s32[2,24]{1,0:T(2,128)S(4)} %get-tuple-element.10.cells_hbm, f32[200,128]{1,0:T(8,128)S(1)} %get-tuple-element.11.sent_a, f32[32,128]{1,0:T(8,128)S(1)} %bitcast.24, f32[4,48,128]{2,1,0:T(8,128)S(1)} %gather_sources.1.source_ref, ...), custom_call_target="tpu_custom_call" | custom-call | flops 1258291200 | bytes 1048576 | tf_op jit(solution)/shard_map/match_second/pallas_call | solution.py:571
  28.5 8.9 %all_to_all.23 = f32[32,1,128]{2,1,0:T(1,128)S(1)} all-to-all(f32[32,1,128]{2,1,0:T(1,128)S(1)} %bitcast.25), channel_id=1, replica_groups=mesh['line'=8,'seg'=4] {'line','seg'}, dimensions={0} | all-to-all | bytes 32768 | tf_op jit(solution)/shard_map/all_to_all | solution.py:584
  37.3 0.7 %solve_last.1 = (f32[1,12]{1,0:T(1,128)}, f32[1,1]{1,0:T(1,128)}) custom-call(f32[32,128]{1,0:T(8,128)S(1)} %bitcast.23), custom_call_target="tpu_custom_call" | custom-call | tf_op jit(solution)/shard_map/solve_last/pallas_call | solution.py:605
Async XLA Ops:
  0.6 4.4 %copy-start = (s32[1,1,2,3072]{3,2,1,0:T(2,128)S(1)}, s32[1,1,2,3072]{3,2,1,0:T(2,128)}, u32[]{:S(2)}) copy-start(s32[1,1,2,3072]{3,2,1,0:T(2,128)} %param.5) | copy-start | bytes 73732
  1.6 7.3 %collective-permute-start.1 = (f32[200,128]{1,0:T(8,128)S(1)}, f32[200,128]{1,0:T(8,128)S(1)}, u32[]{:S(2)}, u32[]{:S(2)}) collective-permute-start(f32[200,128]{1,0:T(8,128)S(1)} %get-tuple-element.12.sent_b), channel_id=1, source_target_pairs={{0,28},{4,8},{8,4},{12,16},{16,12},{20,24},{24,20},{28,0},{1,29},{... | collective-permute-start | bytes 307208 | tf_op jit(solution)/shard_map/ppermute | solution.py:598
  5.0 1.5 %collective-permute-start = (f32[200,128]{1,0:T(8,128)S(1)}, f32[200,128]{1,0:T(8,128)S(1)}, u32[]{:S(2)}, u32[]{:S(2)}) collective-permute-start(f32[200,128]{1,0:T(8,128)S(1)} %get-tuple-element.11.sent_a), channel_id=1, source_target_pairs={{0,4},{4,0},{8,12},{12,8},{16,20},{20,16},{24,28},{28,24},{1,5},{5... | collective-permute-start | bytes 307208 | tf_op jit(solution)/shard_map/ppermute | solution.py:597

commit v10 on v9

--- a/solution.py
+++ b/solution.py
@@ -203,7 +203,7 @@
     around = combine([spread_out(m[k : k + 1, :]) for k in range(3)], [spread_out(sums[k : k + 1, :]) for k in range(3)])
     energy = spread_out(sums[3:4, :]) - 2.0 * around + length * total
     raw = jnp.where(sub < 3, sums + near[side][3] * total, jnp.where(sub == 3, total, jnp.where(sub == 4, energy, 0.0)))
-    return raw * (xt[3] / (total + OUTLIER_MASS)), xt
+    return jnp.where(xt[3] > 0.0, raw / (total + OUTLIER_MASS), 0.0), xt
 
 
 class Lists:

time: 38.2 us -> 38.3 us (level)
  no operation moved by 1% of the time
where the time goes in v10:
time: 38.3 us; the launch traced here: 38 us
  blocking collectives  21.1 us (55%)
  Pallas kernels  12.9 us (34%)
  starting transfers between devices  3.4 us (9%)
  between operations  0.7 us (2%)
    all_to_all x2, blocking collectives, exchange(): return lax.all_to_all(sums, ('line', 'seg'), 0, 0)  21.1 us
    pallas_call x1, Pallas kernels, second_call(): pl.pallas_call(functools.partial(second_kernel, lines, segs), in_specs=[S...  4.93 us
    ppermute x1, starting transfers between devices, on_device(): margin_b = lax.ppermute(sent_b, 'line', pairs_b)  3.4 us
    pallas_call x1, Pallas kernels, other_call(): pl.pallas_call(other_kernel, in_specs=[SMEM] + vmem(5), out_specs=vmem(1)...  2.49 us
    pallas_call x1, Pallas kernels, partner_call(): pl.pallas_call(partner_kernel, in_specs=[SMEM] + vmem(3), out_specs=vmem(...  2.31 us
    pallas_call x1, Pallas kernels, gather_call(): pl.pallas_call(gather_kernel, in_specs=vmem(3), out_specs=vmem(1)[0], out...  1.53 us
    pallas_call x1, Pallas kernels, pack_call(): pl.pallas_call(pack_kernel, in_specs=[HBM] * 3, out_specs=vmem(2) + [SMEM...  0.93 us
  transfers between devices with their start and end apart: 2, of which 0 were waited for; matrix products, arithmetic and copies ran while one was open for 0% of the time, Pallas kernels for 10%

profile of v10, /device:TPU:0, one launch (start us, length us, event | category | flops | bytes accessed | tf_op | source)
XLA Modules:
  0.0 38.0 jit_solution(15067012838496120242)
XLA Ops:
  0.6 0.0 copy-start
  0.6 0.9 %pack_margins.1 = (f32[200,128]{1,0:T(8,128)S(1)}, f32[200,128]{1,0:T(8,128)S(1)}, s32[2,24]{1,0:T(2,128)S(4)}) custom-call(f32[3,256,128]{2,1,0:T(8,128)} %bitcast.28, f32[1,12]{1,0:T(1,128)} %bitcast.30, s32[2,24]{1,0:T(2,128)} %bitcast.29), custom_call_target="tpu_custom_call" | custom-call | tf_op jit(solution)/shard_map/pack_margins/pallas_call | solution.py:75
  1.6 3.4 %collective-permute-start.1 = (f32[200,128]{1,0:T(8,128)S(1)}, f32[200,128]{1,0:T(8,128)S(1)}, u32[]{:S(2)}, u32[]{:S(2)}) collective-permute-start(f32[200,128]{1,0:T(8,128)S(1)} %get-tuple-element.12.sent_b), channel_id=1, source_target_pairs={{0,28},{4,8},{8,4},{12,16},{16,12},{20,24},{24,20},{28,0},{1,29},{... | collective-permute-start | bytes 307208 | tf_op jit(solution)/shard_map/ppermute | solution.py:598
  5.0 0.0 collective-permute-start
  5.0 0.0 copy-done
  5.0 1.5 %gather_sources.1.source_ref = f32[4,48,128]{2,1,0:T(8,128)S(1)} custom-call(s32[48,128]{1,0:T(8,128)S(1)} %bitcast.27, f32[200,128]{1,0:T(8,128)S(1)} %get-tuple-element.11.sent_a, f32[200,128]{1,0:T(8,128)S(1)} %get-tuple-element.12.sent_b), custom_call_target="tpu_custom_call" | custom-call | flops 99999997952 | bytes 1048576 | tf_op jit(solution)/shard_map/gather_sources/pallas_call | solution.py:532
  6.5 0.0 collective-permute-done.margin_a
  6.5 2.3 %match_partner.1.part_ref = f32[6,8,128]{2,1,0:T(8,128)S(1)} custom-call(s32[2,24]{1,0:T(2,128)S(4)} %get-tuple-element.10.cells_hbm, f32[200,128]{1,0:T(8,128)S(1)} %get-tuple-element.11.sent_a, f32[4,48,128]{2,1,0:T(8,128)S(1)} %gather_sources.1.source_ref, f32[200,128]{1,0:T(8,128)S(1)} %collective-permute-done.margin_a), custom_call_target="tpu_custom_call" | custom-call | flops 629145600 | bytes 1048576 | tf_op jit(solution)/shard_map/match_partner/pallas_call | solution.py:544
  8.8 0.0 collective-permute-done.1.margin_b
  8.9 2.5 %match_other.1 = f32[32,128]{1,0:T(8,128)S(1)} custom-call(s32[2,24]{1,0:T(2,128)S(4)} %get-tuple-element.10.cells_hbm, f32[200,128]{1,0:T(8,128)S(1)} %get-tuple-element.11.sent_a, f32[4,48,128]{2,1,0:T(8,128)S(1)} %gather_sources.1.source_ref, f32[6,8,128]{2,1,0:T(8,128)S(1)} %match_partner.1.part_ref, f32[200,128]{1,0:T(8,128)S(1)} %collective-permute-done.margin_a, ...), custom_call_target="tpu_custom_call" | custom-call | flops 629145600 | bytes 1048576 | tf_op jit(solution)/shard_map/match_other/pallas_call | solution.py:557
  11.4 12.2 %all_to_all.22 = f32[32,1,128]{2,1,0:T(1,128)S(1)} all-to-all(f32[32,1,128]{2,1,0:T(1,128)S(1)} %bitcast.26), channel_id=1, replica_groups=mesh['line'=8,'seg'=4] {'line','seg'}, dimensions={0} | all-to-all | bytes 32768 | tf_op jit(solution)/shard_map/all_to_all | solution.py:584
  23.6 4.9 %match_second.1 = (f32[32,128]{1,0:T(8,128)S(1)}, f32[5,48,128]{2,1,0:T(8,128)}) custom-call(s32[2,24]{1,0:T(2,128)S(4)} %get-tuple-element.10.cells_hbm, f32[200,128]{1,0:T(8,128)S(1)} %get-tuple-element.11.sent_a, f32[32,128]{1,0:T(8,128)S(1)} %bitcast.24, f32[4,48,128]{2,1,0:T(8,128)S(1)} %gather_sources.1.source_ref, ...), custom_call_target="tpu_custom_call" | custom-call | flops 1258291200 | bytes 1048576 | tf_op jit(solution)/shard_map/match_second/pallas_call | solution.py:571
  28.5 8.9 %all_to_all.23 = f32[32,1,128]{2,1,0:T(1,128)S(1)} all-to-all(f32[32,1,128]{2,1,0:T(1,128)S(1)} %bitcast.25), channel_id=1, replica_groups=mesh['line'=8,'seg'=4] {'line','seg'}, dimensions={0} | all-to-all | bytes 32768 | tf_op jit(solution)/shard_map/all_to_all | solution.py:584
  37.4 0.7 %solve_last.1 = (f32[1,12]{1,0:T(1,128)}, f32[1,1]{1,0:T(1,128)}) custom-call(f32[32,128]{1,0:T(8,128)S(1)} %bitcast.23), custom_call_target="tpu_custom_call" | custom-call | tf_op jit(solution)/shard_map/solve_last/pallas_call | solution.py:605
Async XLA Ops:
  0.6 4.4 %copy-start = (s32[1,1,2,3072]{3,2,1,0:T(2,128)S(1)}, s32[1,1,2,3072]{3,2,1,0:T(2,128)}, u32[]{:S(2)}) copy-start(s32[1,1,2,3072]{3,2,1,0:T(2,128)} %param.5) | copy-start | bytes 73732
  1.6 7.3 %collective-permute-start.1 = (f32[200,128]{1,0:T(8,128)S(1)}, f32[200,128]{1,0:T(8,128)S(1)}, u32[]{:S(2)}, u32[]{:S(2)}) collective-permute-start(f32[200,128]{1,0:T(8,128)S(1)} %get-tuple-element.12.sent_b), channel_id=1, source_target_pairs={{0,28},{4,8},{8,4},{12,16},{16,12},{20,24},{24,20},{28,0},{1,29},{... | collective-permute-start | bytes 307208 | tf_op jit(solution)/shard_map/ppermute | solution.py:598
  5.0 1.5 %collective-permute-start = (f32[200,128]{1,0:T(8,128)S(1)}, f32[200,128]{1,0:T(8,128)S(1)}, u32[]{:S(2)}, u32[]{:S(2)}) collective-permute-start(f32[200,128]{1,0:T(8,128)S(1)} %get-tuple-element.11.sent_a), channel_id=1, source_target_pairs={{0,4},{4,0},{8,12},{12,8},{16,20},{20,16},{24,28},{28,24},{1,5},{5... | collective-permute-start | bytes 307208 | tf_op jit(solution)/shard_map/ppermute | solution.py:597

commit v11 on v10

--- a/solution.py
+++ b/solution.py
@@ -15,7 +15,7 @@
 MROWS = MARGIN // 128
 TILES = CT // 128
 GROUPS = BLOCK // 8
-LEAD = 48
+LEAD = 8
 NEAR = 1
 LAG = 3
 WIDE = 4

time: 38.3 us -> 38.2 us (level)
  no operation moved by 1% of the time
where the time goes in v11:
time: 38.2 us; the launch traced here: 38 us
  blocking collectives  21.1 us (55%)
  Pallas kernels  12.8 us (34%)
  starting transfers between devices  3.4 us (9%)
  between operations  0.7 us (2%)
    all_to_all x2, blocking collectives, exchange(): return lax.all_to_all(sums, ('line', 'seg'), 0, 0)  21.1 us
    pallas_call x1, Pallas kernels, second_call(): pl.pallas_call(functools.partial(second_kernel, lines, segs), in_specs=[S...  4.89 us
    ppermute x1, starting transfers between devices, on_device(): margin_b = lax.ppermute(sent_b, 'line', pairs_b)  3.4 us
    pallas_call x1, Pallas kernels, other_call(): pl.pallas_call(other_kernel, in_specs=[SMEM] + vmem(5), out_specs=vmem(1)...  2.5 us
    pallas_call x1, Pallas kernels, partner_call(): pl.pallas_call(partner_kernel, in_specs=[SMEM] + vmem(3), out_specs=vmem(...  2.31 us
    pallas_call x1, Pallas kernels, gather_call(): pl.pallas_call(gather_kernel, in_specs=vmem(3), out_specs=vmem(1)[0], out...  1.53 us
    pallas_call x1, Pallas kernels, pack_call(): pl.pallas_call(pack_kernel, in_specs=[HBM] * 3, out_specs=vmem(2) + [SMEM...  0.93 us
  transfers between devices with their start and end apart: 2, of which 0 were waited for; matrix products, arithmetic and copies ran while one was open for 0% of the time, Pallas kernels for 10%

profile of v11, /device:TPU:0, one launch (start us, length us, event | category | flops | bytes accessed | tf_op | source)
XLA Modules:
  0.0 38.0 jit_solution(17934972116383393628)
XLA Ops:
  0.6 0.0 copy-start
  0.6 0.9 %pack_margins.1 = (f32[200,128]{1,0:T(8,128)S(1)}, f32[200,128]{1,0:T(8,128)S(1)}, s32[2,24]{1,0:T(2,128)S(4)}) custom-call(f32[3,256,128]{2,1,0:T(8,128)} %bitcast.28, f32[1,12]{1,0:T(1,128)} %bitcast.30, s32[2,24]{1,0:T(2,128)} %bitcast.29), custom_call_target="tpu_custom_call" | custom-call | tf_op jit(solution)/shard_map/pack_margins/pallas_call | solution.py:75
  1.6 3.4 %collective-permute-start.1 = (f32[200,128]{1,0:T(8,128)S(1)}, f32[200,128]{1,0:T(8,128)S(1)}, u32[]{:S(2)}, u32[]{:S(2)}) collective-permute-start(f32[200,128]{1,0:T(8,128)S(1)} %get-tuple-element.12.sent_b), channel_id=1, source_target_pairs={{0,28},{4,8},{8,4},{12,16},{16,12},{20,24},{24,20},{28,0},{1,29},{... | collective-permute-start | bytes 307208 | tf_op jit(solution)/shard_map/ppermute | solution.py:598
  5.0 0.0 collective-permute-start
  5.0 0.0 copy-done
  5.0 1.5 %gather_sources.1.source_ref = f32[4,48,128]{2,1,0:T(8,128)S(1)} custom-call(s32[48,128]{1,0:T(8,128)S(1)} %bitcast.27, f32[200,128]{1,0:T(8,128)S(1)} %get-tuple-element.11.sent_a, f32[200,128]{1,0:T(8,128)S(1)} %get-tuple-element.12.sent_b), custom_call_target="tpu_custom_call" | custom-call | flops 99999997952 | bytes 1048576 | tf_op jit(solution)/shard_map/gather_sources/pallas_call | solution.py:532
  6.5 0.0 collective-permute-done.margin_a
  6.5 2.3 %match_partner.1.part_ref = f32[6,8,128]{2,1,0:T(8,128)S(1)} custom-call(s32[2,24]{1,0:T(2,128)S(4)} %get-tuple-element.10.cells_hbm, f32[200,128]{1,0:T(8,128)S(1)} %get-tuple-element.11.sent_a, f32[4,48,128]{2,1,0:T(8,128)S(1)} %gather_sources.1.source_ref, f32[200,128]{1,0:T(8,128)S(1)} %collective-permute-done.margin_a), custom_call_target="tpu_custom_call" | custom-call | flops 629145600 | bytes 1048576 | tf_op jit(solution)/shard_map/match_partner/pallas_call | solution.py:544
  8.8 0.0 collective-permute-done.1.margin_b
  8.9 2.5 %match_other.1 = f32[32,128]{1,0:T(8,128)S(1)} custom-call(s32[2,24]{1,0:T(2,128)S(4)} %get-tuple-element.10.cells_hbm, f32[200,128]{1,0:T(8,128)S(1)} %get-tuple-element.11.sent_a, f32[4,48,128]{2,1,0:T(8,128)S(1)} %gather_sources.1.source_ref, f32[6,8,128]{2,1,0:T(8,128)S(1)} %match_partner.1.part_ref, f32[200,128]{1,0:T(8,128)S(1)} %collective-permute-done.margin_a, ...), custom_call_target="tpu_custom_call" | custom-call | flops 629145600 | bytes 1048576 | tf_op jit(solution)/shard_map/match_other/pallas_call | solution.py:557
  11.4 12.2 %all_to_all.22 = f32[32,1,128]{2,1,0:T(1,128)S(1)} all-to-all(f32[32,1,128]{2,1,0:T(1,128)S(1)} %bitcast.26), channel_id=1, replica_groups=mesh['line'=8,'seg'=4] {'line','seg'}, dimensions={0} | all-to-all | bytes 32768 | tf_op jit(solution)/shard_map/all_to_all | solution.py:584
  23.6 4.9 %match_second.1 = (f32[32,128]{1,0:T(8,128)S(1)}, f32[5,48,128]{2,1,0:T(8,128)}) custom-call(s32[2,24]{1,0:T(2,128)S(4)} %get-tuple-element.10.cells_hbm, f32[200,128]{1,0:T(8,128)S(1)} %get-tuple-element.11.sent_a, f32[32,128]{1,0:T(8,128)S(1)} %bitcast.24, f32[4,48,128]{2,1,0:T(8,128)S(1)} %gather_sources.1.source_ref, ...), custom_call_target="tpu_custom_call" | custom-call | flops 1258291200 | bytes 1048576 | tf_op jit(solution)/shard_map/match_second/pallas_call | solution.py:571
  28.5 8.9 %all_to_all.23 = f32[32,1,128]{2,1,0:T(1,128)S(1)} all-to-all(f32[32,1,128]{2,1,0:T(1,128)S(1)} %bitcast.25), channel_id=1, replica_groups=mesh['line'=8,'seg'=4] {'line','seg'}, dimensions={0} | all-to-all | bytes 32768 | tf_op jit(solution)/shard_map/all_to_all | solution.py:584
  37.3 0.7 %solve_last.1 = (f32[1,12]{1,0:T(1,128)}, f32[1,1]{1,0:T(1,128)}) custom-call(f32[32,128]{1,0:T(8,128)S(1)} %bitcast.23), custom_call_target="tpu_custom_call" | custom-call | tf_op jit(solution)/shard_map/solve_last/pallas_call | solution.py:605
Async XLA Ops:
  0.6 4.4 %copy-start = (s32[1,1,2,3072]{3,2,1,0:T(2,128)S(1)}, s32[1,1,2,3072]{3,2,1,0:T(2,128)}, u32[]{:S(2)}) copy-start(s32[1,1,2,3072]{3,2,1,0:T(2,128)} %param.5) | copy-start | bytes 73732
  1.6 7.3 %collective-permute-start.1 = (f32[200,128]{1,0:T(8,128)S(1)}, f32[200,128]{1,0:T(8,128)S(1)}, u32[]{:S(2)}, u32[]{:S(2)}) collective-permute-start(f32[200,128]{1,0:T(8,128)S(1)} %get-tuple-element.12.sent_b), channel_id=1, source_target_pairs={{0,28},{4,8},{8,4},{12,16},{16,12},{20,24},{24,20},{28,0},{1,29},{... | collective-permute-start | bytes 307208 | tf_op jit(solution)/shard_map/ppermute | solution.py:598
  5.0 1.5 %collective-permute-start = (f32[200,128]{1,0:T(8,128)S(1)}, f32[200,128]{1,0:T(8,128)S(1)}, u32[]{:S(2)}, u32[]{:S(2)}) collective-permute-start(f32[200,128]{1,0:T(8,128)S(1)} %get-tuple-element.11.sent_a), channel_id=1, source_target_pairs={{0,4},{4,0},{8,12},{12,8},{16,20},{20,16},{24,28},{28,24},{1,5},{5... | collective-permute-start | bytes 307208 | tf_op jit(solution)/shard_map/ppermute | solution.py:597

commit v12 on v11

--- a/solution.py
+++ b/solution.py
@@ -16,7 +16,7 @@
 TILES = CT // 128
 GROUPS = BLOCK // 8
 LEAD = 8
-NEAR = 1
+NEAR = 2
 LAG = 3
 WIDE = 4
 QUICK_LIMIT = 1000.0

time: 38.2 us -> 38.2 us (level)
  no operation moved by 1% of the time
where the time goes in v12:
time: 38.2 us; the launch traced here: 38 us
  blocking collectives  21.1 us (55%)
  Pallas kernels  12.8 us (34%)
  starting transfers between devices  3.4 us (9%)
  between operations  0.7 us (2%)
    all_to_all x2, blocking collectives, exchange(): return lax.all_to_all(sums, ('line', 'seg'), 0, 0)  21.1 us
    pallas_call x1, Pallas kernels, second_call(): pl.pallas_call(functools.partial(second_kernel, lines, segs), in_specs=[S...  4.9 us
    ppermute x1, starting transfers between devices, on_device(): margin_b = lax.ppermute(sent_b, 'line', pairs_b)  3.4 us
    pallas_call x1, Pallas kernels, other_call(): pl.pallas_call(other_kernel, in_specs=[SMEM] + vmem(5), out_specs=vmem(1)...  2.5 us
    pallas_call x1, Pallas kernels, partner_call(): pl.pallas_call(partner_kernel, in_specs=[SMEM] + vmem(3), out_specs=vmem(...  2.3 us
    pallas_call x1, Pallas kernels, gather_call(): pl.pallas_call(gather_kernel, in_specs=vmem(3), out_specs=vmem(1)[0], out...  1.53 us
    pallas_call x1, Pallas kernels, pack_call(): pl.pallas_call(pack_kernel, in_specs=[HBM] * 3, out_specs=vmem(2) + [SMEM...  0.93 us
  transfers between devices with their start and end apart: 2, of which 0 were waited for; matrix products, arithmetic and copies ran while one was open for 0% of the time, Pallas kernels for 10%

profile of v12, /device:TPU:0, one launch (start us, length us, event | category | flops | bytes accessed | tf_op | source)
XLA Modules:
  0.0 38.0 jit_solution(17934972116383393628)
XLA Ops:
  0.6 0.0 copy-start
  0.6 0.9 %pack_margins.1 = (f32[200,128]{1,0:T(8,128)S(1)}, f32[200,128]{1,0:T(8,128)S(1)}, s32[2,24]{1,0:T(2,128)S(4)}) custom-call(f32[3,256,128]{2,1,0:T(8,128)} %bitcast.28, f32[1,12]{1,0:T(1,128)} %bitcast.30, s32[2,24]{1,0:T(2,128)} %bitcast.29), custom_call_target="tpu_custom_call" | custom-call | tf_op jit(solution)/shard_map/pack_margins/pallas_call | solution.py:75
  1.6 3.4 %collective-permute-start.1 = (f32[200,128]{1,0:T(8,128)S(1)}, f32[200,128]{1,0:T(8,128)S(1)}, u32[]{:S(2)}, u32[]{:S(2)}) collective-permute-start(f32[200,128]{1,0:T(8,128)S(1)} %get-tuple-element.12.sent_b), channel_id=1, source_target_pairs={{0,28},{4,8},{8,4},{12,16},{16,12},{20,24},{24,20},{28,0},{1,29},{... | collective-permute-start | bytes 307208 | tf_op jit(solution)/shard_map/ppermute | solution.py:598
  5.0 0.0 collective-permute-start
  5.0 0.0 copy-done
  5.0 1.5 %gather_sources.1.source_ref = f32[4,48,128]{2,1,0:T(8,128)S(1)} custom-call(s32[48,128]{1,0:T(8,128)S(1)} %bitcast.27, f32[200,128]{1,0:T(8,128)S(1)} %get-tuple-element.11.sent_a, f32[200,128]{1,0:T(8,128)S(1)} %get-tuple-element.12.sent_b), custom_call_target="tpu_custom_call" | custom-call | flops 99999997952 | bytes 1048576 | tf_op jit(solution)/shard_map/gather_sources/pallas_call | solution.py:532
  6.5 0.0 collective-permute-done.margin_a
  6.5 2.3 %match_partner.1.part_ref = f32[6,8,128]{2,1,0:T(8,128)S(1)} custom-call(s32[2,24]{1,0:T(2,128)S(4)} %get-tuple-element.10.cells_hbm, f32[200,128]{1,0:T(8,128)S(1)} %get-tuple-element.11.sent_a, f32[4,48,128]{2,1,0:T(8,128)S(1)} %gather_sources.1.source_ref, f32[200,128]{1,0:T(8,128)S(1)} %collective-permute-done.margin_a), custom_call_target="tpu_custom_call" | custom-call | flops 629145600 | bytes 1048576 | tf_op jit(solution)/shard_map/match_partner/pallas_call | solution.py:544
  8.8 0.0 collective-permute-done.1.margin_b
  8.9 2.5 %match_other.1 = f32[32,128]{1,0:T(8,128)S(1)} custom-call(s32[2,24]{1,0:T(2,128)S(4)} %get-tuple-element.10.cells_hbm, f32[200,128]{1,0:T(8,128)S(1)} %get-tuple-element.11.sent_a, f32[4,48,128]{2,1,0:T(8,128)S(1)} %gather_sources.1.source_ref, f32[6,8,128]{2,1,0:T(8,128)S(1)} %match_partner.1.part_ref, f32[200,128]{1,0:T(8,128)S(1)} %collective-permute-done.margin_a, ...), custom_call_target="tpu_custom_call" | custom-call | flops 629145600 | bytes 1048576 | tf_op jit(solution)/shard_map/match_other/pallas_call | solution.py:557
  11.4 12.2 %all_to_all.22 = f32[32,1,128]{2,1,0:T(1,128)S(1)} all-to-all(f32[32,1,128]{2,1,0:T(1,128)S(1)} %bitcast.26), channel_id=1, replica_groups=mesh['line'=8,'seg'=4] {'line','seg'}, dimensions={0} | all-to-all | bytes 32768 | tf_op jit(solution)/shard_map/all_to_all | solution.py:584
  23.6 4.9 %match_second.1 = (f32[32,128]{1,0:T(8,128)S(1)}, f32[5,48,128]{2,1,0:T(8,128)}) custom-call(s32[2,24]{1,0:T(2,128)S(4)} %get-tuple-element.10.cells_hbm, f32[200,128]{1,0:T(8,128)S(1)} %get-tuple-element.11.sent_a, f32[32,128]{1,0:T(8,128)S(1)} %bitcast.24, f32[4,48,128]{2,1,0:T(8,128)S(1)} %gather_sources.1.source_ref, ...), custom_call_target="tpu_custom_call" | custom-call | flops 1258291200 | bytes 1048576 | tf_op jit(solution)/shard_map/match_second/pallas_call | solution.py:571
  28.5 8.9 %all_to_all.23 = f32[32,1,128]{2,1,0:T(1,128)S(1)} all-to-all(f32[32,1,128]{2,1,0:T(1,128)S(1)} %bitcast.25), channel_id=1, replica_groups=mesh['line'=8,'seg'=4] {'line','seg'}, dimensions={0} | all-to-all | bytes 32768 | tf_op jit(solution)/shard_map/all_to_all | solution.py:584
  37.3 0.7 %solve_last.1 = (f32[1,12]{1,0:T(1,128)}, f32[1,1]{1,0:T(1,128)}) custom-call(f32[32,128]{1,0:T(8,128)S(1)} %bitcast.23), custom_call_target="tpu_custom_call" | custom-call | tf_op jit(solution)/shard_map/solve_last/pallas_call | solution.py:605
Async XLA Ops:
  0.6 4.4 %copy-start = (s32[1,1,2,3072]{3,2,1,0:T(2,128)S(1)}, s32[1,1,2,3072]{3,2,1,0:T(2,128)}, u32[]{:S(2)}) copy-start(s32[1,1,2,3072]{3,2,1,0:T(2,128)} %param.5) | copy-start | bytes 73732
  1.6 7.3 %collective-permute-start.1 = (f32[200,128]{1,0:T(8,128)S(1)}, f32[200,128]{1,0:T(8,128)S(1)}, u32[]{:S(2)}, u32[]{:S(2)}) collective-permute-start(f32[200,128]{1,0:T(8,128)S(1)} %get-tuple-element.12.sent_b), channel_id=1, source_target_pairs={{0,28},{4,8},{8,4},{12,16},{16,12},{20,24},{24,20},{28,0},{1,29},{... | collective-permute-start | bytes 307208 | tf_op jit(solution)/shard_map/ppermute | solution.py:598
  5.0 1.5 %collective-permute-start = (f32[200,128]{1,0:T(8,128)S(1)}, f32[200,128]{1,0:T(8,128)S(1)}, u32[]{:S(2)}, u32[]{:S(2)}) collective-permute-start(f32[200,128]{1,0:T(8,128)S(1)} %get-tuple-element.11.sent_a), channel_id=1, source_target_pairs={{0,4},{4,0},{8,12},{12,8},{16,20},{20,16},{24,28},{28,24},{1,5},{5... | collective-permute-start | bytes 307208 | tf_op jit(solution)/shard_map/ppermute | solution.py:597
